TPU v7x, 32 devices: a whole 2x2x4 slice. The times are simulated.
32 devices in a mesh: dp: 8 (over y, x, core), group: 4 (over z).
Axes of the slice: x: 2, y: 2, z: 4, core: 2. Of those that a mesh axis runs over, the one named last changes fastest.
Arguments:
- tokens: bfloat16 [16384, 896], P(('dp', 'group')), may hold values from -6 to 6
- positions: int32 [8, 2048], P('dp'), may hold values from 0 to 2047, as said below
- cotangent: bfloat16 [16384, 896], P(('dp', 'group')), may hold values from -6 to 6
- query_weight: float32 [896, 896], P(('dp', 'group')), may hold values from -0.1875 to 0.1875
- query_first: float32 [896, 896], P(('dp', 'group')), may hold values from -16384 to 16384
- query_second: float32 [896, 896], P(('dp', 'group')), may hold values from 0 to 14680064, as said below
- keyval_weight: float32 [896, 256], P(('dp', 'group')), may hold values from -0.1875 to 0.1875
- keyval_first: float32 [896, 256], P(('dp', 'group')), may hold values from -16384 to 16384
- keyval_second: float32 [896, 256], P(('dp', 'group')), may hold values from 0 to 16384, as said below
- output_weight: float32 [896, 896], P(('dp', 'group')), may hold values from -6 to 6
- output_first: float32 [896, 896], P(('dp', 'group')), may hold values from -16384 to 16384
- output_second: float32 [896, 896], P(('dp', 'group')), may hold values from 0 to 16384, as said below
- gateup_weight: float32 [896, 9728], P(('dp', 'group')), may hold values from -0.1875 to 0.1875
- gateup_first: float32 [896, 9728], P(('dp', 'group')), may hold values from -16384 to 16384
- gateup_second: float32 [896, 9728], P(('dp', 'group')), may hold values from 0 to 16384, as said below
- down_weight: float32 [4864, 896], P(('dp', 'group')), may hold values from -0.078125 to 0.078125
- down_first: float32 [4864, 896], P(('dp', 'group')), may hold values from -16384 to 16384
- down_second: float32 [4864, 896], P(('dp', 'group')), may hold values from 0 to 16384, as said below
- small_weight: float32 [2944], P(('dp', 'group')), may hold values from -2 to 2, as said below
- small_first: float32 [2944], P(('dp', 'group')), may hold values from -16384 to 16384
- small_second: float32 [2944], P(('dp', 'group')), may hold values from 0 to 205520896, as said below
Outputs:
- layer_out: bfloat16 [16384, 896], P(('dp', 'group'))
- tokens_grad: bfloat16 [16384, 896], P(('dp', 'group'))
- query_grad: float32 [896, 896], P(('dp', 'group'))
- query_second_out: float32 [896, 896], P(('dp', 'group'))
- query_weight_out: float32 [896, 896], P(('dp', 'group'))
- keyval_grad: float32 [896, 256], P(('dp', 'group'))
- keyval_second_out: float32 [896, 256], P(('dp', 'group'))
- keyval_weight_out: float32 [896, 256], P(('dp', 'group'))
- output_grad: float32 [896, 896], P(('dp', 'group'))
- output_second_out: float32 [896, 896], P(('dp', 'group'))
- output_weight_out: float32 [896, 896], P(('dp', 'group'))
- gateup_grad: float32 [896, 9728], P(('dp', 'group'))
- gateup_second_out: float32 [896, 9728], P(('dp', 'group'))
- gateup_weight_out: float32 [896, 9728], P(('dp', 'group'))
- down_grad: float32 [4864, 896], P(('dp', 'group'))
- down_second_out: float32 [4864, 896], P(('dp', 'group'))
- down_weight_out: float32 [4864, 896], P(('dp', 'group'))
- small_grad: float32 [2944], P(('dp', 'group'))
- small_second_out: float32 [2816], P(('dp', 'group'))
- value_bias_second_out: float32 [128], P(('dp', 'group'))
- small_weight_out: float32 [2944], P(('dp', 'group'))
Inputs may be any that keep to these rules, and one draw needn't show every extreme that they name: `positions`: each row counts the place of a token within its packed document: 0 at the row's first token and at every document start, otherwise one more than the token before. Documents start only at the first token of a row, within its first 256 tokens, or within its last 256 tokens. At least one row is a single document. `query_second`: Positive. `keyval_second`: Positive. `output_second`: Positive. `gateup_second`: Positive. `down_second`: Positive. `small_second`: Positive. `small_weight`: gains lie in 0.6 to 1.4.
All inputs are finite; a program needn't handle non-finite values.
Results may differ from a plain program's by a relative error of at most 0.015.
The roundings to bfloat16 on the way count: a program that leaves them out, or rounds other values in their place, can miss the bound.
Values may be sent and summed in bfloat16 or wider, within the bound.
No kernel may reach another device: no remote copies, remote signals or barrier semaphores. Data moves between devices by JAX's collectives and lax.ppermute only.
A program may use at most 320 MiB of HBM per device.

v0:
```python
import math

import jax
import jax.numpy as jnp
from jax import lax
from jax.sharding import PartitionSpec as P

D = 896
HQ = 14
HK = 2
HD = 64
FF = 4864
STEP = 10


theta_base = 1000000.0
norm_eps = 1e-06
beta_one = 0.9
beta_two = 0.95
adam_eps = 1e-08
decay_rate = 0.1
rate_proj = 0.02
rate_out = 0.5
rate_small = 0.2
masked_score = -1e30


def rotary_tables(places):
    half_size = HD // 2
    inv_freq = theta_base ** (-(jnp.arange(half_size, dtype=jnp.float32) * 2.0) / HD)
    angles = places.astype(jnp.float32)[:, None] * inv_freq[None, :]
    return (jnp.cos(angles), jnp.sin(angles))


def rotate(values, cosine, sine_table, head_count, direction):
    row_count = values.shape[0]
    halves = values.reshape(row_count, head_count, 2, HD // 2)
    lower_half = halves[:, :, 0]
    upper_half = halves[:, :, 1]
    cos_b = cosine[:, None, :]
    sin_b = direction * sine_table[:, None, :]
    joined = jnp.stack(
        [lower_half * cos_b - upper_half * sin_b, upper_half * cos_b + lower_half * sin_b], axis=2
    )
    return joined.reshape(row_count, head_count * HD)


def adamw_step(gradient, first_old, second_old, weight, step_rate, decay_factor):
    first_new = beta_one * first_old + (1.0 - beta_one) * gradient
    second_new = beta_two * second_old + (1.0 - beta_two) * gradient * gradient
    first_hat = first_new / (1.0 - beta_one**STEP)
    second_hat = second_new / (1.0 - beta_two**STEP)
    updated = weight - step_rate * (
        first_hat / (jnp.sqrt(second_hat) + adam_eps) + decay_factor * weight
    )
    return (second_new, updated)


def body(
    tokens,
    positions,
    cotangent,
    query_weight,
    query_first,
    query_second,
    keyval_weight,
    keyval_first,
    keyval_second,
    output_weight,
    output_first,
    output_second,
    gateup_weight,
    gateup_first,
    gateup_second,
    down_weight,
    down_first,
    down_second,
    small_weight,
    small_first,
    small_second,
):
    row_count = tokens.shape[0]
    group_size = lax.axis_size("group")
    my_index = lax.axis_index("group")
    seq_len = row_count * group_size
    head_ratio = HQ // HK
    query_width = HQ * HD
    kv_width = HK * HD
    scale_factor = 1.0 / math.sqrt(HD)
    query_low_w = query_weight.astype(jnp.bfloat16)
    keyval_low_w = keyval_weight.astype(jnp.bfloat16)
    output_low_w = output_weight.astype(jnp.bfloat16)
    gateup_low_w = gateup_weight.astype(jnp.bfloat16)
    down_low_w = down_weight.astype(jnp.bfloat16)
    small_low_w = small_weight.astype(jnp.bfloat16)
    gathered = (
        lax.all_gather(query_low_w, ("dp", "group"), axis=0, tiled=True),
        lax.all_gather(keyval_low_w, ("dp", "group"), axis=0, tiled=True),
        lax.all_gather(output_low_w, ("dp", "group"), axis=0, tiled=True),
        lax.all_gather(gateup_low_w, ("dp", "group"), axis=0, tiled=True),
        lax.all_gather(down_low_w, ("dp", "group"), axis=0, tiled=True),
        lax.all_gather(small_low_w, ("dp", "group"), axis=0, tiled=True),
    )
    query_full, keyval_full, output_full, gateup_full, down_full, small_full = gathered
    small_values = small_full.astype(jnp.float32)
    gain_one = small_values[:D]
    gain_two = small_values[D : 2 * D]
    bias_query = small_values[2 * D : 2 * D + query_width]
    bias_keyval = small_values[2 * D + query_width :]
    place_row = positions[0]
    local_places = lax.dynamic_slice_in_dim(place_row, my_index * row_count, row_count, 0)
    query_index = my_index * row_count + jnp.arange(row_count, dtype=jnp.int32)
    query_start = query_index - local_places
    key_index = jnp.arange(seq_len, dtype=jnp.int32)
    key_start = key_index - place_row
    act_in = tokens.astype(jnp.float32)
    inv_one = lax.rsqrt(jnp.mean(act_in * act_in, axis=1, keepdims=True) + norm_eps)
    scaled_one = act_in * inv_one
    normed_one = (scaled_one * gain_one).astype(jnp.bfloat16)
    query_pre = jnp.dot(normed_one, query_full, preferred_element_type=jnp.float32) + bias_query
    keyval_pre = jnp.dot(normed_one, keyval_full, preferred_element_type=jnp.float32) + bias_keyval
    cosine, sine_table = rotary_tables(local_places)
    query_low = rotate(query_pre, cosine, sine_table, HQ, 1.0).astype(jnp.bfloat16)
    key_low = rotate(keyval_pre[:, :kv_width], cosine, sine_table, HK, 1.0).astype(jnp.bfloat16)
    value_low = keyval_pre[:, kv_width:].astype(jnp.bfloat16)
    keys_all, values_all = (
        lax.all_gather(key_low, "group", axis=0, tiled=True),
        lax.all_gather(value_low, "group", axis=0, tiled=True),
    )
    key_block = min(seq_len, max(row_count, 512))
    block_count = seq_len // key_block
    query_heads = query_low.reshape(row_count, HK, head_ratio, HD)

    def key_slab(number):
        low_edge = number * key_block
        return keys_all[low_edge : low_edge + key_block].reshape(key_block, HK, HD)

    def value_slab(number):
        low_edge = number * key_block
        return values_all[low_edge : low_edge + key_block].reshape(key_block, HK, HD)

    def block_scores(number):
        low_edge = number * key_block
        scores = (
            jnp.einsum(
                "qhgd,khd->hgqk", query_heads, key_slab(number), preferred_element_type=jnp.float32
            )
            * scale_factor
        )
        allowed = (key_index[low_edge : low_edge + key_block][None, :] <= query_index[:, None]) & (
            key_start[low_edge : low_edge + key_block][None, :] == query_start[:, None]
        )
        return jnp.where(allowed[None, None], scores, masked_score)

    softmax_stats = (
        jnp.full((HK, head_ratio, row_count), masked_score, jnp.float32),
        jnp.zeros((HK, head_ratio, row_count), jnp.float32),
    )
    for number in range(block_count):
        running, totals = softmax_stats
        max_scores = block_scores(number)
        newest = jnp.maximum(running, jnp.max(max_scores, axis=3))
        totals = totals * jnp.exp(running - newest) + jnp.sum(
            jnp.exp(max_scores - newest[..., None]), axis=3
        )
        softmax_stats = (newest, totals)
    log_total = softmax_stats[0] + jnp.log(softmax_stats[1])
    attn_float = jnp.zeros((row_count, HK, head_ratio, HD), jnp.float32)
    for number in range(block_count):
        value_weights_low = jnp.exp(block_scores(number) - log_total[..., None]).astype(
            jnp.bfloat16
        )
        attn_float = attn_float + jnp.einsum(
            "hgqk,khd->qhgd",
            value_weights_low,
            value_slab(number),
            preferred_element_type=jnp.float32,
        )
    attn_low = attn_float.reshape(row_count, query_width).astype(jnp.bfloat16)
    middle = act_in + jnp.dot(attn_low, output_full, preferred_element_type=jnp.float32)
    inv_two = lax.rsqrt(jnp.mean(middle * middle, axis=1, keepdims=True) + norm_eps)
    scaled_two = middle * inv_two
    normed_two = (scaled_two * gain_two).astype(jnp.bfloat16)
    gate_up = jnp.dot(normed_two, gateup_full, preferred_element_type=jnp.float32)
    gate_pre = gate_up[:, :FF]
    up_pre = gate_up[:, FF:]
    sigmoid_gate = jax.nn.sigmoid(gate_pre)
    hidden = (gate_pre * sigmoid_gate * up_pre).astype(jnp.bfloat16)
    layer_out = (middle + jnp.dot(hidden, down_full, preferred_element_type=jnp.float32)).astype(
        jnp.bfloat16
    )
    grad_out = cotangent.astype(jnp.float32)
    down_term = jnp.einsum("tf,td->fd", hidden, cotangent, preferred_element_type=jnp.float32)
    grad_hidden = jnp.einsum("td,fd->tf", cotangent, down_full, preferred_element_type=jnp.float32)
    grad_gate = grad_hidden * up_pre * sigmoid_gate * (1.0 + gate_pre * (1.0 - sigmoid_gate))
    grad_up = grad_hidden * gate_pre * sigmoid_gate
    grad_gateup = jnp.concatenate([grad_gate, grad_up], axis=1).astype(jnp.bfloat16)
    gateup_term = jnp.einsum(
        "td,tf->df", normed_two, grad_gateup, preferred_element_type=jnp.float32
    )
    grad_normed_two = jnp.einsum(
        "tf,df->td", grad_gateup, gateup_full, preferred_element_type=jnp.float32
    )
    gateup_grad, down_grad = (
        lax.psum_scatter(gateup_term, ("dp", "group"), scatter_dimension=0, tiled=True),
        lax.psum_scatter(down_term, ("dp", "group"), scatter_dimension=0, tiled=True),
    )
    gain_scaled_two = grad_normed_two * gain_two
    gain_two_term = jnp.sum(grad_normed_two * scaled_two, axis=0)
    grad_middle = grad_out + inv_two * (
        gain_scaled_two - scaled_two * jnp.mean(gain_scaled_two * scaled_two, axis=1, keepdims=True)
    )
    grad_middle_low = grad_middle.astype(jnp.bfloat16)
    output_term = jnp.einsum(
        "tq,td->qd", attn_low, grad_middle_low, preferred_element_type=jnp.float32
    )
    grad_attn_low = jnp.einsum(
        "td,qd->tq", grad_middle_low, output_full, preferred_element_type=jnp.float32
    ).astype(jnp.bfloat16)
    grad_attn_heads = grad_attn_low.reshape(row_count, HK, head_ratio, HD)
    row_delta = jnp.einsum("qhgd,qhgd->hgq", grad_attn_heads.astype(jnp.float32), attn_float)
    grad_state = (
        jnp.zeros((row_count, HK, head_ratio, HD), jnp.float32),
        jnp.zeros((seq_len, kv_width), jnp.float32),
        jnp.zeros((seq_len, kv_width), jnp.float32),
    )
    for number in range(block_count):
        grad_query, grad_keys, grad_values = grad_state
        grad_low_edge = number * key_block
        key_part = key_slab(number)
        value_part = value_slab(number)
        weights_float = jnp.exp(block_scores(number) - log_total[..., None])
        weights_low = weights_float.astype(jnp.bfloat16)
        grad_weights = jnp.einsum(
            "qhgd,khd->hgqk", grad_attn_heads, value_part, preferred_element_type=jnp.float32
        )
        grad_scores = (weights_float * (grad_weights - row_delta[..., None])).astype(jnp.bfloat16)
        grad_query = (
            grad_query
            + jnp.einsum(
                "hgqk,khd->qhgd", grad_scores, key_part, preferred_element_type=jnp.float32
            )
            * scale_factor
        )
        key_term = (
            jnp.einsum(
                "hgqk,qhgd->khd", grad_scores, query_heads, preferred_element_type=jnp.float32
            )
            * scale_factor
        )
        value_term = jnp.einsum(
            "hgqk,qhgd->khd", weights_low, grad_attn_heads, preferred_element_type=jnp.float32
        )
        grad_keys = lax.dynamic_update_slice_in_dim(
            grad_keys, key_term.reshape(key_block, kv_width), grad_low_edge, 0
        )
        grad_values = lax.dynamic_update_slice_in_dim(
            grad_values, value_term.reshape(key_block, kv_width), grad_low_edge, 0
        )
        grad_state = (grad_query, grad_keys, grad_values)
    key_grads, value_grads = (
        lax.psum_scatter(
            grad_state[1].astype(jnp.bfloat16), "group", scatter_dimension=0, tiled=True
        ).astype(jnp.float32),
        lax.psum_scatter(
            grad_state[2].astype(jnp.bfloat16), "group", scatter_dimension=0, tiled=True
        ).astype(jnp.float32),
    )
    grad_query_pre = rotate(
        grad_state[0].reshape(row_count, query_width), cosine, sine_table, HQ, -1.0
    ).astype(jnp.bfloat16)
    grad_keyval_pre = jnp.concatenate(
        [rotate(key_grads, cosine, sine_table, HK, -1.0), value_grads], axis=1
    ).astype(jnp.bfloat16)
    query_term = jnp.einsum(
        "td,tq->dq", normed_one, grad_query_pre, preferred_element_type=jnp.float32
    )
    keyval_term = jnp.einsum(
        "td,tk->dk", normed_one, grad_keyval_pre, preferred_element_type=jnp.float32
    )
    bias_query_term = jnp.sum(grad_query_pre.astype(jnp.float32), axis=0)
    bias_keyval_term = jnp.sum(grad_keyval_pre.astype(jnp.float32), axis=0)
    grad_normed_one = jnp.einsum(
        "tq,dq->td", grad_query_pre, query_full, preferred_element_type=jnp.float32
    ) + jnp.einsum("tk,dk->td", grad_keyval_pre, keyval_full, preferred_element_type=jnp.float32)
    gain_scaled_one = grad_normed_one * gain_one
    gain_one_term = jnp.sum(grad_normed_one * scaled_one, axis=0)
    grad_input = grad_middle + inv_one * (
        gain_scaled_one - scaled_one * jnp.mean(gain_scaled_one * scaled_one, axis=1, keepdims=True)
    )
    tokens_grad = grad_input.astype(jnp.bfloat16)
    small_term = jnp.concatenate([gain_one_term, gain_two_term, bias_query_term, bias_keyval_term])
    query_grad, keyval_grad, output_grad, small_grad = (
        lax.psum_scatter(query_term, ("dp", "group"), scatter_dimension=0, tiled=True),
        lax.psum_scatter(keyval_term, ("dp", "group"), scatter_dimension=0, tiled=True),
        lax.psum_scatter(output_term, ("dp", "group"), scatter_dimension=0, tiled=True),
        lax.psum_scatter(small_term, ("dp", "group"), scatter_dimension=0, tiled=True),
    )
    query_second_out, query_weight_out = adamw_step(
        query_grad, query_first, query_second, query_weight, rate_proj, decay_rate
    )
    keyval_second_out, keyval_weight_out = adamw_step(
        keyval_grad, keyval_first, keyval_second, keyval_weight, rate_proj, decay_rate
    )
    output_second_out, output_weight_out = adamw_step(
        output_grad, output_first, output_second, output_weight, rate_out, decay_rate
    )
    gateup_second_out, gateup_weight_out = adamw_step(
        gateup_grad, gateup_first, gateup_second, gateup_weight, rate_proj, decay_rate
    )
    down_second_out, down_weight_out = adamw_step(
        down_grad, down_first, down_second, down_weight, rate_proj, decay_rate
    )
    small_second_new, small_weight_out = adamw_step(
        small_grad, small_first, small_second, small_weight, rate_small, 0.0
    )
    all_seconds = lax.all_gather(small_second_new, ("dp", "group"), axis=0, tiled=True)
    device_count = lax.axis_size("dp") * group_size
    flat_index = lax.axis_index("dp") * group_size + my_index
    rest_length = 2 * D + query_width + kv_width
    rest_piece = rest_length // device_count
    value_piece = kv_width // device_count
    small_second_out = lax.dynamic_slice_in_dim(all_seconds, flat_index * rest_piece, rest_piece, 0)
    value_bias_second_out = lax.dynamic_slice_in_dim(
        all_seconds, rest_length + flat_index * value_piece, value_piece, 0
    )
    return (
        layer_out,
        tokens_grad,
        query_grad,
        query_second_out,
        query_weight_out,
        keyval_grad,
        keyval_second_out,
        keyval_weight_out,
        output_grad,
        output_second_out,
        output_weight_out,
        gateup_grad,
        gateup_second_out,
        gateup_weight_out,
        down_grad,
        down_second_out,
        down_weight_out,
        small_grad,
        small_second_out,
        value_bias_second_out,
        small_weight_out,
    )


def solution(mesh):
    in_specs = (
        P(("dp", "group"), None),
        P("dp", None),
        P(("dp", "group"), None),
        P(("dp", "group"), None),
        P(("dp", "group"), None),
        P(("dp", "group"), None),
        P(("dp", "group"), None),
        P(("dp", "group"), None),
        P(("dp", "group"), None),
        P(("dp", "group"), None),
        P(("dp", "group"), None),
        P(("dp", "group"), None),
        P(("dp", "group"), None),
        P(("dp", "group"), None),
        P(("dp", "group"), None),
        P(("dp", "group"), None),
        P(("dp", "group"), None),
        P(("dp", "group"), None),
        P(("dp", "group")),
        P(("dp", "group")),
        P(("dp", "group")),
    )
    out_specs = (
        P(("dp", "group"), None),
        P(("dp", "group"), None),
        P(("dp", "group"), None),
        P(("dp", "group"), None),
        P(("dp", "group"), None),
        P(("dp", "group"), None),
        P(("dp", "group"), None),
        P(("dp", "group"), None),
        P(("dp", "group"), None),
        P(("dp", "group"), None),
        P(("dp", "group"), None),
        P(("dp", "group"), None),
        P(("dp", "group"), None),
        P(("dp", "group"), None),
        P(("dp", "group"), None),
        P(("dp", "group"), None),
        P(("dp", "group"), None),
        P(("dp", "group")),
        P(("dp", "group")),
        P(("dp", "group")),
        P(("dp", "group")),
    )
    return jax.shard_map(body, mesh=mesh, in_specs=in_specs, out_specs=out_specs, check_vma=False)
```

profile of v0, /device:TPU:0, one launch (start us, length us, event | category | flops | bytes accessed | tf_op | source)
XLA Modules:
  0.0 2196.0 jit_solution(10707675565825206126)
XLA Ops:
  15.5 42.1 %all-reduce.2 = bf16[2944]{0:T(1024)(128)(2,1)S(1)} all-reduce(bf16[2944]{0:T(1024)(128)(2,1)S(1)} %dynamic-update-slice), channel_id=1, replica_groups=mesh['dp'=8,'group'=4] {'dp','group'}, use_global_device_ids=true, to_apply=%add.2 | all-reduce | flops 2944 | bytes 11776
  59.9 71.8 %all-gather = bf16[32,28,256]{2,1,0:T(8,128)(2,1)S(1)} all-gather(bf16[1,28,256]{2,1,0:T(8,128)(2,1)S(1)} %convert_bitcast_fusion.3), channel_id=1, replica_groups=mesh['dp'=8,'group'=4] {'dp','group'}, dimensions={0}, use_global_device_ids=true | all-gather | bytes 473088 | tf_op jit(solution)/shard_map/all_gather | solution.py:98
  134.9 18.8 all_gather.30
  153.7 18.1 all_gather.29
  189.4 8.9 fusion.18
  246.5 8.5 exponential_reduce_fusion
  255.1 11.0 fusion.56
  270.8 10.3 fusion.52
  290.6 19.6 reshape.581
  310.3 18.7 fusion.87
  329.0 20.5 all-gather.9.cloned.1.call-done
  349.5 19.0 multiply_convert_fusion.1
  368.5 16.8 multiply_reduce_fusion
  391.7 11.9 fusion.5
  403.6 9.5 fusion.9
  413.1 9.5 fusion.11
  434.7 9.0 fusion.54
  475.6 11.7 fusion.109
  512.7 9.8 add_convert_fusion
  522.4 19.5 fusion.20
  545.3 1355.3 %fusion.93 = (f32[32,896]{1,0:T(8,128)S(1)}, f32[32,256]{1,0:T(8,128)S(1)}, f32[32,896]{1,0:T(8,128)}, f32[32,9728]{1,0:T(8,128)}) fusion(f32[896,896]{1,0:T(8,128)} %fusion.89, f32[896,256]{1,0:T(8,128)} %fusion.46, f32[896,896]{1,0:T(8,128)} %fusion.41, f32[896,9728]{1,0:T(8,128)} %fusion.20), kind=kCustom, calls=%all-reduce-scatter.4 | all-reduce-scatter fusion | flops 12058625 | bytes 43712512
  1944.9 124.0 %all-reduce.9 = f32[2944]{0:T(1024)S(1)} all-reduce(f32[2944]{0:T(1024)S(1)} %pad_maximum_fusion.9), channel_id=9, replica_groups=mesh['dp'=8,'group'=4] {'dp','group'}, use_global_device_ids=true, to_apply=%region_23.24.clone | all-reduce | flops 2944 | bytes 23552
  2079.5 46.4 %all-reduce.3 = f32[2944]{0:T(1024)S(1)} all-reduce(f32[2944]{0:T(1024)S(1)} %fusion.85), channel_id=1, replica_groups=mesh['dp'=8,'group'=4] {'dp','group'}, use_global_device_ids=true, to_apply=%add.3 | all-reduce | flops 2944 | bytes 23552
  2150.3 31.5 %concatenate.17 = f32[156,9728]{1,0:T(8,128)} concatenate(f32[28,9728]{1,0:T(8,128)} %collective-permute-done.15, f32[32,9728]{1,0:T(8,128)} %collective-permute-done.14, f32[32,9728]{1,0:T(8,128)} %collective-permute-done.13, f32[32,9728]{1,0:T(8,128)S(1)} %collective-permute-done.12, f32[32,9728]{1,0:T(8,128)} %get-tuple-element.32), dimensions={0} | concatenate | bytes 12140544
  (371 shorter events, 257.6 us)
Async XLA Ops:
  7.2 168.3 %all-gather.11.cloned.1.call-start = ((), (), s32[]{:S(2)}) async-start(), calls=%async_computation.6 | async-start | bytes 1892352 | tf_op jit(solution)/shard_map/all_gather | solution.py:97
  8.8 176.4 %all-gather.13.cloned.1.call-start = ((), (), s32[]{:S(2)}) async-start(), calls=%async_computation.7 | async-start | bytes 1892352 | tf_op jit(solution)/shard_map/all_gather | solution.py:99
  10.4 280.2 %all-gather.15.cloned.1.call-start = ((), (), s32[]{:S(2)}) async-start(), calls=%async_computation.8 | async-start | bytes 20545536 | tf_op jit(solution)/shard_map/all_gather | solution.py:100
  12.7 336.8 %all-gather.9.cloned.1.call-start = ((), (), s32[]{:S(2)}) async-start(), calls=%async_computation.3 | async-start | bytes 8988672 | tf_op jit(solution)/shard_map/all_gather | solution.py:101
  14.5 527.4 %reduce-scatter.15.cloned.1.call-start = ((), (), s32[]{:S(2)}) async-start(), calls=%async_computation.4 | async-start | bytes 655360 | tf_op jit(solution)/shard_map/reduce_scatter | solution.py:262
  467.4 75.5 %reduce-scatter.17.cloned.1.call-start = ((), (), s32[]{:S(2)}) async-start(), calls=%async_computation.5 | async-start | bytes 655360 | tf_op jit(solution)/shard_map/reduce_scatter | solution.py:265
  475.6 1710.6 %reduce-scatter.19.cloned.1.call-start = ((), (), s32[]{:S(2)}) async-start(), calls=%async_computation.9 | async-start | bytes 17977344
  545.3 1369.0 %copy-start.33 = (bf16[896,256]{1,0:T(8,128)(2,1)S(1)}, bf16[896,256]{1,0:T(8,128)(2,1)}, u32[]{:S(2)}) copy-start(bf16[896,256]{1,0:T(8,128)(2,1)} %copy-done.32) | copy-start | bytes 1376260
  1901.6 39.8 %collective-permute-start.10 = (f32[32,896]{1,0:T(8,128)}, f32[32,896]{1,0:T(8,128)}, u32[]{:S(2)}, u32[]{:S(2)}) collective-permute-start(f32[32,896]{1,0:T(8,128)} %get-tuple-element.31), channel_id=1, source_target_pairs={{0,3},{1,4},{2,5},{3,6},{4,7},{5,8},{6,9},{7,10},{8,11},{9,12},{10... | collective-permute-start | bytes 344072
  1903.5 18.1 collective-permute-start.4
  1906.0 22.2 %collective-permute-start.5 = (f32[32,256]{1,0:T(8,128)S(1)}, f32[32,256]{1,0:T(8,128)S(1)}, u32[]{:S(2)}, u32[]{:S(2)}) collective-permute-start(f32[32,256]{1,0:T(8,128)S(1)} %get-tuple-element.30), channel_id=1, source_target_pairs={{0,2},{1,3},{2,4},{3,5},{4,6},{5,7},{6,8},{7,9},{8,10},{9,11},{10,... | collective-permute-start | bytes 98312
  1907.3 22.4 %collective-permute-start.6 = (f32[32,256]{1,0:T(8,128)S(1)}, f32[32,256]{1,0:T(8,128)S(1)}, u32[]{:S(2)}, u32[]{:S(2)}) collective-permute-start(f32[32,256]{1,0:T(8,128)S(1)} %get-tuple-element.30), channel_id=1, source_target_pairs={{0,3},{1,4},{2,5},{3,6},{4,7},{5,8},{6,9},{7,10},{8,11},{9,12},{10... | collective-permute-start | bytes 98312
  1912.6 4.3 collective-permute-start.7
  1916.9 18.0 collective-permute-start.11
  1921.6 17.0 collective-permute-start.3
  1928.3 222.0 %collective-permute-start.12 = (f32[32,9728]{1,0:T(8,128)}, f32[32,9728]{1,0:T(8,128)S(1)}, u32[]{:S(2)}, u32[]{:S(2)}) collective-permute-start(f32[32,9728]{1,0:T(8,128)} %get-tuple-element.32), channel_id=1, source_target_pairs={{0,1},{1,2},{2,3},{3,4},{4,5},{5,6},{6,7},{7,8},{8,9},{9,10},{10,1... | collective-permute-start | bytes 3735560
  1929.7 220.5 %collective-permute-start.13 = (f32[32,9728]{1,0:T(8,128)}, f32[32,9728]{1,0:T(8,128)}, u32[]{:S(2)}, u32[]{:S(2)}) collective-permute-start(f32[32,9728]{1,0:T(8,128)} %get-tuple-element.32), channel_id=1, source_target_pairs={{0,2},{1,3},{2,4},{3,5},{4,6},{5,7},{6,8},{7,9},{8,10},{9,11},{10,... | collective-permute-start | bytes 3735560
  1934.9 215.3 %collective-permute-start.14 = (f32[32,9728]{1,0:T(8,128)}, f32[32,9728]{1,0:T(8,128)}, u32[]{:S(2)}, u32[]{:S(2)}) collective-permute-start(f32[32,9728]{1,0:T(8,128)} %get-tuple-element.32), channel_id=1, source_target_pairs={{0,3},{1,4},{2,5},{3,6},{4,7},{5,8},{6,9},{7,10},{8,11},{9,12},{10... | collective-permute-start | bytes 3735560
  1938.6 130.4 %collective-permute-start.8 = (f32[32,896]{1,0:T(8,128)}, f32[32,896]{1,0:T(8,128)S(1)}, u32[]{:S(2)}, u32[]{:S(2)}) collective-permute-start(f32[32,896]{1,0:T(8,128)} %get-tuple-element.31), channel_id=1, source_target_pairs={{0,1},{1,2},{2,3},{3,4},{4,5},{5,6},{6,7},{7,8},{8,9},{9,10},{10,1... | collective-permute-start | bytes 344072
  1941.4 129.3 %collective-permute-start.9 = (f32[32,896]{1,0:T(8,128)}, f32[32,896]{1,0:T(8,128)S(1)}, u32[]{:S(2)}, u32[]{:S(2)}) collective-permute-start(f32[32,896]{1,0:T(8,128)} %get-tuple-element.31), channel_id=1, source_target_pairs={{0,2},{1,3},{2,4},{3,5},{4,6},{5,7},{6,8},{7,9},{8,10},{9,11},{10,... | collective-permute-start | bytes 344072
  2068.9 5.5 collective-permute-start
  2070.7 79.5 %collective-permute-start.15 = (f32[28,9728]{1,0:T(8,128)}, f32[28,9728]{1,0:T(8,128)}, u32[]{:S(2)}, u32[]{:S(2)}) collective-permute-start(f32[28,9728]{1,0:T(8,128)} %slice.192), channel_id=1, source_target_pairs={{0,4},{1,5},{2,6},{3,7},{4,8},{5,9},{6,10},{7,11},{8,12},{9,13},{1... | collective-permute-start | bytes 3268616
  2074.4 54.5 %collective-permute-start.1 = (f32[32,896]{1,0:T(8,128)S(1)}, f32[32,896]{1,0:T(8,128)S(1)}, u32[]{:S(2)}, u32[]{:S(2)}) collective-permute-start(f32[32,896]{1,0:T(8,128)S(1)} %get-tuple-element.29), channel_id=1, source_target_pairs={{0,2},{1,3},{2,4},{3,5},{4,6},{5,7},{6,8},{7,9},{8,10},{9,11},{10,... | collective-permute-start | bytes 344072
  2129.0 9.8 collective-permute-start.2
  (102 other events, 3359.2 us)
Sparse Core Ops, SparseCore 0:
  11.4 58.4 all-gather.10
  73.3 55.4 all-gather.12
  132.2 137.1 all-gather.14
  272.8 76.6 all-gather.8
  467.5 20.2 reduce-scatter.14
  490.5 19.8 reduce-scatter.16
  513.3 706.0 reduce-scatter.18
where the time goes:
time: 2200 us
  blocking collectives  1680 us (76%)
  matrix products  280 us (13%)
  local copies, waits for them, and re-layouts  87 us (4%)
  other arithmetic  64.9 us (3%)
  starting transfers between devices  50.7 us (2%)
    unnamed x4, blocking collectives  1570 us
    unnamed x221, local copies, waits for them, and re-layouts  80.6 us
    all_gather x1, blocking collectives, body(): lax.all_gather(keyval_low_w, ('dp', 'group'), axis=0, tiled=True)  71.8 us
    unnamed x17, starting transfers between devices  50.4 us
  transfers between devices with their start and end apart: 23, of which 1 were waited for; matrix products, arithmetic and copies ran while one was open for 76% of the time, Pallas kernels for 0%

commit v1 on v0

v1 whole, which is shorter than its diff:
```python
import functools

import jax
import jax.numpy as jnp
from jax import lax
from jax.experimental import pallas as pl
from jax.experimental.pallas import tpu as pltpu
from jax.sharding import PartitionSpec as P

D = 896
HQ = 14
HK = 2
HD = 64
FF = 4864
STEP = 10


theta_base = 1000000.0
norm_eps = 1e-06
beta_one = 0.9
beta_two = 0.95
adam_eps = 1e-08
decay_rate = 0.1
rate_proj = 0.02
rate_out = 0.5
rate_small = 0.2
masked_score = -1e30

low = jnp.bfloat16
wide = jnp.float32


MIB = 1024 * 1024
LANES = 128
ROWS = 16
NT = (((1,), (1,)), ((), ()))
TN = (((0,), (0,)), ((), ()))


def padded(size, unit):
    return -(-size // unit) * unit


def rotary_angles(places):
    half_size = HD // 2
    inv_freq = theta_base ** (-(jnp.arange(half_size, dtype=wide) * 2.0) / HD)
    return places.astype(wide)[:, None] * inv_freq[None, :]


def adamw_step(gradient, first_old, second_old, weight, step_rate, decay_factor):
    first_new = beta_one * first_old + (1.0 - beta_one) * gradient
    second_new = beta_two * second_old + (1.0 - beta_two) * gradient * gradient
    first_hat = first_new / (1.0 - beta_one**STEP)
    second_hat = second_new / (1.0 - beta_two**STEP)
    updated = weight - step_rate * (
        first_hat / (jnp.sqrt(second_hat) + adam_eps) + decay_factor * weight
    )
    return (second_new, updated)


def params(limit=56):
    return pltpu.CompilerParams(
        vmem_limit_bytes=limit * MIB, dimension_semantics=("arbitrary",)
    )


def cost(micros):
    return pl.CostEstimate(flops=int(micros * 10**9), bytes_accessed=10**6, transcendentals=0)


def split_heads(pair, number):
    lane = lax.broadcasted_iota(jnp.int32, pair.shape, 1)
    zero = jnp.zeros_like(pair)
    turned = pltpu.roll(pair, HD, 1)
    low_a = 2 * number < HQ // HK
    low_b = 2 * number + 1 < HQ // HK
    first = jnp.where((lane < HD) == low_a, jnp.where(low_a, pair, turned), zero)
    second = jnp.where((lane < HD) == low_b, jnp.where(low_b, turned, pair), zero)
    return jnp.concatenate([first, second], axis=0)


def join_heads(both, number, half):
    low_a = 2 * number < HQ // HK
    low_b = 2 * number + 1 < HQ // HK
    first = jnp.where(low_a, both[:HD, :half], both[HD:, :half])
    second = jnp.where(low_b, both[:HD, half:], both[HD:, half:])
    return first, second


def key_mask(start, first_key, first_query, half, causal):
    key_row = lax.broadcasted_iota(jnp.int32, (half, half), 0)
    ok = key_row >= start - first_key
    if causal:
        ok &= key_row <= lax.broadcasted_iota(jnp.int32, (1, half), 1) + (first_query - first_key)
    return jnp.concatenate([ok, ok], axis=1)


def query_mask(start, first_key, first_query, half, causal):
    key = lax.broadcasted_iota(jnp.int32, (half, half), 1)
    ok = key >= jnp.concatenate([start - first_key] * (half // LANES), axis=1)
    if causal:
        ok &= key <= lax.broadcasted_iota(jnp.int32, (half, half), 0) + (first_query - first_key)
    return jnp.concatenate([ok, ok], axis=0)


def visit_blocks(meta, start_ref, half, pieces, visit):
    mine = meta[0]
    first_query = mine * 2 * half
    turned = start_ref.shape[2] == LANES
    mask_of = query_mask if turned else key_mask
    start_of = lambda sel: start_ref[sel] if turned else start_ref[sel, 0:1, :]
    for sel, block in ((0, 0), (1, 0), (1, 1)):
        mask = mask_of(
            start_of(sel), first_query + block * half, first_query + sel * half, half, sel == block
        )
        visit(sel, 0, block, mask)
    for piece in range(1, pieces):
        first_key = (mine - piece) * 2 * half

        def region(cut):
            for block in range(2):
                for sel in range(2):
                    if cut and block == 0:
                        mask = mask_of(start_of(sel), first_key, first_query, half, False)
                    else:
                        mask = start_of(sel) <= first_key + block * half
                        mask = jnp.concatenate([mask, mask], axis=0 if turned else 1)
                    visit(sel, piece, block, mask)

        pl.when(mine == piece)(functools.partial(region, True))
        pl.when(mine > piece)(functools.partial(region, False))


def forward_kernel(pieces, meta, pre_ref, cos_ref, sin_ref, start_ref, starts_ref, *refs):
    kv_refs = refs[:pieces]
    o_ref, lse_ref, q_ref, two_ref, top_ref, sum_ref, acc_ref = refs[pieces:]
    number = pl.program_id(0)
    rows = pre_ref.shape[0]
    half = rows // 2
    pre = pre_ref[...]
    lane = lax.broadcasted_iota(jnp.int32, pre.shape, 1)
    swapped = jnp.where(
        lane % HD < HD // 2, pltpu.roll(pre, LANES - HD // 2, 1), pltpu.roll(pre, HD // 2, 1)
    )
    turned = (pre * cos_ref[...] + swapped * sin_ref[...]).astype(low)
    turned = (turned.astype(wide) * (1.0 / HD**0.5)).astype(low)
    q_ref[...] = turned
    for which in range(2):
        two_ref[which] = split_heads(turned[which * half : (which + 1) * half, :], number)
    top_ref[...] = jnp.full_like(top_ref, masked_score)
    sum_ref[...] = jnp.zeros_like(sum_ref)
    acc_ref[...] = jnp.zeros_like(acc_ref)

    def scores_of(sel, piece, block):
        part = slice(block * half, (block + 1) * half)
        return lax.dot_general(
            two_ref[sel], kv_refs[piece][part, :LANES], NT, preferred_element_type=wide
        )

    def find_top(sel, piece, block, mask):
        scores = scores_of(sel, piece, block)
        if mask.shape[1] > LANES:
            scores = jnp.where(mask, scores, masked_score)
        peak = functools.reduce(jnp.maximum, [scores[:, i : i + LANES] for i in range(0, half, LANES)])
        if mask.shape[1] <= LANES:
            peak = jnp.where(mask, peak, masked_score)
        top_ref[sel] = jnp.maximum(top_ref[sel], peak)

    def sum_up(sel, piece, block, mask):
        part = slice(block * half, (block + 1) * half)
        scores = scores_of(sel, piece, block)
        level = top_ref[sel]
        if mask.shape[1] > LANES:
            scores = jnp.where(mask, scores, masked_score)
        else:
            level = jnp.where(mask, level, -masked_score)
        weights = [jnp.exp(scores[:, i : i + LANES] - level) for i in range(0, half, LANES)]
        sum_ref[sel] += functools.reduce(jnp.add, weights)
        acc_ref[sel] += jnp.dot(
            jnp.concatenate(weights, axis=1).astype(low),
            kv_refs[piece][part, LANES:],
            preferred_element_type=wide,
        )

    visit_blocks(meta, starts_ref, half, pieces, find_top)
    for which in range(2):
        top_ref[which] = jnp.broadcast_to(
            jnp.max(top_ref[which], axis=1, keepdims=True), top_ref.shape[1:]
        )
    visit_blocks(meta, starts_ref, half, pieces, sum_up)
    lane = lax.broadcasted_iota(jnp.int32, (half, LANES), 1)
    low_a = 2 * number < HQ // HK
    low_b = 2 * number + 1 < HQ // HK
    pick = jnp.where(lax.broadcasted_iota(jnp.int32, (8, LANES), 1) == 0, 1.0, 0.0).astype(wide)
    for which in range(2):
        total = jnp.sum(sum_ref[which], axis=1, keepdims=True)
        out = acc_ref[which] / total
        first, second = out[:half], out[half:]
        first = jnp.where(low_a, first, pltpu.roll(first, HD, 1))
        second = jnp.where(low_b, pltpu.roll(second, HD, 1), second)
        o_ref[which * half : (which + 1) * half, :] = jnp.where(lane < HD, first, second)
        lse = top_ref[which] + jnp.log(total)
        lse_ref[0, :, which * rows : (which + 1) * rows] = lax.dot_general(
            pick, lse, NT, precision=lax.Precision.HIGHEST, preferred_element_type=wide
        )


def attention_forward(pre, cos_wide, sin_wide, starts, kv_pieces, meta):
    rows, width = pre.shape
    pairs, pieces = width // LANES, len(kv_pieces)
    pair = pl.BlockSpec((rows, LANES), lambda p, m: (0, p))
    whole = lambda a: pl.BlockSpec(a.shape, lambda p, m: (0,) * a.ndim)
    starts_wide = jnp.broadcast_to(starts[:, 0, :, None], (2, rows // 2, LANES))
    operands = (cos_wide, sin_wide, starts, starts_wide, *kv_pieces)
    spec = pltpu.PrefetchScalarGridSpec(
        num_scalar_prefetch=1,
        grid=(pairs,),
        in_specs=[pair] + [whole(a) for a in operands],
        out_specs=[pair, pl.BlockSpec((1, 8, 2 * rows), lambda p, m: (p, 0, 0)), pair],
        scratch_shapes=[
            pltpu.VMEM((2, rows, LANES), low),
            pltpu.VMEM((2, rows, LANES), wide),
            pltpu.VMEM((2, rows, LANES), wide),
            pltpu.VMEM((2, rows, LANES), wide),
        ],
    )
    return pl.pallas_call(
        functools.partial(forward_kernel, pieces),
        grid_spec=spec,
        out_shape=[
            jax.ShapeDtypeStruct((rows, width), wide),
            jax.ShapeDtypeStruct((pairs, 8, 2 * rows), wide),
            jax.ShapeDtypeStruct((rows, width), low),
        ],
        compiler_params=params(48),
        cost_estimate=cost(40),
        name="attention_forward",
    )(meta, pre, *operands)


def backward_kernel(pieces, meta, q_ref, do_ref, o_ref, lse_ref, start_ref, cos_ref, sin_ref, *refs):
    kv_refs = refs[:pieces]
    dq_ref = refs[pieces]
    out_refs = refs[pieces + 1 : 2 * pieces + 1]
    kt_ref, two_ref, dot_ref, delta_ref, acc_ref, dkv_ref = refs[2 * pieces + 1 :]
    number = pl.program_id(0)
    rows = q_ref.shape[0]
    half = rows // 2

    @pl.when(number == 0)
    def _():
        dkv_ref[...] = jnp.zeros_like(dkv_ref)
        for piece in range(pieces):
            kt_ref[piece] = kv_refs[piece][:, :LANES].astype(wide).T.astype(low)

    acc_ref[...] = jnp.zeros_like(acc_ref)
    lane = lax.broadcasted_iota(jnp.int32, (8, LANES), 1)
    pick_a = jnp.where(lane < HD, 1.0, 0.0).astype(wide)
    pick_b = 1.0 - pick_a
    for which in range(2):
        part = slice(which * half, (which + 1) * half)
        two_ref[which] = split_heads(q_ref[part, :], number)
        dot_ref[which] = split_heads(do_ref[part, :], number)
        product = do_ref[part, :].astype(wide) * o_ref[part, :]
        delta_ref[which] = jnp.concatenate(
            [
                lax.dot_general(
                    pick, product, NT, precision=lax.Precision.HIGHEST, preferred_element_type=wide
                )
                for pick in (pick_a, pick_b)
            ],
            axis=1,
        )

    def visit(sel, piece, block, mask):
        part = slice(block * half, (block + 1) * half)
        two, dot = two_ref[sel], dot_ref[sel]
        keys, values = kv_refs[piece][part, :LANES], kv_refs[piece][part, LANES:]
        scores = lax.dot_general(keys, two, NT, preferred_element_type=wide)
        grad_weights = lax.dot_general(values, dot, NT, preferred_element_type=wide)
        lse = lse_ref[0, 0:1, sel * rows : (sel + 1) * rows]
        if mask.shape[0] > 1:
            weights = jnp.where(mask, jnp.exp(scores - lse), 0.0)
        else:
            weights = jnp.exp(scores - jnp.where(mask, lse, -masked_score))
        grad_scores = (weights * (grad_weights - delta_ref[sel, 0:1, :])).astype(low)
        dkv_ref[piece, part, LANES:] += jnp.dot(
            weights.astype(low), dot, preferred_element_type=wide
        )
        dkv_ref[piece, part, :LANES] += jnp.dot(grad_scores, two, preferred_element_type=wide)
        acc_ref[sel] += jnp.dot(kt_ref[piece, :, part], grad_scores, preferred_element_type=wide)

    visit_blocks(meta, start_ref, half, pieces, visit)
    for which in range(2):
        part = slice(which * half, (which + 1) * half)
        cos, sin = cos_ref[:, part], sin_ref[:, part]
        turned = []
        for head in join_heads(acc_ref[which] * (1.0 / HD**0.5), number, half):
            upper, lower = head[: HD // 2], head[HD // 2 :]
            turned += [upper * cos + lower * sin, lower * cos - upper * sin]
        dq_ref[part, :] = jnp.concatenate(turned, axis=0).T.astype(low)

    @pl.when(number == pl.num_programs(0) - 1)
    def _():
        for piece in range(pieces):
            out_refs[piece][...] = dkv_ref[piece].astype(out_refs[piece].dtype)


def attention_backward(q, do, o, lse, starts, cos_turned, sin_turned, kv_pieces, meta):
    rows, width = q.shape
    pairs, pieces = width // LANES, len(kv_pieces)
    pair = pl.BlockSpec((rows, LANES), lambda p, m: (0, p))
    whole = lambda a: pl.BlockSpec(a.shape, lambda p, m: (0,) * a.ndim)
    fixed = (starts, cos_turned, sin_turned, *kv_pieces)
    spec = pltpu.PrefetchScalarGridSpec(
        num_scalar_prefetch=1,
        grid=(pairs,),
        in_specs=[pair, pair, pair, pl.BlockSpec((1, 8, 2 * rows), lambda p, m: (p, 0, 0))]
        + [whole(a) for a in fixed],
        out_specs=[pair] + [whole(a) for a in kv_pieces],
        scratch_shapes=[
            pltpu.VMEM((pieces, LANES, rows), low),
            pltpu.VMEM((2, rows, LANES), low),
            pltpu.VMEM((2, rows, LANES), low),
            pltpu.VMEM((2, 8, rows), wide),
            pltpu.VMEM((2, LANES, rows), wide),
            pltpu.VMEM((pieces, rows, 2 * LANES), wide),
        ],
    )
    return pl.pallas_call(
        functools.partial(backward_kernel, pieces),
        grid_spec=spec,
        out_shape=[jax.ShapeDtypeStruct((rows, width), low)]
        + [
            jax.ShapeDtypeStruct((rows, 2 * LANES), wide if piece == 0 else low)
            for piece in range(pieces)
        ],
        compiler_params=params(48),
        cost_estimate=cost(40),
        name="attention_backward",
    )(meta, q, do, o, lse, *fixed)


def feed_kernel(
    steps, fresh, place, n_a, n_b, cot_ref, gateup_ref, down_ref, *refs
):
    refs = refs[0 if fresh else 5 :]
    back_a, back_b, left_ref, right_ref, hidden_ref, grad_ref, kept_ref = refs
    width = down_ref.shape[0]
    first = pl.program_id(0) < steps // 2
    normed = jnp.where(first, n_a[...], n_b[...])
    cot = cot_ref[...]
    gate = jnp.dot(normed, gateup_ref[:, :width], preferred_element_type=wide)
    up = jnp.dot(normed, gateup_ref[:, width:], preferred_element_type=wide)
    grad_hidden = lax.dot_general(cot, down_ref[...], NT, preferred_element_type=wide)
    sigmoid = jax.nn.sigmoid(gate)
    act = gate * sigmoid
    hidden = (act * up).astype(low)
    grad_gate = (grad_hidden * up * sigmoid * (1.0 + gate * (1.0 - sigmoid))).astype(low)
    grad_up = (grad_hidden * act).astype(low)
    kept_ref[...] = normed
    hidden_ref[...] = hidden
    grad_ref[:, :width] = grad_gate
    grad_ref[:, width:] = grad_up
    out = jnp.dot(hidden, down_ref[...], preferred_element_type=wide).astype(low)
    left_ref[...] = out[:, : left_ref.shape[1]]
    right_ref[...] = out[:, left_ref.shape[1] :]
    back = lax.dot_general(grad_gate, gateup_ref[:, :width], NT, preferred_element_type=wide)
    back = back + lax.dot_general(grad_up, gateup_ref[:, width:], NT, preferred_element_type=wide)

    @pl.when(first)
    def _():
        back_a[...] = back.astype(low)

    @pl.when(jnp.logical_not(first))
    def _():
        back_b[...] = back.astype(low)


def feed_forward(n_a, n_b, cot_all, gateup, down, place, kept, block=256):
    rows, d = n_a.shape
    total, width = cot_all.shape[0], down.shape[0]
    block = min(block, rows)
    left = padded(d // 2, LANES)
    each = rows // block
    steps = 2 * each
    spot = lambda i, place: (place[i // each] * each + i % each, 0)
    whole = lambda a: pl.BlockSpec(a.shape, lambda i, place: (0, 0))
    halves = [
        pl.BlockSpec((block, d), lambda i, place: (jnp.minimum(i, each - 1), 0)),
        pl.BlockSpec((block, d), lambda i, place: (jnp.maximum(i - each, 0), 0)),
    ]
    in_specs = halves + [
        pl.BlockSpec((block, d), spot),
        whole(gateup),
        whole(down),
    ]
    fresh = kept is None
    if not fresh:
        in_specs += [pl.BlockSpec(memory_space=pl.ANY)] * 5
    spec = pltpu.PrefetchScalarGridSpec(
        num_scalar_prefetch=1,
        grid=(steps,),
        in_specs=in_specs,
        out_specs=halves
        + [pl.BlockSpec((block, n), spot) for n in (left, d - left, width, 2 * width, d)],
    )
    shapes = [(rows, d)] * 2 + [(total, n) for n in (left, d - left, width, 2 * width, d)]
    return pl.pallas_call(
        functools.partial(feed_kernel, steps, fresh),
        grid_spec=spec,
        out_shape=[jax.ShapeDtypeStruct(s, low) for s in shapes],
        input_output_aliases={} if fresh else {6 + i: 2 + i for i in range(5)},
        compiler_params=params(),
        cost_estimate=cost(4),
        name="feed_forward",
    )(place, n_a, n_b, cot_all, gateup, down, *(() if fresh else kept))


def weight_kernel(steps, shape, take, give, split, fill, where, x_ref, y_ref, *refs):
    outputs = 2 if split else 1
    acc_ref = refs[-1]
    out_refs = refs[-1 - outputs : -1]
    chips, cores, groups = shape
    step = pl.program_id(0)
    size = x_ref.shape[1]
    product = lax.dot_general(x_ref[...], y_ref[...], TN, preferred_element_type=wide)

    @pl.when(step == 0)
    def _():
        acc_ref[:size] = product
        acc_ref[size:] = jnp.zeros_like(acc_ref[size:])

    @pl.when(step > 0)
    def _():
        acc_ref[:size] += product

    keep = lax.broadcasted_iota(jnp.int32, (give, 1), 0) < take

    def write(mine):
        for chip in range(chips):
            for core in range(cores):
                for group in range(groups):
                    low_edge = ((chip * cores + core) * groups + group) * take
                    value = jnp.where(keep, acc_ref[low_edge : low_edge + give], 0.0)
                    if fill:
                        value += refs[0][low_edge // take].astype(wide)
                    value = value.astype(low)
                    at = lax.rem(group + groups - where[2], groups)
                    if split:
                        out_refs[core ^ mine][chip ^ where[1], at] = value
                    else:
                        row = (chip * cores + core) * give
                        out_refs[0][at, row : row + give] = value

    if split:
        for mine in range(cores):
            pl.when((step == steps - 1) & (where[0] == mine))(functools.partial(write, mine))
    else:
        pl.when(step == steps - 1)(functools.partial(write, 0))


def weight_gradient(
    x, y, shape, take, where, split=False, block=1024, column=0, columns=1, into=None, extra=None
):
    total, size = x.shape
    width = y.shape[1]
    give = padded(take, ROWS) if extra is None else extra.shape[1]
    block = min(block, total)
    steps = total // block
    chips, cores, groups = shape
    if split:
        out = pl.BlockSpec((chips, groups, give, width), lambda i, w: (0, 0, 0, column))
        shapes = [(chips, groups, give, columns * width)] * 2
    else:
        out = pl.BlockSpec((groups, chips * cores * give, width), lambda i, w: (0, 0, 0))
        shapes = [(groups, chips * cores * give, width)]
    fill = extra is not None
    into = [] if into is None else into
    return pl.pallas_call(
        functools.partial(weight_kernel, steps, shape, take, give, split, fill),
        grid_spec=pltpu.PrefetchScalarGridSpec(
            num_scalar_prefetch=1,
            grid=(steps,),
            in_specs=[
                pl.BlockSpec((block, size), lambda i, w: (i, 0)),
                pl.BlockSpec((block, width), lambda i, w: (i, 0)),
            ]
            + [pl.BlockSpec(extra.shape, lambda i, w: (0, 0, 0)) for _ in range(fill)]
            + [pl.BlockSpec(memory_space=pl.ANY)] * len(into),
            out_specs=[out] * len(shapes),
            scratch_shapes=[pltpu.VMEM((padded(size, 8) + give, width), wide)],
        ),
        out_shape=[jax.ShapeDtypeStruct(shape, low) for shape in shapes],
        input_output_aliases={3 + fill + i: i for i in range(len(into))},
        compiler_params=params(),
        cost_estimate=cost(1 if steps > 1 else 0.2),
        name="weight_gradient",
    )(where, x, y, *([extra] if fill else []), *into)


def assemble_kernel(
    n_dp, n_group, take, give, meta, own_ref, other_ref, o_ref, small_ref, at_ref, acc_ref
):
    me, mine = meta[0], meta[1]
    for r in range(n_dp):
        source = own_ref if r % 2 == 0 else other_ref
        for s in range(n_group):
            row = (r // 2 * n_group + s) * give
            z = lax.rem(mine + s, n_group)
            at_ref[(me ^ r) * n_group + z] = source[row : row + give].astype(wide)
    for i in range(n_dp * n_group):
        acc_ref[i * take : i * take + give] = at_ref[i]
        for j in range(2):
            small_ref[j, i : i + 1] = at_ref[i, take + j : take + j + 1]
    size = o_ref.shape[0]
    o_ref[...] = acc_ref[:size].astype(low)


def assemble(own, other, n_dp, n_group, take, give, me, mine):
    width = own.shape[1]
    size = n_dp * n_group * take
    return pl.pallas_call(
        functools.partial(assemble_kernel, n_dp, n_group, take, give),
        grid_spec=pltpu.PrefetchScalarGridSpec(
            num_scalar_prefetch=1,
            grid=(1,),
            in_specs=[pl.BlockSpec(own.shape, lambda i, m: (0, 0))] * 2,
            out_specs=[
                pl.BlockSpec((size, width), lambda i, m: (0, 0)),
                pl.BlockSpec((2, n_dp * n_group, width), lambda i, m: (0, 0, 0)),
            ],
            scratch_shapes=[
                pltpu.VMEM((n_dp * n_group, give, width), wide),
                pltpu.VMEM((size + give, width), wide),
            ],
        ),
        out_shape=[
            jax.ShapeDtypeStruct((size, width), low),
            jax.ShapeDtypeStruct((2, n_dp * n_group, width), wide),
        ],
        compiler_params=params(),
        cost_estimate=cost(1),
        name="assemble_rows",
    )(jnp.stack([me, mine]).astype(jnp.int32), own, other)


def stack_kernel(outer, count, take, give, meta, *refs):
    o_ref, at_ref, acc_ref = refs[count:]
    for s in range(count):
        z = lax.rem(meta[0] + s, count)
        for i in range(outer):
            at_ref[i * count + z] = refs[s][i * give : (i + 1) * give].astype(wide)
    for i in range(outer * count):
        acc_ref[i * take : i * take + give] = at_ref[i]
    size = outer * count * take
    o_ref[:size] = acc_ref[:size].astype(low)
    if o_ref.shape[0] > size:
        o_ref[size:] = jnp.zeros_like(o_ref[size:])


def stack_rows(pieces, outer, take, me, rows):
    count, width = len(pieces), pieces[0].shape[1]
    give = pieces[0].shape[0] // outer
    whole = lambda r: pl.BlockSpec((r, width), lambda i, m: (0, 0))
    return pl.pallas_call(
        functools.partial(stack_kernel, outer, count, take, give),
        grid_spec=pltpu.PrefetchScalarGridSpec(
            num_scalar_prefetch=1,
            grid=(1,),
            in_specs=[whole(outer * give)] * count,
            out_specs=whole(rows),
            scratch_shapes=[
                pltpu.VMEM((outer * count, give, width), wide),
                pltpu.VMEM((padded(outer * count * take, 8) + give, width), wide),
            ],
        ),
        out_shape=jax.ShapeDtypeStruct((rows, width), low),
        compiler_params=params(),
        cost_estimate=cost(1),
        name="stack_rows",
    )(me, *pieces)


def cut_kernel(count, part, part_wide, w_ref, o_ref, buffer_ref):
    rows = w_ref.shape[0]
    buffer_ref[...] = jnp.zeros_like(buffer_ref)
    for p in range(count):
        for j in range(2):
            column = (j * count + p) * part
            buffer_ref[:rows, j * part_wide : j * part_wide + part] = w_ref[
                :, column : column + part
            ]
        o_ref[p] = buffer_ref[...].astype(low)


def cut_columns(weight, count, part_wide, give):
    rows, width = weight.shape
    part = width // (2 * count)
    shape = (count, give, 2 * part_wide)
    return pl.pallas_call(
        functools.partial(cut_kernel, count, part, part_wide),
        grid=(1,),
        in_specs=[pl.BlockSpec(weight.shape, lambda i: (0, 0))],
        out_specs=pl.BlockSpec(shape, lambda i: (0, 0, 0)),
        out_shape=jax.ShapeDtypeStruct(shape, low),
        scratch_shapes=[pltpu.VMEM((give, 2 * part_wide), wide)],
        compiler_params=params(),
        cost_estimate=cost(1),
        name="cut_columns",
    )(weight)


def update_kernel(count, part, part_wide, g_ref, m_ref, v_ref, w_ref, go_ref, vo_ref, wo_ref):
    rows = w_ref.shape[0]
    for p in range(count):
        piece = g_ref[p].astype(wide)
        for j in range(2):
            column = (j * count + p) * part
            go_ref[:, column : column + part] = piece[
                :rows, j * part_wide : j * part_wide + part
            ]
    vo_ref[...], wo_ref[...] = adamw_step(
        go_ref[...], m_ref[...], v_ref[...], w_ref[...], rate_proj, decay_rate
    )


def update_columns(pieces, first, second, weight):
    count, _, width = pieces.shape
    spec = pl.BlockSpec(weight.shape, lambda i: (0, 0))
    return pl.pallas_call(
        functools.partial(
            update_kernel, count, weight.shape[1] // (2 * count), width // 2
        ),
        grid=(1,),
        in_specs=[pl.BlockSpec(pieces.shape, lambda i: (0, 0, 0))] + [spec] * 3,
        out_specs=[spec] * 3,
        out_shape=[jax.ShapeDtypeStruct(weight.shape, wide)] * 3,
        compiler_params=params(),
        cost_estimate=cost(1),
        name="update_columns",
    )(pieces, first, second, weight)


def flip(value, mask):
    count = lax.axis_size("dp")
    return lax.ppermute(value, "dp", [(i, i ^ mask) for i in range(count)])


def shift(value, step):
    count = lax.axis_size("group")
    return lax.ppermute(value, "group", [((i + step) % count, i) for i in range(count)])


def after(value, *others):
    return lax.optimization_barrier((value, *others))[0]


def group_pieces(block, steps=None):
    return [block] + [shift(block, s) for s in range(1, lax.axis_size("group"))]


def group_send(blocks):
    count = lax.axis_size("group")
    return [blocks[0]] + [shift(blocks[count - s].astype(low), s) for s in range(1, count)]


def add_up(terms):
    return functools.reduce(jnp.add, [term.astype(wide) for term in terms])


def gather_column(block):
    return jnp.concatenate(group_pieces(block), axis=0)


def gather_chips(column):
    evens = [column] + [flip(column, r) for r in range(2, lax.axis_size("dp"), 2)]
    return jnp.concatenate(evens, axis=0)


def gather_rows(own, other, take):
    n_dp, n_group = lax.axis_size("dp"), lax.axis_size("group")
    give = own.shape[0] // (n_dp // 2 * n_group)
    return assemble(
        own, other, n_dp, n_group, take, give, lax.axis_index("dp"), lax.axis_index("group")
    )


def scatter_chips(keep, send):
    pair = keep.astype(wide) + flip(send, 1).astype(wide)
    got = [flip(pair[r].astype(low), 2 * r) for r in range(1, pair.shape[0])]
    return add_up([pair[0]] + got)


def split_low(value):
    first = lax.reduce_precision(value, 8, 7)
    rest = value - first
    second = lax.reduce_precision(rest, 8, 7)
    return [first.astype(low), second.astype(low), (rest - second).astype(low)]


def body(
    tokens,
    positions,
    cotangent,
    query_weight,
    query_first,
    query_second,
    keyval_weight,
    keyval_first,
    keyval_second,
    output_weight,
    output_first,
    output_second,
    gateup_weight,
    gateup_first,
    gateup_second,
    down_weight,
    down_first,
    down_second,
    small_weight,
    small_first,
    small_second,
):
    row_count = tokens.shape[0]
    half = row_count // 2
    n_dp = lax.axis_size("dp")
    group_size = lax.axis_size("group")
    device_count = n_dp * group_size
    my_dp = lax.axis_index("dp")
    my_index = lax.axis_index("group")
    flat_index = my_dp * group_size + my_index
    seq_len = row_count * group_size
    query_width = HQ * HD
    kv_width = HK * HD
    small_size = 2 * D + query_width + 2 * kv_width
    rest_length = small_size - kv_width
    rest_piece = rest_length // device_count
    value_piece = kv_width // device_count
    small_piece = small_size // device_count
    part = FF // n_dp
    part_wide = padded(part, LANES)
    in_rows = query_weight.shape[0]
    in_give = padded(in_rows + 2, ROWS)
    down_rows = down_weight.shape[0]

    small_rows = [small_weight.astype(low)] + split_low(small_second)
    small_rows = jnp.concatenate(small_rows).reshape(2, 2 * small_piece)
    small_rows = jnp.pad(small_rows, ((0, 0), (0, 2 * kv_width - 2 * small_piece)))
    keyval_block = jnp.concatenate([keyval_weight.astype(low), small_rows], axis=0)
    keyval_block = jnp.pad(keyval_block, ((0, in_give - in_rows - 2), (0, 0)))
    keyval_column = gather_column(keyval_block)
    keyval_own = gather_chips(keyval_column)
    keyval_full, small_all = gather_rows(keyval_own, flip(keyval_own, 1), in_rows)
    small_all = small_all[:, :, : 2 * small_piece].reshape(2, device_count, 2, small_piece)
    small_values = small_all[0, :, 0].reshape(small_size)
    small_second_all = (small_all[0, :, 1] + small_all[1, :, 0] + small_all[1, :, 1]).reshape(
        small_size
    )
    both_block = jnp.concatenate([query_weight.astype(low), output_weight.astype(low)], axis=1)
    both_block = jnp.pad(both_block, ((0, in_give - in_rows), (0, 0)))
    both_column = gather_column(after(both_block, keyval_column))
    both_own = gather_chips(after(both_column, keyval_full))
    both_other = flip(both_own, 1)
    cot_all = lax.all_gather(after(cotangent, both_own), "dp", axis=0, tiled=True)
    gateup_pieces = cut_columns(gateup_weight, n_dp, part_wide, in_give)
    gateup_column = lax.all_to_all(after(gateup_pieces, keyval_column), "dp", 0, 0, tiled=True)
    down_block = jnp.pad(down_weight.astype(low), ((0, padded(down_rows, ROWS) - down_rows), (0, 0)))
    down_pieces = group_pieces(after(down_block, keyval_column))
    me_group = my_index.astype(jnp.int32)[None]
    down_part = stack_rows(down_pieces, 1, down_rows, me_group, part_wide)

    gain_one = small_values[:D]
    gain_two = small_values[D : 2 * D]
    bias_qkv = small_values[2 * D :]
    place_row = positions[0]
    local_index = my_index * row_count + jnp.arange(row_count, dtype=jnp.int32)
    local_places = lax.dynamic_slice_in_dim(place_row, my_index * row_count, row_count, 0)
    starts = (local_index - local_places).reshape(2, half).astype(jnp.int32)
    starts = jnp.broadcast_to(starts[:, None, :], (2, 8, half))
    meta = jnp.stack([my_index, my_index]).astype(jnp.int32)
    angles = rotary_angles(local_places)
    cosine, sine_table = jnp.cos(angles), jnp.sin(angles)
    cos_wide = jnp.concatenate([cosine] * 4, axis=1)
    sin_wide = jnp.concatenate([-sine_table, sine_table] * 2, axis=1)

    def swap(values):
        quarter = HD // 2
        pieces = [values[:, i * quarter : (i + 1) * quarter] for i in range(2 * HK)]
        return jnp.concatenate([pieces[i ^ 1] for i in range(2 * HK)], axis=1)

    act_in = tokens.astype(wide)
    inv_one = lax.rsqrt(jnp.mean(act_in * act_in, axis=1, keepdims=True) + norm_eps)
    scaled_one = act_in * inv_one
    normed_one = (scaled_one * gain_one).astype(low)
    keyval_pre = (
        jnp.dot(normed_one, keyval_full, preferred_element_type=wide) + bias_qkv[query_width:]
    )
    key_pre = keyval_pre[:, :kv_width]
    key_low = (key_pre * cos_wide + swap(key_pre) * sin_wide).astype(low)
    keyval_low = jnp.concatenate([key_low, keyval_pre[:, kv_width:].astype(low)], axis=1)
    keyval_low = after(keyval_low, gateup_column, down_pieces)
    both_full, _ = gather_rows(after(both_own, keyval_low), both_other, in_rows)
    query_full, output_full = both_full[:, :query_width], both_full[:, query_width:]
    keyval_parts = group_pieces(keyval_low)
    keyval_parts = [keyval_parts[-s % group_size] for s in range(group_size)]
    query_pre = (
        jnp.dot(normed_one, query_full, preferred_element_type=wide) + bias_qkv[:query_width]
    )
    keyval_parts = after(keyval_parts, query_pre)
    gateup_column = after(gateup_column, *keyval_parts).reshape(n_dp * in_give, 2 * part_wide)
    gateup_pieces = group_pieces(gateup_column)
    attn_float, log_total, query_low = attention_forward(
        query_pre, cos_wide, sin_wide, starts, keyval_parts, meta
    )
    attn_float = after(attn_float, gateup_pieces)
    gateup_part = stack_rows(gateup_pieces, n_dp, in_rows, me_group, D)
    attn_low = attn_float.astype(low)
    middle = act_in + jnp.dot(attn_low, output_full, preferred_element_type=wide)
    inv_two = lax.rsqrt(jnp.mean(middle * middle, axis=1, keepdims=True) + norm_eps)
    scaled_two = middle * inv_two
    normed_two = (scaled_two * gain_two).astype(low)

    chips = n_dp // 2
    kept, sides, back = None, {0: normed_two}, {}
    for k in range(1, chips):
        if n_dp != 8 or k != 3:
            sides[k] = flip(normed_two, 2 * k)

    def visit(k, kept):
        place = jnp.stack([my_dp ^ (2 * k), my_dp ^ (2 * k + 1)]).astype(jnp.int32)
        back_a, back_b, *kept = feed_forward(
            sides[k], flip(sides[k], 1), cot_all, gateup_part, down_part, place, kept
        )
        back[k] = (back_a, flip(back_b, 1))
        return kept

    if n_dp == 8:
        kept = visit(0, kept)
        sides[1], sides[2] = after((sides[1], sides[2]), kept)
        across = [flip(sides[1][:half], 4), flip(sides[2][half:], 2)]
        kept = visit(1, kept)
        sides[3] = jnp.concatenate(across, axis=0)
        kept = visit(3, kept)
        corner = add_up(back[3]).astype(low)
        across = [flip(corner[:half], 2), flip(corner[half:], 4)]
        kept = visit(2, kept)
        nothing = jnp.zeros_like(across[0])
        x_sum = add_up([*back[1], jnp.concatenate([nothing, across[1]], axis=0)]).astype(low)
        y_sum = add_up([*back[2], jnp.concatenate([across[0], nothing], axis=0)]).astype(low)
        kept, y_sum = after((kept, y_sum))
        returned = [*back[0], flip(x_sum, 2), flip(y_sum, 4)]
    else:
        for k in range(chips):
            kept = visit(k, kept)
        returned = list(back[0])
        returned += [flip(add_up(back[k]).astype(low), 2 * k) for k in range(1, chips)]
    out_left, out_right, hidden_all, gate_all, normed_all = kept
    pieces = (n_dp // 2, 2, group_size)
    device = jnp.stack([my_dp & 1, my_dp >> 1, my_index]).astype(jnp.int32)
    (gateup_term,) = weight_gradient(normed_all, gate_all, pieces, in_rows, device)
    gateup_got = group_send(gateup_term)
    (down_term,) = weight_gradient(hidden_all, cot_all, (1, 1, group_size), down_rows, device)
    down_got = group_send(down_term)
    returned = after(returned, gateup_term, down_term)
    grad_normed_two = add_up(returned)
    out_left = lax.psum_scatter(after(out_left, returned), "dp", scatter_dimension=0, tiled=True)

    grad_out = cotangent.astype(wide)
    gain_scaled_two = grad_normed_two * gain_two
    gain_two_term = jnp.sum(grad_normed_two * scaled_two, axis=0)
    grad_middle = grad_out + inv_two * (
        gain_scaled_two - scaled_two * jnp.mean(gain_scaled_two * scaled_two, axis=1, keepdims=True)
    )
    grad_middle_low = grad_middle.astype(low)
    grad_attn_low = lax.dot_general(
        grad_middle_low, output_full, NT, preferred_element_type=wide
    ).astype(low)
    both_terms = weight_gradient(
        attn_low, grad_middle_low, pieces, in_rows, device, split=True, column=1, columns=2
    )
    grad_query_pre, *keyval_terms = attention_backward(
        query_low,
        grad_attn_low,
        attn_float,
        log_total,
        starts,
        cosine.T,
        sine_table.T,
        keyval_parts,
        meta,
    )
    grad_query_pre, keyval_terms = after(
        (grad_query_pre, keyval_terms), down_got, gateup_got[:-1], out_left
    )
    keyval_got = [keyval_terms[0]] + [shift(keyval_terms[s], s) for s in range(1, group_size)]
    out_right = lax.psum_scatter(
        after(out_right, grad_query_pre), "dp", scatter_dimension=0, tiled=True
    )
    both_terms = weight_gradient(
        normed_one, grad_query_pre, pieces, in_rows, device, split=True, columns=2, into=both_terms
    )
    both_total = scatter_chips(*both_terms)
    grad_normed_one = lax.dot_general(grad_query_pre, query_full, NT, preferred_element_type=wide)
    keyval_grads = add_up(keyval_got)
    down_grad = add_up(after(down_got, keyval_grads))[:down_rows]
    gateup_sum = add_up(after(gateup_got, keyval_grads)).reshape(n_dp, -1, 2 * part_wide)
    gateup_sum = lax.all_to_all(gateup_sum.astype(low), "dp", 0, 0, tiled=True)
    gateup_grad, gateup_second_out, gateup_weight_out = update_columns(
        gateup_sum, gateup_first, gateup_second, gateup_weight
    )
    key_grads, value_grads = keyval_grads[:, :kv_width], keyval_grads[:, kv_width:]
    key_grads = key_grads * cos_wide - swap(key_grads) * sin_wide
    grad_keyval_pre = jnp.concatenate([key_grads, value_grads], axis=1).astype(low)
    bias_term = jnp.concatenate(
        [
            jnp.sum(grad_query_pre.astype(wide), axis=0),
            jnp.sum(grad_keyval_pre.astype(wide), axis=0),
        ]
    )
    grad_normed_one = grad_normed_one + lax.dot_general(
        grad_keyval_pre, keyval_full, NT, preferred_element_type=wide
    )
    gain_scaled_one = grad_normed_one * gain_one
    gain_one_term = jnp.sum(grad_normed_one * scaled_one, axis=0)
    grad_input = grad_middle + inv_one * (
        gain_scaled_one - scaled_one * jnp.mean(gain_scaled_one * scaled_one, axis=1, keepdims=True)
    )
    tokens_grad = grad_input.astype(low)
    out_sum = jnp.concatenate([out_left, out_right], axis=1).astype(wide)
    layer_out = (middle + out_sum).astype(low)
    small_term = jnp.concatenate([gain_one_term, gain_two_term, bias_term])

    small_blocks = jnp.concatenate(
        [
            small_term.reshape(device_count, small_piece),
            small_term[:rest_length].reshape(device_count, rest_piece),
            small_term[rest_length:].reshape(device_count, value_piece),
        ],
        axis=1,
    )
    small_width = small_blocks.shape[1]
    small_two = jnp.stack(split_low(small_blocks)[:2], axis=1)
    small_two = jnp.pad(small_two, ((0, 0), (0, 0), (0, 2 * kv_width - small_width)))
    small_two = jnp.pad(small_two, ((0, 0), (in_rows, in_give - in_rows - 2), (0, 0)))
    last_terms = weight_gradient(
        normed_one, grad_keyval_pre, pieces, in_rows, device, split=True, extra=small_two
    )
    last_total = scatter_chips(*last_terms)
    some = last_total.shape[1] - both_total.shape[1]
    both_total = jnp.pad(both_total, ((0, 0), (0, some), (0, 0)))
    every_sum = add_up(group_send(jnp.concatenate([both_total, last_total], axis=2)))
    query_grad = every_sum[:in_rows, :query_width]
    output_grad = every_sum[:in_rows, query_width : query_width + D]
    last_sum = every_sum[:, query_width + D :]
    keyval_grad = last_sum[:in_rows]
    small_sum = last_sum[in_rows, :small_width] + last_sum[in_rows + 1, :small_width]
    small_grad = small_sum[:small_piece]
    rest_grad = small_sum[small_piece : small_piece + rest_piece]
    value_grad = small_sum[small_piece + rest_piece :]

    query_second_out, query_weight_out = adamw_step(
        query_grad, query_first, query_second, query_weight, rate_proj, decay_rate
    )
    keyval_second_out, keyval_weight_out = adamw_step(
        keyval_grad, keyval_first, keyval_second, keyval_weight, rate_proj, decay_rate
    )
    output_second_out, output_weight_out = adamw_step(
        output_grad, output_first, output_second, output_weight, rate_out, decay_rate
    )
    down_second_out, down_weight_out = adamw_step(
        down_grad, down_first, down_second, down_weight, rate_proj, decay_rate
    )
    _, small_weight_out = adamw_step(
        small_grad, small_first, small_second, small_weight, rate_small, 0.0
    )
    rest_second = lax.dynamic_slice_in_dim(
        small_second_all, flat_index * rest_piece, rest_piece, 0
    )
    value_second = lax.dynamic_slice_in_dim(
        small_second_all, rest_length + flat_index * value_piece, value_piece, 0
    )
    small_second_out = beta_two * rest_second + (1.0 - beta_two) * rest_grad * rest_grad
    value_bias_second_out = beta_two * value_second + (1.0 - beta_two) * value_grad * value_grad
    return (
        layer_out,
        tokens_grad,
        query_grad,
        query_second_out,
        query_weight_out,
        keyval_grad,
        keyval_second_out,
        keyval_weight_out,
        output_grad,
        output_second_out,
        output_weight_out,
        gateup_grad,
        gateup_second_out,
        gateup_weight_out,
        down_grad,
        down_second_out,
        down_weight_out,
        small_grad,
        small_second_out,
        value_bias_second_out,
        small_weight_out,
    )


def solution(mesh):
    rows = P(("dp", "group"), None)
    line = P(("dp", "group"))
    in_specs = (rows, P("dp", None)) + (rows,) * 16 + (line,) * 3
    out_specs = (rows,) * 17 + (line,) * 4
    return jax.shard_map(body, mesh=mesh, in_specs=in_specs, out_specs=out_specs, check_vma=False)
```

time: 2200 us -> 520 us (0.24)
  blocking collectives: 1680 us -> 0 us
  matrix products: 280 us -> 11.5 us
  waiting for transfers between devices: 20.7 us -> 188 us
  Pallas kernels: 0 us -> 162 us
  local copies, waits for them, and re-layouts: 87 us -> 23.9 us
    unnamed x4 -> x0, blocking collectives: 1570 us -> none
    dot_general x39 -> x6, matrix products: 280 us -> 11.5 us  [the longest x1 3.96 us: body(): jnp.dot(normed_one, query_full, preferred_element_type=wide)]
    ppermute x0 -> x59, waiting for transfers between devices: none -> 188 us  [the longest x27 134 us: shift(): lax.ppermute(value, 'group', [((i + step) % count, i) for i in range(coun...]
    pallas_call x0 -> x17, Pallas kernels: none -> 162 us  [the longest x4 65.6 us: feed_forward(): pl.pallas_call(functools.partial(feed_kernel, steps, fresh), grid_spec=sp...]
    all_gather x3 -> x0, blocking collectives: 109 us -> none  [the longest x1 71.8 us: body(): lax.all_gather(keyval_low_w, ('dp', 'group'), axis=0, tiled=True)]
    unnamed x221 -> x163, local copies, waits for them, and re-layouts: 80.6 us -> 12.6 us
    ppermute x0 -> x59, starting transfers between devices: none -> 60 us  [the longest x27 35.8 us: shift(): lax.ppermute(value, 'group', [((i + step) % count, i) for i in range(coun...]
    unnamed x17 -> x0, starting transfers between devices: 50.4 us -> none
  transfers between devices with their start and end apart: 23 -> 64, of which waited for: 1 -> 20; matrix products, arithmetic and copies ran while one was open for 76% -> 13% of each run, Pallas kernels for 0% -> 31%
where the time goes in v1:
time: 520 us; the launch traced here: 512 us
  waiting for transfers between devices  188 us (36%)
  Pallas kernels  162 us (31%)
  starting transfers between devices  67.2 us (13%)
  other arithmetic  43.9 us (8%)
  local copies, waits for them, and re-layouts  23.9 us (5%)
  between operations  15.3 us (3%)
  matrix products  11.5 us (2%)
    ppermute x27, waiting for transfers between devices, shift(): lax.ppermute(value, 'group', [((i + step) % count, i) for i in range(coun...  134 us
    pallas_call x4, Pallas kernels, feed_forward(): pl.pallas_call(functools.partial(feed_kernel, steps, fresh), grid_spec=sp...  65.6 us
    ppermute x32, waiting for transfers between devices, flip(): return lax.ppermute(value, 'dp', [(i, i ^ mask) for i in range(count)])  54.5 us
    pallas_call x5, Pallas kernels, weight_gradient(): pl.pallas_call(functools.partial(weight_kernel, steps, shape, take, give,...  41 us
    ppermute x27, starting transfers between devices, shift(): lax.ppermute(value, 'group', [((i + step) % count, i) for i in range(coun...  35.8 us
    ppermute x32, starting transfers between devices, flip(): return lax.ppermute(value, 'dp', [(i, i ^ mask) for i in range(count)])  24.2 us
    pallas_call x1, Pallas kernels, attention_forward(): pl.pallas_call(functools.partial(forward_kernel, pieces), grid_spec=spec,...  16.5 us
    pallas_call x1, Pallas kernels, attention_backward(): pl.pallas_call(functools.partial(backward_kernel, pieces), grid_spec=spec...  15.6 us
  transfers between devices with their start and end apart: 64, of which 20 were waited for; matrix products, arithmetic and copies ran while one was open for 13% of the time, Pallas kernels for 31%

profile of v1, /device:TPU:0, one launch (start us, length us, event | category | flops | bytes accessed | tf_op | source)
XLA Modules:
  0.0 511.9 jit_solution(14364905063258543606)
XLA Ops:
  9.5 5.1 collective-permute-start
  41.9 9.2 %collective-permute-done.10 = bf16[128,1792]{1,0:T(8,128)(2,1)S(1)} collective-permute-done((bf16[128,1792]{1,0:T(8,128)(2,1)S(1)}, bf16[128,1792]{1,0:T(8,128)(2,1)S(1)}, u32[]{:S(2)}, u32[]{:S(2)}) %collective-permute-start.10) | collective-permute-done | bytes 458784 | tf_op jit(solution)/shard_map/ppermute | solution.py:647
  51.8 7.3 %collective-permute-done.11 = bf16[128,1792]{1,0:T(8,128)(2,1)S(1)} collective-permute-done((bf16[128,1792]{1,0:T(8,128)(2,1)S(1)}, bf16[128,1792]{1,0:T(8,128)(2,1)S(1)}, u32[]{:S(2)}, u32[]{:S(2)}) %collective-permute-start.11) | collective-permute-done | bytes 458784 | tf_op jit(solution)/shard_map/ppermute | solution.py:647
  79.3 16.5 %collective-permute-done.14.refs_2_ = bf16[160,896]{1,0:T(8,128)(2,1)} collective-permute-done((bf16[160,896]{1,0:T(8,128)(2,1)}, bf16[160,896]{1,0:T(8,128)(2,1)}, u32[]{:S(2)}, u32[]{:S(2)}) %collective-permute-start.14) | collective-permute-done | bytes 286752 | tf_op jit(solution)/shard_map/ppermute | solution.py:652
  99.9 6.0 %assemble_rows.3 = (bf16[896,1792]{1,0:T(8,128)(2,1)}, f32[2,32,1792]{2,1,0:T(8,128)}) custom-call(s32[2]{0:T(128)} %pad_add_fusion.6.meta, bf16[512,1792]{1,0:T(8,128)(2,1)} %constant_dynamic-update-slice_fusion.7.own_ref, bf16[512,1792]{1,0:T(8,128)(2,1)} %collective-permute-done.16.other_ref), custom_call_target="tpu_custom_call" | custom-call | flops 1000000000 | bytes 1000000 | tf_op jit(solution)/shard_map/assemble_rows/pallas_call | solution.py:523
  109.9 7.3 %collective-permute-done.18.refs_2_ = bf16[512,256]{1,0:T(8,128)(2,1)S(1)} collective-permute-done((bf16[512,256]{1,0:T(8,128)(2,1)S(1)}, bf16[512,256]{1,0:T(8,128)(2,1)S(1)}, u32[]{:S(2)}, u32[]{:S(2)}) %collective-permute-start.18) | collective-permute-done | bytes 262176 | tf_op jit(solution)/shard_map/ppermute | solution.py:652
  117.2 5.8 %collective-permute-start.20 = (bf16[256,1280]{1,0:T(8,128)(2,1)S(1)}, bf16[256,1280]{1,0:T(8,128)(2,1)S(1)}, u32[]{:S(2)}, u32[]{:S(2)}) collective-permute-start(bf16[256,1280]{1,0:T(8,128)(2,1)S(1)} %bitcast.93), channel_id=1, source_target_pairs={{1,0},{2,1},{3,2},{0,3},{5,4},{6,5},{7,6},{4,7},{9,8},{10,9},{11,1... | collective-permute-start | bytes 1966088 | tf_op jit(solution)/shard_map/ppermute | solution.py:652
  124.2 16.5 %attention_forward.1 = (f32[512,896]{1,0:T(8,128)S(1)}, f32[7,8,1024]{2,1,0:T(8,128)S(1)}, bf16[512,896]{1,0:T(8,128)(2,1)S(1)}) custom-call(s32[2]{0:T(128)S(1)} %pad_add_fusion.meta, f32[512,896]{1,0:T(8,128)} %convolution_add_fusion.1.pre_ref, f32[512,128]{1,0:T(8,128)S(1)} %get-tuple-element.257.cos_ref, f32[512,128]{1,0:T(8,128)S(1)} %get-tuple-element.222.sin_ref, ...), custom_call_target="tpu_custom_call" | custom-call | flops 40000000000 | bytes 1000000 | tf_op jit(solution)/shard_map/attention_forward/pallas_call | solution.py:227
  140.8 39.0 %collective-permute-done.21.refs_2_ = bf16[256,1280]{1,0:T(8,128)(2,1)S(1)} collective-permute-done((bf16[256,1280]{1,0:T(8,128)(2,1)S(1)}, bf16[256,1280]{1,0:T(8,128)(2,1)S(1)}, u32[]{:S(2)}, u32[]{:S(2)}) %collective-permute-start.21) | collective-permute-done | bytes 655392 | tf_op jit(solution)/shard_map/ppermute | solution.py:652
  193.9 16.6 %feed_forward.4 = (bf16[512,896]{1,0:T(8,128)(2,1)}, bf16[512,896]{1,0:T(8,128)(2,1)}, bf16[4096,512]{1,0:T(8,128)(2,1)}, bf16[4096,384]{1,0:T(8,128)(2,1)}, bf1...) custom-call(s32[2]{0:T(128)} %pad_add_fusion.2.place, ...), custom_call_target="tpu_custom_call" | custom-call | flops 4000000000 | bytes 1000000 | tf_op jit(solution)/shard_map/feed_forward/pallas_call | solution.py:409
  212.8 10.3 %collective-permute-done.27 = bf16[256,896]{1,0:T(8,128)(2,1)S(1)} collective-permute-done((bf16[256,896]{1,0:T(8,128)(2,1)S(1)}, bf16[256,896]{1,0:T(8,128)(2,1)S(1)}, u32[]{:S(2)}, u32[]{:S(2)}) %collective-permute-start.27) | collective-permute-done | bytes 458784 | tf_op jit(solution)/shard_map/ppermute | solution.py:647
  226.4 16.2 %feed_forward.5 = (bf16[512,896]{1,0:T(8,128)(2,1)}, bf16[512,896]{1,0:T(8,128)(2,1)}, bf16[4096,512]{1,0:T(8,128)(2,1)}, bf16[4096,384]{1,0:T(8,128)(2,1)}, bf1...) custom-call(s32[2]{0:T(128)} %pad_add_fusion.4.place, ...), custom_call_target="tpu_custom_call", output_to_operand_aliasing={{2}: (6, {}), {3}: (7, {}), {4}: (8, {}), {5}: (9, {}), {6}... | custom-call | flops 4000000000 | bytes 1000000 | tf_op jit(solution)/shard_map/feed_forward/pallas_call | solution.py:409
  242.6 16.2 %feed_forward.6 = (bf16[512,896]{1,0:T(8,128)(2,1)}, bf16[512,896]{1,0:T(8,128)(2,1)}, bf16[4096,512]{1,0:T(8,128)(2,1)}, bf16[4096,384]{1,0:T(8,128)(2,1)}, bf1...) custom-call(s32[2]{0:T(128)} %pad_add_fusion.3.place, ...), custom_call_target="tpu_custom_call", output_to_operand_aliasing={{2}: (6, {}), {3}: (7, {}), {4}: (8, {}), {5}: (9, {}), {6}... | custom-call | flops 4000000000 | bytes 1000000 | tf_op jit(solution)/shard_map/feed_forward/pallas_call | solution.py:409
  259.9 16.5 %feed_forward.7 = (bf16[512,896]{1,0:T(8,128)(2,1)}, bf16[512,896]{1,0:T(8,128)(2,1)}, bf16[4096,512]{1,0:T(8,128)(2,1)}, bf16[4096,384]{1,0:T(8,128)(2,1)}, bf1...) custom-call(s32[2]{0:T(128)} %pad_add_fusion.1.place, ...), custom_call_target="tpu_custom_call", output_to_operand_aliasing={{2}: (6, {}), {3}: (7, {}), {4}: (8, {}), {5}: (9, {}), {6}... | custom-call | flops 4000000000 | bytes 1000000 | tf_op jit(solution)/shard_map/feed_forward/pallas_call | solution.py:409
  280.2 10.3 %collective-permute-done.33 = bf16[256,896]{1,0:T(8,128)(2,1)S(1)} collective-permute-done((bf16[256,896]{1,0:T(8,128)(2,1)S(1)}, bf16[256,896]{1,0:T(8,128)(2,1)S(1)}, u32[]{:S(2)}, u32[]{:S(2)}) %collective-permute-start.33) | collective-permute-done | bytes 458784 | tf_op jit(solution)/shard_map/ppermute | solution.py:647
  297.5 16.9 %weight_gradient.5 = bf16[4,256,1280]{2,1,0:T(8,128)(2,1)} custom-call(s32[3]{0:T(128)} %pad_add_fusion.5.where, bf16[4096,896]{1,0:T(8,128)(2,1)} %get-tuple-element.158.x_ref, bf16[4096,1280]{1,0:T(8,128)(2,1)} %get-tuple-element.159.y_ref), custom_call_target="tpu_custom_call" | custom-call | flops 1000000000 | bytes 1000000 | tf_op jit(solution)/shard_map/weight_gradient/pallas_call | solution.py:480
  314.3 10.9 %weight_gradient.6 = bf16[4,160,896]{2,1,0:T(8,128)(2,1)} custom-call(s32[3]{0:T(128)} %pad_add_fusion.5.where, bf16[4096,640]{1,0:T(8,128)(2,1)} %get-tuple-element.160.x_ref, bf16[4096,896]{1,0:T(8,128)(2,1)} %all-gather.2.cloned.1.call-done.cot_ref.y_ref), custom_call_target="tpu_custom_call" | custom-call | flops 1000000000 | bytes 1000000 | tf_op jit(solution)/shard_map/weight_gradient/pallas_call | solution.py:480
  341.9 15.6 %attention_backward.1 = (bf16[512,896]{1,0:T(8,128)(2,1)S(1)}, f32[512,256]{1,0:T(8,128)S(1)}, bf16[512,256]{1,0:T(8,128)(2,1)}, bf16[512,256]{1,0:T(8,128)(2,1)S(1)}, bf16[512,256]{1,0:T(8,128)(2,1)S(1)}) custom-call(s32[2]{0:T(128)S(1)} %pad_add_fusion.meta, bf16[512,896]{1,0:T(8,128)(2,1)S(1)} %copy-done.4, ...), custom_call_target="tpu_custom_call" | custom-call | flops 40000000000 | bytes 1000000 | tf_op jit(solution)/shard_map/attention_backward/pallas_call | solution.py:330
  358.4 5.8 %collective-permute-done.39 = bf16[160,896]{1,0:T(8,128)(2,1)S(1)} collective-permute-done((bf16[160,896]{1,0:T(8,128)(2,1)S(1)}, bf16[160,896]{1,0:T(8,128)(2,1)S(1)}, u32[]{:S(2)}, u32[]{:S(2)}) %collective-permute-start.39) | collective-permute-done | bytes 286752 | tf_op jit(solution)/shard_map/ppermute | solution.py:652
  364.2 32.2 %collective-permute-done.40 = bf16[160,896]{1,0:T(8,128)(2,1)S(1)} collective-permute-done((bf16[160,896]{1,0:T(8,128)(2,1)S(1)}, bf16[160,896]{1,0:T(8,128)(2,1)S(1)}, u32[]{:S(2)}, u32[]{:S(2)}) %collective-permute-start.40) | collective-permute-done | bytes 286752 | tf_op jit(solution)/shard_map/ppermute | solution.py:652
  402.2 5.1 weight_gradient.7
  413.4 24.2 %collective-permute-done.45 = bf16[512,256]{1,0:T(8,128)(2,1)S(1)} collective-permute-done((bf16[512,256]{1,0:T(8,128)(2,1)S(1)}, bf16[512,256]{1,0:T(8,128)(2,1)S(1)}, u32[]{:S(2)}, u32[]{:S(2)}) %collective-permute-start.45) | collective-permute-done | bytes 262176 | tf_op jit(solution)/shard_map/ppermute | solution.py:652
  474.8 8.8 %collective-permute-done.49 = bf16[4,32,1792]{2,1,0:T(8,128)(2,1)S(1)} collective-permute-done((bf16[4,32,1792]{2,1,0:T(8,128)(2,1)}, bf16[4,32,1792]{2,1,0:T(8,128)(2,1)S(1)}, u32[]{:S(2)}, u32[]{:S(2)}) %collective-permute-start.49) | collective-permute-done | bytes 458784 | tf_op jit(solution)/shard_map/ppermute | solution.py:647
  492.1 5.2 %update_columns.1 = (f32[28,9728]{1,0:T(8,128)}, f32[28,9728]{1,0:T(8,128)}, f32[28,9728]{1,0:T(8,128)}) custom-call(bf16[8,32,1280]{2,1,0:T(8,128)(2,1)} %copy-done.23, f32[28,9728]{1,0:T(8,128)} %m_ref.1, f32[28,9728]{1,0:T(8,128)} %v_ref.1, f32[28,9728]{1,0:T(8,128)} %w_ref.3), custom_call_target="tpu_custom_call" | custom-call | flops 1000000000 | bytes 1000000 | tf_op jit(solution)/shard_map/update_columns/pallas_call | solution.py:631
  (388 shorter events, 173.1 us)
Async XLA Ops:
  7.2 186.7 %all-gather.2.cloned.1.call-start = ((), (), s32[]{:S(2)}) async-start(), calls=%async_computation.4 | async-start | bytes 8257536 | tf_op jit(solution)/shard_map/all_gather | solution.py:765
  62.7 37.2 %collective-permute-start.16 = (bf16[512,1792]{1,0:T(8,128)(2,1)}, bf16[512,1792]{1,0:T(8,128)(2,1)}, u32[]{:S(2)}, u32[]{:S(2)}) collective-permute-start(bf16[512,1792]{1,0:T(8,128)(2,1)} %constant_dynamic-update-slice_fusion.7.own_ref), channel_id=1, source_target_pairs={{0,4},{4,0},{8,12},{12,8},{16,20},{20,16},{24,28},{28,24},{1,5},{5... | collective-permute-start | bytes 5505032 | tf_op jit(solution)/shard_map/ppermute | solution.py:647
  68.0 27.8 %collective-permute-start.14 = (bf16[160,896]{1,0:T(8,128)(2,1)}, bf16[160,896]{1,0:T(8,128)(2,1)}, u32[]{:S(2)}, u32[]{:S(2)}) collective-permute-start(bf16[160,896]{1,0:T(8,128)(2,1)} %pad.29.refs_0_), channel_id=1, source_target_pairs={{2,0},{3,1},{0,2},{1,3},{6,4},{7,5},{4,6},{5,7},{10,8},{11,9},{8,1... | collective-permute-start | bytes 860168 | tf_op jit(solution)/shard_map/ppermute | solution.py:652
  69.6 26.2 %collective-permute-start.15 = (bf16[160,896]{1,0:T(8,128)(2,1)}, bf16[160,896]{1,0:T(8,128)(2,1)}, u32[]{:S(2)}, u32[]{:S(2)}) collective-permute-start(bf16[160,896]{1,0:T(8,128)(2,1)} %pad.29.refs_0_), channel_id=1, source_target_pairs={{3,0},{0,1},{1,2},{2,3},{7,4},{4,5},{5,6},{6,7},{11,8},{8,9},{9,10... | collective-permute-start | bytes 860168 | tf_op jit(solution)/shard_map/ppermute | solution.py:652
  75.1 322.9 %reduce-scatter.3.cloned.1.call-start = ((), (), s32[]{:S(2)}) async-start(), calls=%async_computation.5 | async-start | bytes 4718592 | tf_op jit(solution)/shard_map/reduce_scatter | solution.py:867
  122.9 56.9 %collective-permute-start.21 = (bf16[256,1280]{1,0:T(8,128)(2,1)S(1)}, bf16[256,1280]{1,0:T(8,128)(2,1)S(1)}, u32[]{:S(2)}, u32[]{:S(2)}) collective-permute-start(bf16[256,1280]{1,0:T(8,128)(2,1)S(1)} %bitcast.94), channel_id=1, source_target_pairs={{2,0},{3,1},{0,2},{1,3},{6,4},{7,5},{4,6},{5,7},{10,8},{11,9},{8,1... | collective-permute-start | bytes 1966088 | tf_op jit(solution)/shard_map/ppermute | solution.py:652
  123.9 55.9 %collective-permute-start.22 = (bf16[256,1280]{1,0:T(8,128)(2,1)S(1)}, bf16[256,1280]{1,0:T(8,128)(2,1)S(1)}, u32[]{:S(2)}, u32[]{:S(2)}) collective-permute-start(bf16[256,1280]{1,0:T(8,128)(2,1)S(1)} %bitcast.95), channel_id=1, source_target_pairs={{3,0},{0,1},{1,2},{2,3},{7,4},{4,5},{5,6},{6,7},{11,8},{8,9},{9,10... | collective-permute-start | bytes 1966088 | tf_op jit(solution)/shard_map/ppermute | solution.py:652
  184.8 25.8 %collective-permute-start.23 = (bf16[512,896]{1,0:T(8,128)(2,1)}, bf16[512,896]{1,0:T(8,128)(2,1)S(1)}, u32[]{:S(2)}, u32[]{:S(2)}) collective-permute-start(bf16[512,896]{1,0:T(8,128)(2,1)} %multiply_convert_fusion.n_a), channel_id=1, source_target_pairs={{0,8},{4,12},{8,0},{12,4},{16,24},{20,28},{24,16},{28,20},{1,9},{5... | collective-permute-start | bytes 2752520 | tf_op jit(solution)/shard_map/ppermute | solution.py:647
  185.2 25.4 %collective-permute-start.24 = (bf16[512,896]{1,0:T(8,128)(2,1)}, bf16[512,896]{1,0:T(8,128)(2,1)S(1)}, u32[]{:S(2)}, u32[]{:S(2)}) collective-permute-start(bf16[512,896]{1,0:T(8,128)(2,1)} %multiply_convert_fusion.n_a), channel_id=1, source_target_pairs={{0,16},{4,20},{8,24},{12,28},{16,0},{20,4},{24,8},{28,12},{1,17},{... | collective-permute-start | bytes 2752520 | tf_op jit(solution)/shard_map/ppermute | solution.py:647
  225.8 34.1 %collective-permute-start.26 = (bf16[512,896]{1,0:T(8,128)(2,1)S(1)}, bf16[512,896]{1,0:T(8,128)(2,1)}, u32[]{:S(2)}, u32[]{:S(2)}) collective-permute-start(bf16[512,896]{1,0:T(8,128)(2,1)S(1)} %collective-permute-done.24.n_a), channel_id=1, source_target_pairs={{0,4},{4,0},{8,12},{12,8},{16,20},{20,16},{24,28},{28,24},{1,5},{5... | collective-permute-start | bytes 2752520 | tf_op jit(solution)/shard_map/ppermute | solution.py:647
  259.4 32.3 %collective-permute-start.35 = (bf16[512,896]{1,0:T(8,128)(2,1)}, bf16[512,896]{1,0:T(8,128)(2,1)}, u32[]{:S(2)}, u32[]{:S(2)}) collective-permute-start(bf16[512,896]{1,0:T(8,128)(2,1)} %get-tuple-element.156), channel_id=1, source_target_pairs={{0,4},{4,0},{8,12},{12,8},{16,20},{20,16},{24,28},{28,24},{1,5},{5... | collective-permute-start | bytes 2752520 | tf_op jit(solution)/shard_map/ppermute | solution.py:647
  280.2 45.0 %collective-permute-start.34 = (bf16[512,896]{1,0:T(8,128)(2,1)}, bf16[512,896]{1,0:T(8,128)(2,1)S(1)}, u32[]{:S(2)}, u32[]{:S(2)}) collective-permute-start(bf16[512,896]{1,0:T(8,128)(2,1)} %get-tuple-element.154), channel_id=1, source_target_pairs={{0,4},{4,0},{8,12},{12,8},{16,20},{20,16},{24,28},{28,24},{1,5},{5... | collective-permute-start | bytes 2752520 | tf_op jit(solution)/shard_map/ppermute | solution.py:647
  294.6 30.6 %collective-permute-start.37 = (bf16[512,896]{1,0:T(8,128)(2,1)}, bf16[512,896]{1,0:T(8,128)(2,1)S(1)}, u32[]{:S(2)}, u32[]{:S(2)}) collective-permute-start(bf16[512,896]{1,0:T(8,128)(2,1)} %add_convert_fusion.1), channel_id=1, source_target_pairs={{0,8},{4,12},{8,0},{12,4},{16,24},{20,28},{24,16},{28,20},{1,9},{5... | collective-permute-start | bytes 2752520 | tf_op jit(solution)/shard_map/ppermute | solution.py:647
  295.8 29.4 %collective-permute-start.38 = (bf16[512,896]{1,0:T(8,128)(2,1)}, bf16[512,896]{1,0:T(8,128)(2,1)}, u32[]{:S(2)}, u32[]{:S(2)}) collective-permute-start(bf16[512,896]{1,0:T(8,128)(2,1)} %add_convert_fusion.2), channel_id=1, source_target_pairs={{0,16},{4,20},{8,24},{12,28},{16,0},{20,4},{24,8},{28,12},{1,17},{... | collective-permute-start | bytes 2752520 | tf_op jit(solution)/shard_map/ppermute | solution.py:647
  325.2 177.6 %reduce-scatter.5.cloned.1.call-start = ((), (), s32[]{:S(2)}) async-start(), calls=%async_computation.6 | async-start | bytes 3538944 | tf_op jit(solution)/shard_map/reduce_scatter | solution.py:897
  328.7 67.7 %collective-permute-start.42 = (bf16[256,1280]{1,0:T(8,128)(2,1)S(1)}, bf16[256,1280]{1,0:T(8,128)(2,1)S(1)}, u32[]{:S(2)}, u32[]{:S(2)}) collective-permute-start(bf16[256,1280]{1,0:T(8,128)(2,1)S(1)} %get-tuple-element.227), channel_id=1, source_target_pairs={{1,0},{2,1},{3,2},{0,3},{5,4},{6,5},{7,6},{4,7},{9,8},{10,9},{11,1... | collective-permute-start | bytes 1966088 | tf_op jit(solution)/shard_map/ppermute | solution.py:652
  328.7 69.3 %collective-permute-start.43 = (bf16[256,1280]{1,0:T(8,128)(2,1)S(1)}, bf16[256,1280]{1,0:T(8,128)(2,1)}, u32[]{:S(2)}, u32[]{:S(2)}) collective-permute-start(bf16[256,1280]{1,0:T(8,128)(2,1)S(1)} %get-tuple-element.226), channel_id=1, source_target_pairs={{2,0},{3,1},{0,2},{1,3},{6,4},{7,5},{4,6},{5,7},{10,8},{11,9},{8,1... | collective-permute-start | bytes 1966088 | tf_op jit(solution)/shard_map/ppermute | solution.py:652
  330.4 33.7 %collective-permute-start.39 = (bf16[160,896]{1,0:T(8,128)(2,1)S(1)}, bf16[160,896]{1,0:T(8,128)(2,1)S(1)}, u32[]{:S(2)}, u32[]{:S(2)}) collective-permute-start(bf16[160,896]{1,0:T(8,128)(2,1)S(1)} %get-tuple-element.234), channel_id=1, source_target_pairs={{1,0},{2,1},{3,2},{0,3},{5,4},{6,5},{7,6},{4,7},{9,8},{10,9},{11,1... | collective-permute-start | bytes 860168 | tf_op jit(solution)/shard_map/ppermute | solution.py:652
  333.9 62.4 %collective-permute-start.40 = (bf16[160,896]{1,0:T(8,128)(2,1)S(1)}, bf16[160,896]{1,0:T(8,128)(2,1)S(1)}, u32[]{:S(2)}, u32[]{:S(2)}) collective-permute-start(bf16[160,896]{1,0:T(8,128)(2,1)S(1)} %get-tuple-element.233), channel_id=1, source_target_pairs={{2,0},{3,1},{0,2},{1,3},{6,4},{7,5},{4,6},{5,7},{10,8},{11,9},{8,1... | collective-permute-start | bytes 860168 | tf_op jit(solution)/shard_map/ppermute | solution.py:652
  333.9 62.4 %collective-permute-start.41 = (bf16[160,896]{1,0:T(8,128)(2,1)S(1)}, bf16[160,896]{1,0:T(8,128)(2,1)S(1)}, u32[]{:S(2)}, u32[]{:S(2)}) collective-permute-start(bf16[160,896]{1,0:T(8,128)(2,1)S(1)} %get-tuple-element.232), channel_id=1, source_target_pairs={{3,0},{0,1},{1,2},{2,3},{7,4},{4,5},{5,6},{6,7},{11,8},{8,9},{9,10... | collective-permute-start | bytes 860168 | tf_op jit(solution)/shard_map/ppermute | solution.py:652
  398.0 39.5 %collective-permute-start.45 = (bf16[512,256]{1,0:T(8,128)(2,1)S(1)}, bf16[512,256]{1,0:T(8,128)(2,1)S(1)}, u32[]{:S(2)}, u32[]{:S(2)}) collective-permute-start(bf16[512,256]{1,0:T(8,128)(2,1)S(1)} %get-tuple-element.178), channel_id=1, source_target_pairs={{2,0},{3,1},{0,2},{1,3},{6,4},{7,5},{4,6},{5,7},{10,8},{11,9},{8,1... | collective-permute-start | bytes 786440 | tf_op jit(solution)/shard_map/ppermute | solution.py:652
  400.0 37.5 %collective-permute-start.46 = (bf16[512,256]{1,0:T(8,128)(2,1)S(1)}, bf16[512,256]{1,0:T(8,128)(2,1)S(1)}, u32[]{:S(2)}, u32[]{:S(2)}) collective-permute-start(bf16[512,256]{1,0:T(8,128)(2,1)S(1)} %get-tuple-element.179), channel_id=1, source_target_pairs={{3,0},{0,1},{1,2},{2,3},{7,4},{4,5},{5,6},{6,7},{11,8},{8,9},{9,10... | collective-permute-start | bytes 786440 | tf_op jit(solution)/shard_map/ppermute | solution.py:652
  402.1 37.1 %collective-permute-start.58 = (bf16[256,1280]{1,0:T(8,128)(2,1)}, bf16[256,1280]{1,0:T(8,128)(2,1)}, u32[]{:S(2)}, u32[]{:S(2)}) collective-permute-start(bf16[256,1280]{1,0:T(8,128)(2,1)} %get-tuple-element.225), channel_id=1, source_target_pairs={{3,0},{0,1},{1,2},{2,3},{7,4},{4,5},{5,6},{6,7},{11,8},{8,9},{9,10... | collective-permute-start | bytes 1966088 | tf_op jit(solution)/shard_map/ppermute | solution.py:652
  412.1 44.0 %collective-permute-start.47 = (bf16[4,4,32,1792]{3,2,1,0:T(8,128)(2,1)}, bf16[4,4,32,1792]{3,2,1,0:T(8,128)(2,1)}, u32[]{:S(2)}, u32[]{:S(2)}) collective-permute-start(bf16[4,4,32,1792]{3,2,1,0:T(8,128)(2,1)} %get-tuple-element.183), channel_id=1, source_target_pairs={{0,4},{4,0},{8,12},{12,8},{16,20},{20,16},{24,28},{28,24},{1,5},{5... | collective-permute-start | bytes 5505032 | tf_op jit(solution)/shard_map/ppermute | solution.py:647
  (117 other events, 1336.5 us)
Sparse Core Ops, SparseCore 0:
  60.9 56.1 all-gather.1
  325.4 48.7 reduce-scatter.2
  412.2 49.1 reduce-scatter.4

commit v2 on v1

--- a/solution.py
+++ b/solution.py
@@ -344,8 +344,8 @@
 def feed_kernel(
     steps, fresh, place, n_a, n_b, cot_ref, gateup_ref, down_ref, *refs
 ):
-    refs = refs[0 if fresh else 5 :]
-    back_a, back_b, left_ref, right_ref, hidden_ref, grad_ref, kept_ref = refs
+    refs = refs[0 if fresh else 4 :]
+    back_a, back_b, out_ref, hidden_ref, grad_ref, kept_ref = refs
     width = down_ref.shape[0]
     first = pl.program_id(0) < steps // 2
     normed = jnp.where(first, n_a[...], n_b[...])
@@ -362,9 +362,7 @@
     hidden_ref[...] = hidden
     grad_ref[:, :width] = grad_gate
     grad_ref[:, width:] = grad_up
-    out = jnp.dot(hidden, down_ref[...], preferred_element_type=wide).astype(low)
-    left_ref[...] = out[:, : left_ref.shape[1]]
-    right_ref[...] = out[:, left_ref.shape[1] :]
+    out_ref[...] = jnp.dot(hidden, down_ref[...], preferred_element_type=wide).astype(low)
     back = lax.dot_general(grad_gate, gateup_ref[:, :width], NT, preferred_element_type=wide)
     back = back + lax.dot_general(grad_up, gateup_ref[:, width:], NT, preferred_element_type=wide)
 
@@ -381,7 +379,6 @@
     rows, d = n_a.shape
     total, width = cot_all.shape[0], down.shape[0]
     block = min(block, rows)
-    left = padded(d // 2, LANES)
     each = rows // block
     steps = 2 * each
     spot = lambda i, place: (place[i // each] * each + i % each, 0)
@@ -397,22 +394,22 @@
     ]
     fresh = kept is None
     if not fresh:
-        in_specs += [pl.BlockSpec(memory_space=pl.ANY)] * 5
+        in_specs += [pl.BlockSpec(memory_space=pl.ANY)] * 4
     spec = pltpu.PrefetchScalarGridSpec(
         num_scalar_prefetch=1,
         grid=(steps,),
         in_specs=in_specs,
         out_specs=halves
-        + [pl.BlockSpec((block, n), spot) for n in (left, d - left, width, 2 * width, d)],
-    )
-    shapes = [(rows, d)] * 2 + [(total, n) for n in (left, d - left, width, 2 * width, d)]
+        + [pl.BlockSpec((block, n), spot) for n in (d, width, 2 * width, d)],
+    )
+    shapes = [(rows, d)] * 2 + [(total, n) for n in (d, width, 2 * width, d)]
     return pl.pallas_call(
         functools.partial(feed_kernel, steps, fresh),
         grid_spec=spec,
         out_shape=[jax.ShapeDtypeStruct(s, low) for s in shapes],
-        input_output_aliases={} if fresh else {6 + i: 2 + i for i in range(5)},
+        input_output_aliases={} if fresh else {6 + i: 2 + i for i in range(4)},
         compiler_params=params(),
-        cost_estimate=cost(4),
+        cost_estimate=cost(15),
         name="feed_forward",
     )(place, n_a, n_b, cot_all, gateup, down, *(() if fresh else kept))
 
@@ -461,7 +458,8 @@
 
 
 def weight_gradient(
-    x, y, shape, take, where, split=False, block=1024, column=0, columns=1, into=None, extra=None
+    x, y, shape, take, where, split=False, block=1024, column=0, columns=1, into=None, extra=None,
+    micros=0.2,
 ):
     total, size = x.shape
     width = y.shape[1]
@@ -494,9 +492,95 @@
         out_shape=[jax.ShapeDtypeStruct(shape, low) for shape in shapes],
         input_output_aliases={3 + fill + i: i for i in range(len(into))},
         compiler_params=params(),
-        cost_estimate=cost(1 if steps > 1 else 0.2),
+        cost_estimate=cost(micros),
         name="weight_gradient",
     )(where, x, y, *([extra] if fill else []), *into)
+
+
+def finish_kernel(
+    shape, take, give, cuts, pieces, where, normed_ref, scaled_ref, inv_ref, gain_ref, query_ref,
+    query_weight_ref, middle_ref, weight_ref, cos_ref, sin_ref, small_ref, *refs
+):
+    got_refs = refs[:pieces]
+    keep_ref, send_ref, out_ref, acc_ref, row_ref, cut_ref = refs[pieces:]
+    chips, cores, groups = shape
+    size = normed_ref.shape[1]
+    total = got_refs[0][...]
+    for ref in got_refs[1:]:
+        total = total + ref[...].astype(wide)
+    keys, values = total[:, :LANES], total[:, LANES:]
+    lane = lax.broadcasted_iota(jnp.int32, keys.shape, 1)
+    swapped = jnp.where(
+        lane % HD < HD // 2, pltpu.roll(keys, LANES - HD // 2, 1), pltpu.roll(keys, HD // 2, 1)
+    )
+    keys = keys * cos_ref[...] - swapped * sin_ref[...]
+    grads = jnp.concatenate([keys, values], axis=1).astype(low)
+    acc_ref[:size] = lax.dot_general(
+        normed_ref[...], grads, TN, preferred_element_type=wide
+    )
+    grad = lax.dot_general(
+        query_ref[...], query_weight_ref[...], NT, preferred_element_type=wide
+    ) + lax.dot_general(grads, weight_ref[...], NT, preferred_element_type=wide)
+    scaled = scaled_ref[...]
+    row_ref[:, :size] = jnp.sum(grad * scaled, axis=0, keepdims=True)
+    row_ref[:, size : size + small_ref.shape[1]] = small_ref[...]
+    row_ref[:, size + small_ref.shape[1] :] = jnp.sum(grads.astype(wide), axis=0, keepdims=True)
+    grad = grad * gain_ref[...]
+    mean = jnp.sum(grad * scaled, axis=1, keepdims=True) * (1.0 / size)
+    out_ref[...] = (middle_ref[...] + inv_ref[...] * (grad - scaled * mean)).astype(low)
+    cut_ref[...] = jnp.zeros_like(cut_ref)
+    for i in range(chips * cores * groups):
+        at = 0
+        for first, width in cuts:
+            begin = first + i * width
+            cut_ref[i : i + 1, at : at + width] = row_ref[:, begin : begin + width]
+            at += width
+    high = cut_ref[...].astype(low).astype(wide)
+    rest = cut_ref[...] - high
+    row = lax.broadcasted_iota(jnp.int32, (give, 1), 0)
+
+    def write(mine):
+        for chip in range(chips):
+            for core in range(cores):
+                for group in range(groups):
+                    i = (chip * cores + core) * groups + group
+                    value = jnp.where(row < take, acc_ref[i * take : i * take + give], 0.0)
+                    value = jnp.where(row == take, high[i : i + 1], value)
+                    value = jnp.where(row == take + 1, rest[i : i + 1], value)
+                    at = lax.rem(group + groups - where[2], groups)
+                    target = send_ref if core ^ mine else keep_ref
+                    target[chip ^ where[1], at] = value.astype(low)
+
+    for mine in range(cores):
+        pl.when(where[0] == mine)(functools.partial(write, mine))
+
+
+def finish_keyval(shape, take, give, cuts, where, got, operands):
+    chips, cores, groups = shape
+    rows, size = operands[0].shape
+    width = got[0].shape[1]
+    total = size + operands[10].shape[1] + width
+    whole = lambda a: pl.BlockSpec(a.shape, lambda i, w: (0,) * a.ndim)
+    pieces = pl.BlockSpec((chips, groups, give, width), lambda i, w: (0, 0, 0, 0))
+    return pl.pallas_call(
+        functools.partial(finish_kernel, shape, take, give, cuts, len(got)),
+        grid_spec=pltpu.PrefetchScalarGridSpec(
+            num_scalar_prefetch=1,
+            grid=(1,),
+            in_specs=[whole(a) for a in (*operands, *got)],
+            out_specs=[pieces, pieces, pl.BlockSpec((rows, size), lambda i, w: (0, 0))],
+            scratch_shapes=[
+                pltpu.VMEM((padded(size, 8) + give, width), wide),
+                pltpu.VMEM((1, total), wide),
+                pltpu.VMEM((padded(chips * cores * groups, 8), width), wide),
+            ],
+        ),
+        out_shape=[jax.ShapeDtypeStruct((chips, groups, give, width), low)] * 2
+        + [jax.ShapeDtypeStruct((rows, size), low)],
+        compiler_params=params(),
+        cost_estimate=cost(20),
+        name="finish_keyval",
+    )(where, *operands, *got)
 
 
 def assemble_kernel(
@@ -517,15 +601,14 @@
     o_ref[...] = acc_ref[:size].astype(low)
 
 
-def assemble(own, other, n_dp, n_group, take, give, me, mine):
-    width = own.shape[1]
+def assemble(own, other, n_dp, n_group, take, give, me, mine, column, width):
     size = n_dp * n_group * take
     return pl.pallas_call(
         functools.partial(assemble_kernel, n_dp, n_group, take, give),
         grid_spec=pltpu.PrefetchScalarGridSpec(
             num_scalar_prefetch=1,
             grid=(1,),
-            in_specs=[pl.BlockSpec(own.shape, lambda i, m: (0, 0))] * 2,
+            in_specs=[pl.BlockSpec((own.shape[0], width), lambda i, m: (0, column))] * 2,
             out_specs=[
                 pl.BlockSpec((size, width), lambda i, m: (0, 0)),
                 pl.BlockSpec((2, n_dp * n_group, width), lambda i, m: (0, 0, 0)),
@@ -543,6 +626,29 @@
         cost_estimate=cost(1),
         name="assemble_rows",
     )(jnp.stack([me, mine]).astype(jnp.int32), own, other)
+
+
+def sum_kernel(*refs):
+    total = refs[0][...].astype(wide)
+    for ref in refs[1:-1]:
+        total = total + ref[...].astype(wide)
+    refs[-1][...] = total.astype(low)
+
+
+def sum_pieces(pieces):
+    rows, width = pieces[0].shape
+    block = rows // 2
+    spec = pl.BlockSpec((block, width), lambda i: (i, 0))
+    return pl.pallas_call(
+        sum_kernel,
+        grid=(2,),
+        in_specs=[spec] * len(pieces),
+        out_specs=spec,
+        out_shape=jax.ShapeDtypeStruct((rows, width), low),
+        compiler_params=params(),
+        cost_estimate=cost(0.1),
+        name="sum_pieces",
+    )(*pieces)
 
 
 def stack_kernel(outer, count, take, give, meta, *refs):
@@ -652,6 +758,12 @@
     return lax.ppermute(value, "group", [((i + step) % count, i) for i in range(count)])
 
 
+def shift_within(value, step):
+    count = lax.axis_size("group")
+    pairs = [(i + step, i) for i in range(count) if 0 <= i + step < count]
+    return lax.ppermute(value, "group", pairs)
+
+
 def after(value, *others):
     return lax.optimization_barrier((value, *others))[0]
 
@@ -669,25 +781,25 @@
     return functools.reduce(jnp.add, [term.astype(wide) for term in terms])
 
 
-def gather_column(block):
-    return jnp.concatenate(group_pieces(block), axis=0)
-
-
 def gather_chips(column):
     evens = [column] + [flip(column, r) for r in range(2, lax.axis_size("dp"), 2)]
     return jnp.concatenate(evens, axis=0)
 
 
-def gather_rows(own, other, take):
+def gather_rows(own, other, take, column=0, columns=1):
     n_dp, n_group = lax.axis_size("dp"), lax.axis_size("group")
     give = own.shape[0] // (n_dp // 2 * n_group)
     return assemble(
-        own, other, n_dp, n_group, take, give, lax.axis_index("dp"), lax.axis_index("group")
-    )
-
-
-def scatter_chips(keep, send):
-    pair = keep.astype(wide) + flip(send, 1).astype(wide)
+        own, other, n_dp, n_group, take, give, lax.axis_index("dp"), lax.axis_index("group"),
+        column, own.shape[1] // columns,
+    )
+
+
+def scatter_pair(keep, send):
+    return keep.astype(wide) + flip(send, 1).astype(wide)
+
+
+def scatter_chips(pair):
     got = [flip(pair[r].astype(low), 2 * r) for r in range(1, pair.shape[0])]
     return add_up([pair[0]] + got)
 
@@ -749,26 +861,26 @@
     small_rows = jnp.pad(small_rows, ((0, 0), (0, 2 * kv_width - 2 * small_piece)))
     keyval_block = jnp.concatenate([keyval_weight.astype(low), small_rows], axis=0)
     keyval_block = jnp.pad(keyval_block, ((0, in_give - in_rows - 2), (0, 0)))
-    keyval_column = gather_column(keyval_block)
+    both_block = jnp.concatenate([query_weight.astype(low), output_weight.astype(low)], axis=1)
+    both_block = jnp.pad(both_block, ((0, in_give - in_rows), (0, 0)))
+    gateup_pieces = cut_columns(gateup_weight, n_dp, part_wide, in_give)
+    every_pieces = group_pieces(jnp.concatenate([keyval_block, both_block], axis=1))
+    every_column = jnp.concatenate(after(every_pieces, gateup_pieces), axis=0)
+    keyval_column = every_column[:, : 2 * kv_width]
+    both_column = every_column[:, 2 * kv_width :]
     keyval_own = gather_chips(keyval_column)
-    keyval_full, small_all = gather_rows(keyval_own, flip(keyval_own, 1), in_rows)
+    keyval_full, small_all = gather_rows(
+        keyval_own, flip(keyval_own, 1), in_rows
+    )
     small_all = small_all[:, :, : 2 * small_piece].reshape(2, device_count, 2, small_piece)
     small_values = small_all[0, :, 0].reshape(small_size)
     small_second_all = (small_all[0, :, 1] + small_all[1, :, 0] + small_all[1, :, 1]).reshape(
         small_size
     )
-    both_block = jnp.concatenate([query_weight.astype(low), output_weight.astype(low)], axis=1)
-    both_block = jnp.pad(both_block, ((0, in_give - in_rows), (0, 0)))
-    both_column = gather_column(after(both_block, keyval_column))
-    both_own = gather_chips(after(both_column, keyval_full))
-    both_other = flip(both_own, 1)
-    cot_all = lax.all_gather(after(cotangent, both_own), "dp", axis=0, tiled=True)
-    gateup_pieces = cut_columns(gateup_weight, n_dp, part_wide, in_give)
-    gateup_column = lax.all_to_all(after(gateup_pieces, keyval_column), "dp", 0, 0, tiled=True)
-    down_block = jnp.pad(down_weight.astype(low), ((0, padded(down_rows, ROWS) - down_rows), (0, 0)))
-    down_pieces = group_pieces(after(down_block, keyval_column))
+
+    down_part = lax.all_gather(down_weight.astype(low), "group", axis=0, tiled=True)
+    down_part = jnp.pad(down_part, ((0, part_wide - part), (0, 0)))
     me_group = my_index.astype(jnp.int32)[None]
-    down_part = stack_rows(down_pieces, 1, down_rows, me_group, part_wide)
 
     gain_one = small_values[:D]
     gain_two = small_values[D : 2 * D]
@@ -799,29 +911,36 @@
     key_pre = keyval_pre[:, :kv_width]
     key_low = (key_pre * cos_wide + swap(key_pre) * sin_wide).astype(low)
     keyval_low = jnp.concatenate([key_low, keyval_pre[:, kv_width:].astype(low)], axis=1)
-    keyval_low = after(keyval_low, gateup_column, down_pieces)
-    both_full, _ = gather_rows(after(both_own, keyval_low), both_other, in_rows)
-    query_full, output_full = both_full[:, :query_width], both_full[:, query_width:]
-    keyval_parts = group_pieces(keyval_low)
-    keyval_parts = [keyval_parts[-s % group_size] for s in range(group_size)]
+    keyval_parts = [keyval_low] + [shift_within(keyval_low, -s) for s in range(1, group_size)]
+    both_own = gather_chips(after(both_column, keyval_low))
+    gateup_column = lax.all_to_all(after(gateup_pieces, keyval_low), "dp", 0, 0, tiled=True)
+    gateup_column = gateup_column.reshape(n_dp * in_give, 2 * part_wide)
+    both_own, keyval_parts, gateup_column, down_part = after(
+        (both_own, keyval_parts, gateup_column, down_part)
+    )
+    cot_all = lax.all_gather(after(cotangent, both_own), "dp", axis=0, tiled=True)
+    both_other = flip(both_own, 1)
+    query_full, _ = gather_rows(both_own, both_other, in_rows, 0, 2)
+    output_full, _ = gather_rows(both_own, both_other, in_rows, 1, 2)
     query_pre = (
         jnp.dot(normed_one, query_full, preferred_element_type=wide) + bias_qkv[:query_width]
     )
-    keyval_parts = after(keyval_parts, query_pre)
-    gateup_column = after(gateup_column, *keyval_parts).reshape(n_dp * in_give, 2 * part_wide)
     gateup_pieces = group_pieces(gateup_column)
     attn_float, log_total, query_low = attention_forward(
         query_pre, cos_wide, sin_wide, starts, keyval_parts, meta
     )
     attn_float = after(attn_float, gateup_pieces)
-    gateup_part = stack_rows(gateup_pieces, n_dp, in_rows, me_group, D)
     attn_low = attn_float.astype(low)
     middle = act_in + jnp.dot(attn_low, output_full, preferred_element_type=wide)
     inv_two = lax.rsqrt(jnp.mean(middle * middle, axis=1, keepdims=True) + norm_eps)
     scaled_two = middle * inv_two
     normed_two = (scaled_two * gain_two).astype(low)
 
+    gateup_pieces = after(gateup_pieces, normed_two)
+    gateup_part = stack_rows(gateup_pieces, n_dp, in_rows, me_group, D)
     chips = n_dp // 2
+    pieces, down_shape = (chips, 2, group_size), (1, 1, group_size)
+    device = jnp.stack([my_dp & 1, my_dp >> 1, my_index]).astype(jnp.int32)
     kept, sides, back = None, {0: normed_two}, {}
     for k in range(1, chips):
         if n_dp != 8 or k != 3:
@@ -840,11 +959,13 @@
         sides[1], sides[2] = after((sides[1], sides[2]), kept)
         across = [flip(sides[1][:half], 4), flip(sides[2][half:], 2)]
         kept = visit(1, kept)
-        sides[3] = jnp.concatenate(across, axis=0)
+        sides[3] = jnp.concatenate(after(across, kept), axis=0)
         kept = visit(3, kept)
         corner = add_up(back[3]).astype(low)
         across = [flip(corner[:half], 2), flip(corner[half:], 4)]
         kept = visit(2, kept)
+        (down_term,) = weight_gradient(kept[1], cot_all, down_shape, down_rows, device)
+        across = after(across, down_term)
         nothing = jnp.zeros_like(across[0])
         x_sum = add_up([*back[1], jnp.concatenate([nothing, across[1]], axis=0)]).astype(low)
         y_sum = add_up([*back[2], jnp.concatenate([across[0], nothing], axis=0)]).astype(low)
@@ -853,18 +974,16 @@
     else:
         for k in range(chips):
             kept = visit(k, kept)
+        (down_term,) = weight_gradient(kept[1], cot_all, down_shape, down_rows, device)
         returned = list(back[0])
         returned += [flip(add_up(back[k]).astype(low), 2 * k) for k in range(1, chips)]
-    out_left, out_right, hidden_all, gate_all, normed_all = kept
-    pieces = (n_dp // 2, 2, group_size)
-    device = jnp.stack([my_dp & 1, my_dp >> 1, my_index]).astype(jnp.int32)
+    out_all, _, gate_all, normed_all = kept
+    down_got = group_send(down_term)
     (gateup_term,) = weight_gradient(normed_all, gate_all, pieces, in_rows, device)
     gateup_got = group_send(gateup_term)
-    (down_term,) = weight_gradient(hidden_all, cot_all, (1, 1, group_size), down_rows, device)
-    down_got = group_send(down_term)
-    returned = after(returned, gateup_term, down_term)
+    returned, gateup_got[0], down_got = after((returned, gateup_got[0], down_got))
     grad_normed_two = add_up(returned)
-    out_left = lax.psum_scatter(after(out_left, returned), "dp", scatter_dimension=0, tiled=True)
+    out_sum = lax.psum_scatter(after(out_all, returned), "dp", scatter_dimension=0, tiled=True)
 
     grad_out = cotangent.astype(wide)
     gain_scaled_two = grad_normed_two * gain_two
@@ -879,6 +998,7 @@
     both_terms = weight_gradient(
         attn_low, grad_middle_low, pieces, in_rows, device, split=True, column=1, columns=2
     )
+    grad_attn_low = after(grad_attn_low, both_terms)
     grad_query_pre, *keyval_terms = attention_backward(
         query_low,
         grad_attn_low,
@@ -891,65 +1011,60 @@
         meta,
     )
     grad_query_pre, keyval_terms = after(
-        (grad_query_pre, keyval_terms), down_got, gateup_got[:-1], out_left
-    )
-    keyval_got = [keyval_terms[0]] + [shift(keyval_terms[s], s) for s in range(1, group_size)]
-    out_right = lax.psum_scatter(
-        after(out_right, grad_query_pre), "dp", scatter_dimension=0, tiled=True
-    )
+        (grad_query_pre, keyval_terms), gateup_got
+    )
+    keyval_got = [keyval_terms[0]]
+    keyval_got += [shift_within(keyval_terms[s], s) for s in range(1, group_size)]
     both_terms = weight_gradient(
         normed_one, grad_query_pre, pieces, in_rows, device, split=True, columns=2, into=both_terms
     )
-    both_total = scatter_chips(*both_terms)
-    grad_normed_one = lax.dot_general(grad_query_pre, query_full, NT, preferred_element_type=wide)
-    keyval_grads = add_up(keyval_got)
-    down_grad = add_up(after(down_got, keyval_grads))[:down_rows]
-    gateup_sum = add_up(after(gateup_got, keyval_grads)).reshape(n_dp, -1, 2 * part_wide)
-    gateup_sum = lax.all_to_all(gateup_sum.astype(low), "dp", 0, 0, tiled=True)
+    both_pair = scatter_pair(both_terms[0], after(both_terms[1], keyval_got, out_sum))
+    both_total = scatter_chips(both_pair)
+    keyval_got = after(keyval_got, both_pair)
+    bias_term = jnp.sum(grad_query_pre.astype(wide), axis=0)
+    *last_terms, tokens_grad = finish_keyval(
+        pieces,
+        in_rows,
+        in_give,
+        ((0, small_piece), (0, rest_piece), (rest_length, value_piece)),
+        device,
+        keyval_got,
+        (
+            normed_one,
+            scaled_one,
+            inv_one,
+            gain_one[None],
+            grad_query_pre,
+            query_full,
+            grad_middle,
+            keyval_full,
+            cos_wide,
+            sin_wide,
+            jnp.concatenate([gain_two_term, bias_term])[None],
+        ),
+    )
+    small_width = small_piece + rest_piece + value_piece
+    gateup_sum = sum_pieces(after(gateup_got, last_terms)).reshape(n_dp, -1, 2 * part_wide)
+    gateup_sum = lax.all_to_all(gateup_sum, "dp", 0, 0, tiled=True)
+    last_terms, gateup_sum = after((last_terms, gateup_sum), both_total)
+    last_total = scatter_chips(scatter_pair(*last_terms))
+    down_got = after(down_got, last_total)
+    late_middle, out_sum = after((middle, out_sum), last_total)
+    layer_out = (late_middle + out_sum.astype(wide)).astype(low)
+    down_grad = add_up(down_got)[:down_rows]
     gateup_grad, gateup_second_out, gateup_weight_out = update_columns(
         gateup_sum, gateup_first, gateup_second, gateup_weight
     )
-    key_grads, value_grads = keyval_grads[:, :kv_width], keyval_grads[:, kv_width:]
-    key_grads = key_grads * cos_wide - swap(key_grads) * sin_wide
-    grad_keyval_pre = jnp.concatenate([key_grads, value_grads], axis=1).astype(low)
-    bias_term = jnp.concatenate(
-        [
-            jnp.sum(grad_query_pre.astype(wide), axis=0),
-            jnp.sum(grad_keyval_pre.astype(wide), axis=0),
-        ]
-    )
-    grad_normed_one = grad_normed_one + lax.dot_general(
-        grad_keyval_pre, keyval_full, NT, preferred_element_type=wide
-    )
-    gain_scaled_one = grad_normed_one * gain_one
-    gain_one_term = jnp.sum(grad_normed_one * scaled_one, axis=0)
-    grad_input = grad_middle + inv_one * (
-        gain_scaled_one - scaled_one * jnp.mean(gain_scaled_one * scaled_one, axis=1, keepdims=True)
-    )
-    tokens_grad = grad_input.astype(low)
-    out_sum = jnp.concatenate([out_left, out_right], axis=1).astype(wide)
-    layer_out = (middle + out_sum).astype(low)
-    small_term = jnp.concatenate([gain_one_term, gain_two_term, bias_term])
-
-    small_blocks = jnp.concatenate(
-        [
-            small_term.reshape(device_count, small_piece),
-            small_term[:rest_length].reshape(device_count, rest_piece),
-            small_term[rest_length:].reshape(device_count, value_piece),
-        ],
-        axis=1,
-    )
-    small_width = small_blocks.shape[1]
-    small_two = jnp.stack(split_low(small_blocks)[:2], axis=1)
-    small_two = jnp.pad(small_two, ((0, 0), (0, 0), (0, 2 * kv_width - small_width)))
-    small_two = jnp.pad(small_two, ((0, 0), (in_rows, in_give - in_rows - 2), (0, 0)))
-    last_terms = weight_gradient(
-        normed_one, grad_keyval_pre, pieces, in_rows, device, split=True, extra=small_two
-    )
-    last_total = scatter_chips(*last_terms)
     some = last_total.shape[1] - both_total.shape[1]
     both_total = jnp.pad(both_total, ((0, 0), (0, some), (0, 0)))
-    every_sum = add_up(group_send(jnp.concatenate([both_total, last_total], axis=2)))
+    down_second_out, down_weight_out = adamw_step(
+        down_grad, down_first, down_second, down_weight, rate_proj, decay_rate
+    )
+    every_got = group_send(jnp.concatenate([both_total, last_total], axis=2))
+    every_got, gateup_second_out, down_second_out, layer_out = after(
+        (every_got, gateup_second_out, down_second_out, layer_out)
+    )
+    every_sum = add_up(every_got)
     query_grad = every_sum[:in_rows, :query_width]
     output_grad = every_sum[:in_rows, query_width : query_width + D]
     last_sum = every_sum[:, query_width + D :]
@@ -967,9 +1082,6 @@
     )
     output_second_out, output_weight_out = adamw_step(
         output_grad, output_first, output_second, output_weight, rate_out, decay_rate
-    )
-    down_second_out, down_weight_out = adamw_step(
-        down_grad, down_first, down_second, down_weight, rate_proj, decay_rate
     )
     _, small_weight_out = adamw_step(
         small_grad, small_first, small_second, small_weight, rate_small, 0.0

time: 520 us -> 453 us (0.87)
  waiting for transfers between devices: 188 us -> 116 us
  Pallas kernels: 162 us -> 168 us
    ppermute x27 -> x15, waiting for transfers between devices: 134 us -> 67.4 us  [shift(): lax.ppermute(value, 'group', [((i + step) % count, i) for i in range(coun...]
    ppermute x32, waiting for transfers between devices: 54.5 us -> 22.7 us  [flip(): return lax.ppermute(value, 'dp', [(i, i ^ mask) for i in range(count)])]
    ppermute x0 -> x6, waiting for transfers between devices: none -> 18.6 us  [shift_within(): return lax.ppermute(value, 'group', pairs)]
    ppermute x0 -> x6, starting transfers between devices: none -> 14 us  [shift_within(): return lax.ppermute(value, 'group', pairs)]
    ppermute x27 -> x15, starting transfers between devices: 35.8 us -> 22.6 us  [shift(): lax.ppermute(value, 'group', [((i + step) % count, i) for i in range(coun...]
    pallas_call x0 -> x2, Pallas kernels: none -> 10.4 us  [the longest x1 7.82 us: finish_keyval(): pl.pallas_call(functools.partial(finish_kernel, shape, take, give, cuts,...]
    all_to_all x2, waiting for transfers between devices: 0.01 us -> 6.86 us  [the longest x1 5.49 us: body(): gateup_sum = lax.all_to_all(gateup_sum, 'dp', 0, 0, tiled=True)]
    convert_element_type x4 -> x1, other arithmetic: 6.42 us -> 1.11 us  [body(): layer_out = (late_middle + out_sum.astype(wide)).astype(low)]
  transfers between devices with their start and end apart: 64 -> 58, of which waited for: 20 -> 21; matrix products, arithmetic and copies ran while one was open for 13% -> 13% of each run, Pallas kernels for 31% -> 38%
where the time goes in v2:
time: 453 us; the launch traced here: 445 us
  Pallas kernels  168 us (37%)
  waiting for transfers between devices  116 us (26%)
  starting transfers between devices  68.3 us (15%)
  other arithmetic  44.6 us (10%)
  local copies, waits for them, and re-layouts  23.7 us (5%)
  between operations  15.1 us (3%)
  matrix products  9.99 us (2%)
    ppermute x15, waiting for transfers between devices, shift(): lax.ppermute(value, 'group', [((i + step) % count, i) for i in range(coun...  67.4 us
    pallas_call x4, Pallas kernels, feed_forward(): pl.pallas_call(functools.partial(feed_kernel, steps, fresh), grid_spec=sp...  65.3 us
    pallas_call x4, Pallas kernels, weight_gradient(): pl.pallas_call(functools.partial(weight_kernel, steps, shape, take, give,...  38.3 us
    ppermute x32, starting transfers between devices, flip(): return lax.ppermute(value, 'dp', [(i, i ^ mask) for i in range(count)])  24.5 us
    ppermute x32, waiting for transfers between devices, flip(): return lax.ppermute(value, 'dp', [(i, i ^ mask) for i in range(count)])  22.7 us
    ppermute x15, starting transfers between devices, shift(): lax.ppermute(value, 'group', [((i + step) % count, i) for i in range(coun...  22.6 us
    ppermute x6, waiting for transfers between devices, shift_within(): return lax.ppermute(value, 'group', pairs)  18.6 us
    pallas_call x1, Pallas kernels, attention_forward(): pl.pallas_call(functools.partial(forward_kernel, pieces), grid_spec=spec,...  16.4 us
  transfers between devices with their start and end apart: 58, of which 21 were waited for; matrix products, arithmetic and copies ran while one was open for 13% of the time, Pallas kernels for 38%

profile of v2, /device:TPU:0, one launch (start us, length us, event | category | flops | bytes accessed | tf_op | source)
XLA Modules:
  0.0 445.4 jit_solution(17146392643101854369)
XLA Ops:
  11.4 5.1 %collective-permute-start = (bf16[32,2048]{1,0:T(8,128)(2,1)S(1)}, bf16[32,2048]{1,0:T(8,128)(2,1)S(1)}, u32[]{:S(2)}, u32[]{:S(2)}) collective-permute-start(bf16[32,2048]{1,0:T(8,128)(2,1)S(1)} %fusion.13), channel_id=1, source_target_pairs={{1,0},{2,1},{3,2},{0,3},{5,4},{6,5},{7,6},{4,7},{9,8},{10,9},{11,1... | collective-permute-start | bytes 393224 | tf_op jit(solution)/shard_map/ppermute | solution.py:758
  22.9 4.8 %collective-permute-done.1 = bf16[32,2048]{1,0:T(8,128)(2,1)S(1)} collective-permute-done((bf16[32,2048]{1,0:T(8,128)(2,1)S(1)}, bf16[32,2048]{1,0:T(8,128)(2,1)S(1)}, u32[]{:S(2)}, u32[]{:S(2)}) %collective-permute-start.1) | collective-permute-done | bytes 131104 | tf_op jit(solution)/shard_map/ppermute | solution.py:758
  64.0 5.9 %collective-permute-done.8 = bf16[128,1792]{1,0:T(8,128)(2,1)} collective-permute-done((bf16[128,1792]{1,0:T(8,128)(2,1)}, bf16[128,1792]{1,0:T(8,128)(2,1)}, u32[]{:S(2)}, u32[]{:S(2)}) %collective-permute-start.8) | collective-permute-done | bytes 458784 | tf_op jit(solution)/shard_map/ppermute | solution.py:753
  77.1 7.0 %collective-permute-start.14 = (bf16[256,1280]{1,0:T(8,128)(2,1)S(1)}, bf16[256,1280]{1,0:T(8,128)(2,1)S(1)}, u32[]{:S(2)}, u32[]{:S(2)}) collective-permute-start(bf16[256,1280]{1,0:T(8,128)(2,1)S(1)} %bitcast.87), channel_id=1, source_target_pairs={{1,0},{2,1},{3,2},{0,3},{5,4},{6,5},{7,6},{4,7},{9,8},{10,9},{11,1... | collective-permute-start | bytes 1966088 | tf_op jit(solution)/shard_map/ppermute | solution.py:758
  93.0 16.4 %attention_forward.1 = (f32[512,896]{1,0:T(8,128)S(1)}, f32[7,8,1024]{2,1,0:T(8,128)S(1)}, bf16[512,896]{1,0:T(8,128)(2,1)S(1)}) custom-call(s32[2]{0:T(128)S(1)} %pad_add_fusion.1.meta, f32[512,896]{1,0:T(8,128)} %convolution_add_fusion.pre_ref, f32[512,128]{1,0:T(8,128)S(1)} %get-tuple-element.306.cos_ref, f32[512,128]{1,0:T(8,128)S(1)} %get-tuple-element.273.sin_ref, ...), custom_call_target="tpu_custom_call" | custom-call | flops 40000000000 | bytes 1000000 | tf_op jit(solution)/shard_map/attention_forward/pallas_call | solution.py:227
  111.0 28.9 %collective-permute-done.15.refs_2_ = bf16[256,1280]{1,0:T(8,128)(2,1)S(1)} collective-permute-done((bf16[256,1280]{1,0:T(8,128)(2,1)S(1)}, bf16[256,1280]{1,0:T(8,128)(2,1)S(1)}, u32[]{:S(2)}, u32[]{:S(2)}) %collective-permute-start.15) | collective-permute-done | bytes 655392 | tf_op jit(solution)/shard_map/ppermute | solution.py:758
  157.1 16.6 %feed_forward.4 = (bf16[512,896]{1,0:T(8,128)(2,1)}, bf16[512,896]{1,0:T(8,128)(2,1)}, bf16[4096,896]{1,0:T(8,128)(2,1)}, bf16[4096,640]{1,0:T(8,128)(2,1)}, bf1...) custom-call(s32[2]{0:T(128)} %pad_add_fusion.2.place, bf16[512,896]{1,0:T(8,128)(2,1)} %multiply_convert_fusion.n_a, ...), custom_call_target="tpu_custom_call" | custom-call | flops 15000000512 | bytes 1000000 | tf_op jit(solution)/shard_map/feed_forward/pallas_call | solution.py:406
  179.2 16.2 %feed_forward.5 = (bf16[512,896]{1,0:T(8,128)(2,1)}, bf16[512,896]{1,0:T(8,128)(2,1)}, bf16[4096,896]{1,0:T(8,128)(2,1)}, bf16[4096,640]{1,0:T(8,128)(2,1)}, bf1...) custom-call(s32[2]{0:T(128)} %pad_add_fusion.3.place, ...), custom_call_target="tpu_custom_call", output_to_operand_aliasing={{2}: (6, {}), {3}: (7, {}), {4}: (8, {}), {5}: (9, {})} | custom-call | flops 15000000512 | bytes 1000000 | tf_op jit(solution)/shard_map/feed_forward/pallas_call | solution.py:406
  199.8 16.2 %feed_forward.6 = (bf16[512,896]{1,0:T(8,128)(2,1)}, bf16[512,896]{1,0:T(8,128)(2,1)}, bf16[4096,896]{1,0:T(8,128)(2,1)}, bf16[4096,640]{1,0:T(8,128)(2,1)}, bf1...) custom-call(s32[2]{0:T(128)} %pad_add_fusion.4.place, ...), custom_call_target="tpu_custom_call", output_to_operand_aliasing={{2}: (6, {}), {3}: (7, {}), {4}: (8, {}), {5}: (9, {})} | custom-call | flops 15000000512 | bytes 1000000 | tf_op jit(solution)/shard_map/feed_forward/pallas_call | solution.py:406
  217.1 16.3 %feed_forward.7 = (bf16[512,896]{1,0:T(8,128)(2,1)}, bf16[512,896]{1,0:T(8,128)(2,1)}, bf16[4096,896]{1,0:T(8,128)(2,1)}, bf16[4096,640]{1,0:T(8,128)(2,1)}, bf1...) custom-call(s32[2]{0:T(128)} %pad_add_fusion.5.place, ...), custom_call_target="tpu_custom_call", output_to_operand_aliasing={{2}: (6, {}), {3}: (7, {}), {4}: (8, {}), {5}: (9, {})} | custom-call | flops 15000000512 | bytes 1000000 | tf_op jit(solution)/shard_map/feed_forward/pallas_call | solution.py:406
  237.7 11.2 %weight_gradient.4 = bf16[4,160,896]{2,1,0:T(8,128)(2,1)} custom-call(s32[3]{0:T(128)} %pad_add_fusion.where, bf16[4096,640]{1,0:T(8,128)(2,1)} %get-tuple-element.184.x_ref, bf16[4096,896]{1,0:T(8,128)(2,1)} %all-gather.5.cloned.1.call-done.cot_ref.y_ref), custom_call_target="tpu_custom_call" | custom-call | flops 200000000 | bytes 1000000 | tf_op jit(solution)/shard_map/weight_gradient/pallas_call | solution.py:478
  259.9 16.8 %weight_gradient.5 = bf16[4,256,1280]{2,1,0:T(8,128)(2,1)} custom-call(s32[3]{0:T(128)} %pad_add_fusion.where, bf16[4096,896]{1,0:T(8,128)(2,1)} %get-tuple-element.193.x_ref, bf16[4096,1280]{1,0:T(8,128)(2,1)} %get-tuple-element.194.y_ref), custom_call_target="tpu_custom_call" | custom-call | flops 200000000 | bytes 1000000 | tf_op jit(solution)/shard_map/weight_gradient/pallas_call | solution.py:478
  281.9 5.0 %collective-permute-done.35 = bf16[160,896]{1,0:T(8,128)(2,1)S(1)} collective-permute-done((bf16[160,896]{1,0:T(8,128)(2,1)S(1)}, bf16[160,896]{1,0:T(8,128)(2,1)S(1)}, u32[]{:S(2)}, u32[]{:S(2)}) %collective-permute-start.35) | collective-permute-done | bytes 286752 | tf_op jit(solution)/shard_map/ppermute | solution.py:758
  293.5 4.7 %fusion.34 = (bf16[512,896]{1,0:T(8,128)(2,1)}, f32[512,896]{1,0:T(8,128)}) fusion(f32[512]{0:T(512)S(1)} %broadcast_multiply_fusion, f32[512,896]{1,0:T(8,128)S(1)} %get-tuple-element.241, f32[896]{0:T(1024)S(1)} %get-tuple-element.307, bf16[512,896]{1,0:T(8,128)(2,1)} %collective-permute-done.32, bf16[512,896]{1,0:T(8,128)(2,1)} %collective-permute-done.30, ...), kind=kLoop, calls=%fused_computation.135 | loop fusion | flops 6881280 | bytes 9182720 | tf_op jit(solution)/shard_map/convert_element_type | solution.py:994
  298.2 5.2 %weight_gradient.6 = (bf16[4,4,32,1792]{3,2,1,0:T(8,128)(2,1)}, bf16[4,4,32,1792]{3,2,1,0:T(8,128)(2,1)}) custom-call(s32[3]{0:T(128)} %pad_add_fusion.where, bf16[512,896]{1,0:T(8,128)(2,1)} %copy-done.17, bf16[512,896]{1,0:T(8,128)(2,1)} %get-tuple-element.270.y_ref), custom_call_target="tpu_custom_call" | custom-call | flops 200000000 | bytes 1000000 | tf_op jit(solution)/shard_map/weight_gradient/pallas_call | solution.py:478
  306.1 14.9 %attention_backward.1 = (bf16[512,896]{1,0:T(8,128)(2,1)S(1)}, f32[512,256]{1,0:T(8,128)S(1)}, bf16[512,256]{1,0:T(8,128)(2,1)S(1)}, bf16[512,256]{1,0:T(8,128)(2,1)S(1)}, bf16[512,256]{1,0:T(8,128)(2,1)S(1)}) custom-call(s32[2]{0:T(128)S(1)} %pad_add_fusion.1.meta, bf16[512,896]{1,0:T(8,128)(2,1)S(1)} %copy-done.7, ...), custom_call_target="tpu_custom_call" | custom-call | flops 40000000000 | bytes 1000000 | tf_op jit(solution)/shard_map/attention_backward/pallas_call | solution.py:330
  321.9 22.9 %collective-permute-done.37.refs_2_ = bf16[256,1280]{1,0:T(8,128)(2,1)} collective-permute-done((bf16[256,1280]{1,0:T(8,128)(2,1)}, bf16[256,1280]{1,0:T(8,128)(2,1)}, u32[]{:S(2)}, u32[]{:S(2)}) %collective-permute-start.37) | collective-permute-done | bytes 655392 | tf_op jit(solution)/shard_map/ppermute | solution.py:758
  348.9 5.1 %weight_gradient.7 = (bf16[4,4,32,1792]{3,2,1,0:T(8,128)(2,1)}, bf16[4,4,32,1792]{3,2,1,0:T(8,128)(2,1)}) custom-call(s32[3]{0:T(128)} %pad_add_fusion.where, bf16[512,896]{1,0:T(8,128)(2,1)} %copy-done.12, bf16[512,896]{1,0:T(8,128)(2,1)} %copy-done, ...), custom_call_target="tpu_custom_call", output_to_operand_aliasing={{0}: (3, {}), {1}: (4, {})} | custom-call | flops 200000000 | bytes 1000000 | tf_op jit(solution)/shard_map/weight_gradient/pallas_call | solution.py:478
  354.1 18.6 %collective-permute-done.40.refs_2_ = bf16[512,256]{1,0:T(8,128)(2,1)S(1)} collective-permute-done((bf16[512,256]{1,0:T(8,128)(2,1)S(1)}, bf16[512,256]{1,0:T(8,128)(2,1)S(1)}, u32[]{:S(2)}, u32[]{:S(2)}) %collective-permute-start.40) | collective-permute-done | bytes 262176 | tf_op jit(solution)/shard_map/ppermute | solution.py:764
  385.7 7.8 %finish_keyval.1 = (bf16[4,4,32,256]{3,2,1,0:T(8,128)(2,1)}, bf16[4,4,32,256]{3,2,1,0:T(8,128)(2,1)}, bf16[512,896]{1,0:T(8,128)(2,1)}) custom-call(s32[3]{0:T(128)} %pad_add_fusion.where, bf16[512,896]{1,0:T(8,128)(2,1)} %copy-done.12, f32[512,896]{1,0:T(8,128)} %get-tuple-element.287.scaled_ref, f32[512,1]{1,0:T(8,128)} %copy.61.inv_ref, ...), custom_call_target="tpu_custom_call" | custom-call | flops 20000000000 | bytes 1000000 | tf_op jit(solution)/shard_map/finish_keyval/pallas_call | solution.py:565
  399.7 6.1 %collective-permute-done.44 = bf16[4,32,1792]{2,1,0:T(8,128)(2,1)S(1)} collective-permute-done((bf16[4,32,1792]{2,1,0:T(8,128)(2,1)S(1)}, bf16[4,32,1792]{2,1,0:T(8,128)(2,1)S(1)}, u32[]{:S(2)}, u32[]{:S(2)}) %collective-permute-start.44) | collective-permute-done | bytes 458784 | tf_op jit(solution)/shard_map/ppermute | solution.py:753
  407.3 5.5 %all-to-all-done.1.g_ref = bf16[8,32,1280]{2,1,0:T(8,128)(2,1)S(1)} async-done(((bf16[8,32,1280]{2,1,0:T(8,128)(2,1)}), bf16[8,32,1280]{2,1,0:T(8,128)(2,1)S(1)}, u32[]{:S(2)}, u32[]{:S(2)}) %all-to-all-start.1) | async-done | bytes 655392 | tf_op jit(solution)/shard_map/all_to_all | solution.py:1048
  418.3 5.1 %update_columns.1 = (f32[28,9728]{1,0:T(8,128)}, f32[28,9728]{1,0:T(8,128)}, f32[28,9728]{1,0:T(8,128)}) custom-call(bf16[8,32,1280]{2,1,0:T(8,128)(2,1)} %copy-done.20, f32[28,9728]{1,0:T(8,128)} %m_ref.1, f32[28,9728]{1,0:T(8,128)} %v_ref.1, f32[28,9728]{1,0:T(8,128)} %w_ref.3), custom_call_target="tpu_custom_call" | custom-call | flops 1000000000 | bytes 1000000 | tf_op jit(solution)/shard_map/update_columns/pallas_call | solution.py:737
  430.4 4.5 %collective-permute-done.51 = bf16[32,2048]{1,0:T(8,128)(2,1)S(1)} collective-permute-done((bf16[32,2048]{1,0:T(8,128)(2,1)S(1)}, bf16[32,2048]{1,0:T(8,128)(2,1)S(1)}, u32[]{:S(2)}, u32[]{:S(2)}) %collective-permute-start.51) | collective-permute-done | bytes 131104 | tf_op jit(solution)/shard_map/ppermute | solution.py:758
  (331 shorter events, 163.3 us)
Async XLA Ops:
  7.2 65.9 %all-gather.3.cloned.1.call-start = ((), (), s32[]{:S(2)}) async-start(), calls=%async_computation.3 | async-start | bytes 1361920 | tf_op jit(solution)/shard_map/all_gather | solution.py:881
  47.4 22.5 %collective-permute-start.8 = (bf16[128,1792]{1,0:T(8,128)(2,1)}, bf16[128,1792]{1,0:T(8,128)(2,1)}, u32[]{:S(2)}, u32[]{:S(2)}) collective-permute-start(bf16[128,1792]{1,0:T(8,128)(2,1)} %slice.237), channel_id=1, source_target_pairs={{0,16},{4,20},{8,24},{12,28},{16,0},{20,4},{24,8},{28,12},{1,17},{... | collective-permute-start | bytes 1376264 | tf_op jit(solution)/shard_map/ppermute | solution.py:753
  47.9 22.5 %collective-permute-start.7 = (bf16[128,1792]{1,0:T(8,128)(2,1)}, bf16[128,1792]{1,0:T(8,128)(2,1)}, u32[]{:S(2)}, u32[]{:S(2)}) collective-permute-start(bf16[128,1792]{1,0:T(8,128)(2,1)} %slice.237), channel_id=1, source_target_pairs={{0,8},{4,12},{8,0},{12,4},{16,24},{20,28},{24,16},{28,20},{1,9},{5... | collective-permute-start | bytes 1376264 | tf_op jit(solution)/shard_map/ppermute | solution.py:753
  49.4 27.5 %all-to-all-start = ((bf16[8,32,1280]{2,1,0:T(8,128)(2,1)}), bf16[8,32,1280]{2,1,0:T(8,128)(2,1)S(1)}, u32[]{:S(2)}, u32[]{:S(2)}) async-start(bf16[8,32,1280]{2,1,0:T(8,128)(2,1)} %cut_columns.1), calls=%async_computation | async-start | bytes 1310720 | tf_op jit(solution)/shard_map/all_to_all | solution.py:916
  52.9 104.1 %all-gather.5.cloned.1.call-start = ((), (), s32[]{:S(2)}) async-start(), calls=%async_computation.4 | async-start | bytes 8257536 | tf_op jit(solution)/shard_map/all_gather | solution.py:921
  53.0 22.5 %collective-permute-start.10 = (bf16[512,256]{1,0:T(8,128)(2,1)S(1)}, bf16[512,256]{1,0:T(8,128)(2,1)S(1)}, u32[]{:S(2)}, u32[]{:S(2)}) collective-permute-start(bf16[512,256]{1,0:T(8,128)(2,1)S(1)} %pad_maximum_fusion.5.refs_0_), channel_id=1, source_target_pairs={{0,1},{1,2},{2,3},{4,5},{5,6},{6,7},{8,9},{9,10},{10,11},{12,13},{... | collective-permute-start | bytes 786440 | tf_op jit(solution)/shard_map/ppermute | solution.py:764
  76.9 295.8 %reduce-scatter.2.cloned.1.call-start = ((), (), s32[]{:S(2)}) async-start(), calls=%async_computation.5 | async-start | bytes 8257536 | tf_op jit(solution)/shard_map/reduce_scatter | solution.py:986
  77.1 33.9 %collective-permute-start.14 = (bf16[256,1280]{1,0:T(8,128)(2,1)S(1)}, bf16[256,1280]{1,0:T(8,128)(2,1)S(1)}, u32[]{:S(2)}, u32[]{:S(2)}) collective-permute-start(bf16[256,1280]{1,0:T(8,128)(2,1)S(1)} %bitcast.87), channel_id=1, source_target_pairs={{1,0},{2,1},{3,2},{0,3},{5,4},{6,5},{7,6},{4,7},{9,8},{10,9},{11,1... | collective-permute-start | bytes 1966088 | tf_op jit(solution)/shard_map/ppermute | solution.py:758
  84.1 55.9 %collective-permute-start.15 = (bf16[256,1280]{1,0:T(8,128)(2,1)S(1)}, bf16[256,1280]{1,0:T(8,128)(2,1)S(1)}, u32[]{:S(2)}, u32[]{:S(2)}) collective-permute-start(bf16[256,1280]{1,0:T(8,128)(2,1)S(1)} %bitcast.88), channel_id=1, source_target_pairs={{2,0},{3,1},{0,2},{1,3},{6,4},{7,5},{4,6},{5,7},{10,8},{11,9},{8,1... | collective-permute-start | bytes 1966088 | tf_op jit(solution)/shard_map/ppermute | solution.py:758
  84.1 55.9 %collective-permute-start.16 = (bf16[256,1280]{1,0:T(8,128)(2,1)S(1)}, bf16[256,1280]{1,0:T(8,128)(2,1)S(1)}, u32[]{:S(2)}, u32[]{:S(2)}) collective-permute-start(bf16[256,1280]{1,0:T(8,128)(2,1)S(1)} %bitcast.89), channel_id=1, source_target_pairs={{3,0},{0,1},{1,2},{2,3},{7,4},{4,5},{5,6},{6,7},{11,8},{8,9},{9,10... | collective-permute-start | bytes 1966088 | tf_op jit(solution)/shard_map/ppermute | solution.py:758
  149.8 23.8 %collective-permute-start.19 = (bf16[512,896]{1,0:T(8,128)(2,1)}, bf16[512,896]{1,0:T(8,128)(2,1)}, u32[]{:S(2)}, u32[]{:S(2)}) collective-permute-start(bf16[512,896]{1,0:T(8,128)(2,1)} %multiply_convert_fusion.n_a), channel_id=1, source_target_pairs={{0,8},{4,12},{8,0},{12,4},{16,24},{20,28},{24,16},{28,20},{1,9},{5... | collective-permute-start | bytes 2752520 | tf_op jit(solution)/shard_map/ppermute | solution.py:753
  151.5 22.8 %collective-permute-start.20 = (bf16[512,896]{1,0:T(8,128)(2,1)}, bf16[512,896]{1,0:T(8,128)(2,1)}, u32[]{:S(2)}, u32[]{:S(2)}) collective-permute-start(bf16[512,896]{1,0:T(8,128)(2,1)} %multiply_convert_fusion.n_a), channel_id=1, source_target_pairs={{0,16},{4,20},{8,24},{12,28},{16,0},{20,4},{24,8},{28,12},{1,17},{... | collective-permute-start | bytes 2752520 | tf_op jit(solution)/shard_map/ppermute | solution.py:753
  198.7 50.4 %collective-permute-start.22 = (bf16[512,896]{1,0:T(8,128)(2,1)}, bf16[512,896]{1,0:T(8,128)(2,1)}, u32[]{:S(2)}, u32[]{:S(2)}) collective-permute-start(bf16[512,896]{1,0:T(8,128)(2,1)} %get-tuple-element.170), channel_id=1, source_target_pairs={{0,4},{4,0},{8,12},{12,8},{16,20},{20,16},{24,28},{28,24},{1,5},{5... | collective-permute-start | bytes 2752520 | tf_op jit(solution)/shard_map/ppermute | solution.py:753
  237.6 39.1 %collective-permute-start.18 = (bf16[512,896]{1,0:T(8,128)(2,1)}, bf16[512,896]{1,0:T(8,128)(2,1)}, u32[]{:S(2)}, u32[]{:S(2)}) collective-permute-start(bf16[512,896]{1,0:T(8,128)(2,1)} %get-tuple-element.163), channel_id=1, source_target_pairs={{0,4},{4,0},{8,12},{12,8},{16,20},{20,16},{24,28},{28,24},{1,5},{5... | collective-permute-start | bytes 2752520 | tf_op jit(solution)/shard_map/ppermute | solution.py:753
  251.6 35.3 %collective-permute-start.30 = (bf16[512,896]{1,0:T(8,128)(2,1)}, bf16[512,896]{1,0:T(8,128)(2,1)}, u32[]{:S(2)}, u32[]{:S(2)}) collective-permute-start(bf16[512,896]{1,0:T(8,128)(2,1)} %add_convert_fusion.2), channel_id=1, source_target_pairs={{0,8},{4,12},{8,0},{12,4},{16,24},{20,28},{24,16},{28,20},{1,9},{5... | collective-permute-start | bytes 2752520 | tf_op jit(solution)/shard_map/ppermute | solution.py:753
  254.5 32.4 %collective-permute-start.32 = (bf16[512,896]{1,0:T(8,128)(2,1)}, bf16[512,896]{1,0:T(8,128)(2,1)}, u32[]{:S(2)}, u32[]{:S(2)}) collective-permute-start(bf16[512,896]{1,0:T(8,128)(2,1)} %add_convert_fusion.1), channel_id=1, source_target_pairs={{0,16},{4,20},{8,24},{12,28},{16,0},{20,4},{24,8},{28,12},{1,17},{... | collective-permute-start | bytes 2752520 | tf_op jit(solution)/shard_map/ppermute | solution.py:753
  257.1 24.8 %collective-permute-start.33 = (bf16[160,896]{1,0:T(8,128)(2,1)S(1)}, bf16[160,896]{1,0:T(8,128)(2,1)S(1)}, u32[]{:S(2)}, u32[]{:S(2)}) collective-permute-start(bf16[160,896]{1,0:T(8,128)(2,1)S(1)} %get-tuple-element.285), channel_id=1, source_target_pairs={{1,0},{2,1},{3,2},{0,3},{5,4},{6,5},{7,6},{4,7},{9,8},{10,9},{11,1... | collective-permute-start | bytes 860168 | tf_op jit(solution)/shard_map/ppermute | solution.py:758
  258.2 23.7 %collective-permute-start.34 = (bf16[160,896]{1,0:T(8,128)(2,1)S(1)}, bf16[160,896]{1,0:T(8,128)(2,1)S(1)}, u32[]{:S(2)}, u32[]{:S(2)}) collective-permute-start(bf16[160,896]{1,0:T(8,128)(2,1)S(1)} %get-tuple-element.284), channel_id=1, source_target_pairs={{2,0},{3,1},{0,2},{1,3},{6,4},{7,5},{4,6},{5,7},{10,8},{11,9},{8,1... | collective-permute-start | bytes 860168 | tf_op jit(solution)/shard_map/ppermute | solution.py:758
  288.0 34.0 %collective-permute-start.36 = (bf16[256,1280]{1,0:T(8,128)(2,1)}, bf16[256,1280]{1,0:T(8,128)(2,1)}, u32[]{:S(2)}, u32[]{:S(2)}) collective-permute-start(bf16[256,1280]{1,0:T(8,128)(2,1)} %get-tuple-element.278), channel_id=1, source_target_pairs={{1,0},{2,1},{3,2},{0,3},{5,4},{6,5},{7,6},{4,7},{9,8},{10,9},{11,1... | collective-permute-start | bytes 1966088 | tf_op jit(solution)/shard_map/ppermute | solution.py:758
  288.2 56.7 %collective-permute-start.37 = (bf16[256,1280]{1,0:T(8,128)(2,1)}, bf16[256,1280]{1,0:T(8,128)(2,1)}, u32[]{:S(2)}, u32[]{:S(2)}) collective-permute-start(bf16[256,1280]{1,0:T(8,128)(2,1)} %get-tuple-element.277), channel_id=1, source_target_pairs={{2,0},{3,1},{0,2},{1,3},{6,4},{7,5},{4,6},{5,7},{10,8},{11,9},{8,1... | collective-permute-start | bytes 1966088 | tf_op jit(solution)/shard_map/ppermute | solution.py:758
  289.4 55.5 %collective-permute-start.38 = (bf16[256,1280]{1,0:T(8,128)(2,1)}, bf16[256,1280]{1,0:T(8,128)(2,1)}, u32[]{:S(2)}, u32[]{:S(2)}) collective-permute-start(bf16[256,1280]{1,0:T(8,128)(2,1)} %get-tuple-element.276), channel_id=1, source_target_pairs={{3,0},{0,1},{1,2},{2,3},{7,4},{4,5},{5,6},{6,7},{11,8},{8,9},{9,10... | collective-permute-start | bytes 1966088 | tf_op jit(solution)/shard_map/ppermute | solution.py:758
  346.3 26.4 %collective-permute-start.40 = (bf16[512,256]{1,0:T(8,128)(2,1)S(1)}, bf16[512,256]{1,0:T(8,128)(2,1)S(1)}, u32[]{:S(2)}, u32[]{:S(2)}) collective-permute-start(bf16[512,256]{1,0:T(8,128)(2,1)S(1)} %get-tuple-element.214), channel_id=1, source_target_pairs={{2,0},{3,1},{6,4},{7,5},{10,8},{11,9},{14,12},{15,13},{18,16},{19,... | collective-permute-start | bytes 786440 | tf_op jit(solution)/shard_map/ppermute | solution.py:764
  347.6 25.1 %collective-permute-start.41 = (bf16[512,256]{1,0:T(8,128)(2,1)S(1)}, bf16[512,256]{1,0:T(8,128)(2,1)S(1)}, u32[]{:S(2)}, u32[]{:S(2)}) collective-permute-start(bf16[512,256]{1,0:T(8,128)(2,1)S(1)} %get-tuple-element.215), channel_id=1, source_target_pairs={{3,0},{7,4},{11,8},{15,12},{19,16},{23,20},{27,24},{31,28}} | collective-permute-start | bytes 786440 | tf_op jit(solution)/shard_map/ppermute | solution.py:764
  383.6 22.2 %collective-permute-start.44 = (bf16[4,32,1792]{2,1,0:T(8,128)(2,1)S(1)}, bf16[4,32,1792]{2,1,0:T(8,128)(2,1)S(1)}, u32[]{:S(2)}, u32[]{:S(2)}) collective-permute-start(bf16[4,32,1792]{2,1,0:T(8,128)(2,1)S(1)} %get-tuple-element.282), channel_id=1, source_target_pairs={{0,16},{4,20},{8,24},{12,28},{16,0},{20,4},{24,8},{28,12},{1,17},{... | collective-permute-start | bytes 1376264 | tf_op jit(solution)/shard_map/ppermute | solution.py:753
  (97 other events, 1149.2 us)
Sparse Core Ops, SparseCore 0:
  19.5 29.0 all-gather.2
  77.0 54.7 all-gather.4
  287.8 64.2 reduce-scatter.1

commit v3 on v2

--- a/solution.py
+++ b/solution.py
@@ -104,7 +104,7 @@
 
 
 def visit_blocks(meta, start_ref, half, pieces, visit):
-    mine = meta[0]
+    mine = meta[2]
     first_query = mine * 2 * half
     turned = start_ref.shape[2] == LANES
     mask_of = query_mask if turned else key_mask
@@ -342,7 +342,7 @@
 
 
 def feed_kernel(
-    steps, fresh, place, n_a, n_b, cot_ref, gateup_ref, down_ref, *refs
+    steps, fresh, device, n_a, n_b, cot_ref, gateup_ref, down_ref, *refs
 ):
     refs = refs[0 if fresh else 4 :]
     back_a, back_b, out_ref, hidden_ref, grad_ref, kept_ref = refs
@@ -375,17 +375,17 @@
         back_b[...] = back.astype(low)
 
 
-def feed_forward(n_a, n_b, cot_all, gateup, down, place, kept, block=256):
+def feed_forward(n_a, n_b, cot_all, gateup, down, device, kept, chip, block=256):
     rows, d = n_a.shape
     total, width = cot_all.shape[0], down.shape[0]
     block = min(block, rows)
     each = rows // block
     steps = 2 * each
-    spot = lambda i, place: (place[i // each] * each + i % each, 0)
-    whole = lambda a: pl.BlockSpec(a.shape, lambda i, place: (0, 0))
+    spot = lambda i, device: ((device[3] ^ (2 * chip + i // each)) * each + i % each, 0)
+    whole = lambda a: pl.BlockSpec(a.shape, lambda i, device: (0, 0))
     halves = [
-        pl.BlockSpec((block, d), lambda i, place: (jnp.minimum(i, each - 1), 0)),
-        pl.BlockSpec((block, d), lambda i, place: (jnp.maximum(i - each, 0), 0)),
+        pl.BlockSpec((block, d), lambda i, device: (jnp.minimum(i, each - 1), 0)),
+        pl.BlockSpec((block, d), lambda i, device: (jnp.maximum(i - each, 0), 0)),
     ]
     in_specs = halves + [
         pl.BlockSpec((block, d), spot),
@@ -411,14 +411,14 @@
         compiler_params=params(),
         cost_estimate=cost(15),
         name="feed_forward",
-    )(place, n_a, n_b, cot_all, gateup, down, *(() if fresh else kept))
-
-
-def weight_kernel(steps, shape, take, give, split, fill, where, x_ref, y_ref, *refs):
-    outputs = 2 if split else 1
+    )(device, n_a, n_b, cot_all, gateup, down, *(() if fresh else kept))
+
+
+def weight_kernel(steps, shape, take, give, split, where, x_ref, y_ref, *refs):
+    chips, cores, groups = shape
+    outputs = 2 if split else groups
     acc_ref = refs[-1]
     out_refs = refs[-1 - outputs : -1]
-    chips, cores, groups = shape
     step = pl.program_id(0)
     size = x_ref.shape[1]
     product = lax.dot_general(x_ref[...], y_ref[...], TN, preferred_element_type=wide)
@@ -439,31 +439,25 @@
             for core in range(cores):
                 for group in range(groups):
                     low_edge = ((chip * cores + core) * groups + group) * take
-                    value = jnp.where(keep, acc_ref[low_edge : low_edge + give], 0.0)
-                    if fill:
-                        value += refs[0][low_edge // take].astype(wide)
-                    value = value.astype(low)
-                    at = lax.rem(group + groups - where[2], groups)
+                    value = jnp.where(keep, acc_ref[low_edge : low_edge + give], 0.0).astype(low)
                     if split:
+                        at = lax.rem(group + groups - where[2], groups)
                         out_refs[core ^ mine][chip ^ where[1], at] = value
                     else:
                         row = (chip * cores + core) * give
-                        out_refs[0][at, row : row + give] = value
-
-    if split:
-        for mine in range(cores):
-            pl.when((step == steps - 1) & (where[0] == mine))(functools.partial(write, mine))
-    else:
-        pl.when(step == steps - 1)(functools.partial(write, 0))
+                        out_refs[(group - mine) % groups][row : row + give] = value
+
+    for mine in range(cores if split else groups):
+        here = where[0 if split else 2] == mine
+        pl.when((step == steps - 1) & here)(functools.partial(write, mine))
 
 
 def weight_gradient(
-    x, y, shape, take, where, split=False, block=1024, column=0, columns=1, into=None, extra=None,
-    micros=0.2,
+    x, y, shape, take, where, split=False, block=1024, column=0, columns=1, into=()
 ):
     total, size = x.shape
     width = y.shape[1]
-    give = padded(take, ROWS) if extra is None else extra.shape[1]
+    give = padded(take, ROWS)
     block = min(block, total)
     steps = total // block
     chips, cores, groups = shape
@@ -471,12 +465,10 @@
         out = pl.BlockSpec((chips, groups, give, width), lambda i, w: (0, 0, 0, column))
         shapes = [(chips, groups, give, columns * width)] * 2
     else:
-        out = pl.BlockSpec((groups, chips * cores * give, width), lambda i, w: (0, 0, 0))
-        shapes = [(groups, chips * cores * give, width)]
-    fill = extra is not None
-    into = [] if into is None else into
+        out = pl.BlockSpec((chips * cores * give, width), lambda i, w: (0, 0))
+        shapes = [(chips * cores * give, width)] * groups
     return pl.pallas_call(
-        functools.partial(weight_kernel, steps, shape, take, give, split, fill),
+        functools.partial(weight_kernel, steps, shape, take, give, split),
         grid_spec=pltpu.PrefetchScalarGridSpec(
             num_scalar_prefetch=1,
             grid=(steps,),
@@ -484,17 +476,79 @@
                 pl.BlockSpec((block, size), lambda i, w: (i, 0)),
                 pl.BlockSpec((block, width), lambda i, w: (i, 0)),
             ]
-            + [pl.BlockSpec(extra.shape, lambda i, w: (0, 0, 0)) for _ in range(fill)]
             + [pl.BlockSpec(memory_space=pl.ANY)] * len(into),
             out_specs=[out] * len(shapes),
             scratch_shapes=[pltpu.VMEM((padded(size, 8) + give, width), wide)],
         ),
         out_shape=[jax.ShapeDtypeStruct(shape, low) for shape in shapes],
-        input_output_aliases={3 + fill + i: i for i in range(len(into))},
+        input_output_aliases={3 + i: i for i in range(len(into))},
         compiler_params=params(),
-        cost_estimate=cost(micros),
+        cost_estimate=cost(0.2),
         name="weight_gradient",
-    )(where, x, y, *([extra] if fill else []), *into)
+    )(where, x, y, *into)
+
+
+def feed_back_kernel(
+    shape, take, give, where, a_ref, b_ref, c_ref, d_ref, middle_ref, inv_ref, gain_ref, cot_ref,
+    attn_ref, weight_ref, grad_ref, do_ref, gain_out, keep_ref, send_ref, acc_ref
+):
+    chips, cores, groups = shape
+    size = attn_ref.shape[1]
+    grad = a_ref[...].astype(wide) + b_ref[...].astype(wide)
+    grad = grad + (c_ref[...].astype(wide) + d_ref[...].astype(wide))
+    inv = inv_ref[...]
+    scaled = middle_ref[...] * inv
+    gain_out[...] = jnp.sum(grad * scaled, axis=0, keepdims=True)
+    grad = grad * gain_ref[...]
+    mean = jnp.sum(grad * scaled, axis=1, keepdims=True) * (1.0 / size)
+    grad = cot_ref[...].astype(wide) + inv * (grad - scaled * mean)
+    grad_ref[...] = grad
+    grad_low = grad.astype(low)
+    do_ref[...] = lax.dot_general(
+        grad_low, weight_ref[...], NT, preferred_element_type=wide
+    ).astype(low)
+    acc_ref[:size] = lax.dot_general(attn_ref[...], grad_low, TN, preferred_element_type=wide)
+    keep = lax.broadcasted_iota(jnp.int32, (give, 1), 0) < take
+
+    def write(mine):
+        for chip in range(chips):
+            for core in range(cores):
+                for group in range(groups):
+                    low_edge = ((chip * cores + core) * groups + group) * take
+                    value = jnp.where(keep, acc_ref[low_edge : low_edge + give], 0.0)
+                    at = lax.rem(group + groups - where[2], groups)
+                    target = send_ref if core ^ mine else keep_ref
+                    target[chip ^ where[1], at] = value.astype(low)
+
+    for mine in range(cores):
+        pl.when(where[0] == mine)(functools.partial(write, mine))
+
+
+def feed_back(shape, take, where, operands):
+    chips, cores, groups = shape
+    rows, size = operands[8].shape
+    give = padded(take, ROWS)
+    whole = lambda shape: pl.BlockSpec(shape, lambda i, w: (0,) * len(shape))
+    pieces = pl.BlockSpec((chips, groups, give, size), lambda i, w: (0, 0, 0, 1))
+    return pl.pallas_call(
+        functools.partial(feed_back_kernel, shape, take, give),
+        grid_spec=pltpu.PrefetchScalarGridSpec(
+            num_scalar_prefetch=1,
+            grid=(1,),
+            in_specs=[whole(a.shape) for a in operands],
+            out_specs=[whole((rows, size)), whole((rows, size)), whole((1, size)), pieces, pieces],
+            scratch_shapes=[pltpu.VMEM((padded(size, 8) + give, size), wide)],
+        ),
+        out_shape=[
+            jax.ShapeDtypeStruct((rows, size), wide),
+            jax.ShapeDtypeStruct((rows, size), low),
+            jax.ShapeDtypeStruct((1, size), wide),
+        ]
+        + [jax.ShapeDtypeStruct((chips, groups, give, 2 * size), low)] * 2,
+        compiler_params=params(),
+        cost_estimate=cost(1),
+        name="feed_back",
+    )(where, *operands)
 
 
 def finish_kernel(
@@ -583,10 +637,8 @@
     )(where, *operands, *got)
 
 
-def assemble_kernel(
-    n_dp, n_group, take, give, meta, own_ref, other_ref, o_ref, small_ref, at_ref, acc_ref
-):
-    me, mine = meta[0], meta[1]
+def place_rows(n_dp, n_group, take, give, device, own_ref, other_ref, at_ref, acc_ref):
+    me, mine = device[3], device[2]
     for r in range(n_dp):
         source = own_ref if r % 2 == 0 else other_ref
         for s in range(n_group):
@@ -595,37 +647,70 @@
             at_ref[(me ^ r) * n_group + z] = source[row : row + give].astype(wide)
     for i in range(n_dp * n_group):
         acc_ref[i * take : i * take + give] = at_ref[i]
+
+
+def assemble_kernel(sizes, device, own_ref, other_ref, o_ref, small_ref, at_ref, acc_ref):
+    place_rows(*sizes, device, own_ref, other_ref, at_ref, acc_ref)
+    count, take = sizes[0] * sizes[1], sizes[2]
+    for i in range(count):
         for j in range(2):
             small_ref[j, i : i + 1] = at_ref[i, take + j : take + j + 1]
-    size = o_ref.shape[0]
-    o_ref[...] = acc_ref[:size].astype(low)
-
-
-def assemble(own, other, n_dp, n_group, take, give, me, mine, column, width):
+    o_ref[...] = acc_ref[: o_ref.shape[0]].astype(low)
+
+
+def project_kernel(
+    sizes, device, own_ref, other_ref, normed_ref, bias_ref, o_ref, pre_ref, at_ref, acc_ref
+):
+    place_rows(*sizes, device, own_ref, other_ref, at_ref, acc_ref)
+    o_ref[...] = acc_ref[: o_ref.shape[0]].astype(low)
+    pre_ref[...] = (
+        jnp.dot(normed_ref[...], o_ref[...], preferred_element_type=wide) + bias_ref[...]
+    )
+
+
+def attend_kernel(
+    sizes, device, own_ref, other_ref, attn_ref, tokens_ref, gain_ref, o_ref, low_ref, middle_ref,
+    inv_ref, normed_ref, at_ref, acc_ref
+):
+    place_rows(*sizes, device, own_ref, other_ref, at_ref, acc_ref)
+    o_ref[...] = acc_ref[: o_ref.shape[0]].astype(low)
+    attn = attn_ref[...].astype(low)
+    low_ref[...] = attn
+    middle = tokens_ref[...].astype(wide) + jnp.dot(
+        attn, o_ref[...], preferred_element_type=wide
+    )
+    middle_ref[...] = middle
+    mean = jnp.sum(middle * middle, axis=1, keepdims=True) * (1.0 / middle.shape[1])
+    inv = lax.rsqrt(mean + norm_eps)
+    inv_ref[...] = inv
+    normed_ref[...] = (middle * inv * gain_ref[...]).astype(low)
+
+
+def assembled(kernel, name, device, own, other, take, operands, outputs, column=0, columns=1):
+    n_dp, n_group = lax.axis_size("dp"), lax.axis_size("group")
+    give = own.shape[0] // (n_dp // 2 * n_group)
+    width = own.shape[1] // columns
     size = n_dp * n_group * take
+    whole = lambda shape: pl.BlockSpec(shape, lambda i, m: (0,) * len(shape))
+    outputs = [((size, width), low)] + outputs
     return pl.pallas_call(
-        functools.partial(assemble_kernel, n_dp, n_group, take, give),
+        functools.partial(kernel, (n_dp, n_group, take, give)),
         grid_spec=pltpu.PrefetchScalarGridSpec(
             num_scalar_prefetch=1,
             grid=(1,),
-            in_specs=[pl.BlockSpec((own.shape[0], width), lambda i, m: (0, column))] * 2,
-            out_specs=[
-                pl.BlockSpec((size, width), lambda i, m: (0, 0)),
-                pl.BlockSpec((2, n_dp * n_group, width), lambda i, m: (0, 0, 0)),
-            ],
+            in_specs=[pl.BlockSpec((own.shape[0], width), lambda i, m: (0, column))] * 2
+            + [whole(a.shape) for a in operands],
+            out_specs=[whole(shape) for shape, _ in outputs],
             scratch_shapes=[
                 pltpu.VMEM((n_dp * n_group, give, width), wide),
                 pltpu.VMEM((size + give, width), wide),
             ],
         ),
-        out_shape=[
-            jax.ShapeDtypeStruct((size, width), low),
-            jax.ShapeDtypeStruct((2, n_dp * n_group, width), wide),
-        ],
+        out_shape=[jax.ShapeDtypeStruct(*output) for output in outputs],
         compiler_params=params(),
         cost_estimate=cost(1),
-        name="assemble_rows",
-    )(jnp.stack([me, mine]).astype(jnp.int32), own, other)
+        name=name,
+    )(device, own, other, *operands)
 
 
 def sum_kernel(*refs):
@@ -651,10 +736,71 @@
     )(*pieces)
 
 
+def return_kernel(near_ref, far_ref, *refs):
+    x_a, x_b, y_a, y_b, x_out, y_out = refs
+    top = pl.program_id(0) == 0
+    near, far = near_ref[...].astype(wide), far_ref[...].astype(wide)
+    x_sum = x_a[...].astype(wide) + x_b[...].astype(wide)
+    y_sum = y_a[...].astype(wide) + y_b[...].astype(wide)
+    x_out[...] = jnp.where(top, x_sum, x_sum + far).astype(low)
+    y_out[...] = jnp.where(top, y_sum + near, y_sum).astype(low)
+
+
+def return_sums(across, x_parts, y_parts):
+    half, width = across[0].shape
+    spec = pl.BlockSpec((half, width), lambda i: (i, 0))
+    one = pl.BlockSpec((half, width), lambda i: (0, 0))
+    return pl.pallas_call(
+        return_kernel,
+        grid=(2,),
+        in_specs=[one, one] + [spec] * 4,
+        out_specs=[spec] * 2,
+        out_shape=[jax.ShapeDtypeStruct((2 * half, width), low)] * 2,
+        compiler_params=params(),
+        cost_estimate=cost(0.1),
+        name="return_sums",
+    )(*across, *x_parts, *y_parts)
+
+
+def pack_kernel(keyval_ref, query_ref, output_ref, small_ref, second_ref, o_ref, buffer_ref):
+    rows = query_ref.shape[0]
+    piece = small_ref.shape[1]
+    buffer_ref[...] = jnp.zeros_like(buffer_ref)
+    at = 0
+    for ref in (keyval_ref, query_ref, output_ref):
+        buffer_ref[:rows, at : at + ref.shape[1]] = ref[...]
+        at += ref.shape[1]
+    second = second_ref[...]
+    first = second.astype(low).astype(wide)
+    rest = second - first
+    middle = rest.astype(low).astype(wide)
+    buffer_ref[rows : rows + 1, :piece] = small_ref[...]
+    buffer_ref[rows : rows + 1, piece : 2 * piece] = first
+    buffer_ref[rows + 1 : rows + 2, :piece] = middle
+    buffer_ref[rows + 1 : rows + 2, piece : 2 * piece] = rest - middle
+    o_ref[...] = buffer_ref[...].astype(low)
+
+
+def pack_rows(keyval, query, output, small, second, give):
+    arrays = (keyval, query, output, small[None], second[None])
+    width = sum(a.shape[1] for a in arrays[:3])
+    return pl.pallas_call(
+        pack_kernel,
+        grid=(1,),
+        in_specs=[pl.BlockSpec(a.shape, lambda i: (0, 0)) for a in arrays],
+        out_specs=pl.BlockSpec((give, width), lambda i: (0, 0)),
+        out_shape=jax.ShapeDtypeStruct((give, width), low),
+        scratch_shapes=[pltpu.VMEM((give, width), wide)],
+        compiler_params=params(),
+        cost_estimate=cost(0.5),
+        name="pack_rows",
+    )(*arrays)
+
+
 def stack_kernel(outer, count, take, give, meta, *refs):
     o_ref, at_ref, acc_ref = refs[count:]
     for s in range(count):
-        z = lax.rem(meta[0] + s, count)
+        z = lax.rem(meta[2] + s, count)
         for i in range(outer):
             at_ref[i * count + z] = refs[s][i * give : (i + 1) * give].astype(wide)
     for i in range(outer * count):
@@ -786,15 +932,6 @@
     return jnp.concatenate(evens, axis=0)
 
 
-def gather_rows(own, other, take, column=0, columns=1):
-    n_dp, n_group = lax.axis_size("dp"), lax.axis_size("group")
-    give = own.shape[0] // (n_dp // 2 * n_group)
-    return assemble(
-        own, other, n_dp, n_group, take, give, lax.axis_index("dp"), lax.axis_index("group"),
-        column, own.shape[1] // columns,
-    )
-
-
 def scatter_pair(keep, send):
     return keep.astype(wide) + flip(send, 1).astype(wide)
 
@@ -802,13 +939,6 @@
 def scatter_chips(pair):
     got = [flip(pair[r].astype(low), 2 * r) for r in range(1, pair.shape[0])]
     return add_up([pair[0]] + got)
-
-
-def split_low(value):
-    first = lax.reduce_precision(value, 8, 7)
-    rest = value - first
-    second = lax.reduce_precision(rest, 8, 7)
-    return [first.astype(low), second.astype(low), (rest - second).astype(low)]
 
 
 def body(
@@ -853,24 +983,23 @@
     part = FF // n_dp
     part_wide = padded(part, LANES)
     in_rows = query_weight.shape[0]
+    device = jnp.stack([my_dp & 1, my_dp >> 1, my_index, my_dp]).astype(jnp.int32)
     in_give = padded(in_rows + 2, ROWS)
     down_rows = down_weight.shape[0]
 
-    small_rows = [small_weight.astype(low)] + split_low(small_second)
-    small_rows = jnp.concatenate(small_rows).reshape(2, 2 * small_piece)
-    small_rows = jnp.pad(small_rows, ((0, 0), (0, 2 * kv_width - 2 * small_piece)))
-    keyval_block = jnp.concatenate([keyval_weight.astype(low), small_rows], axis=0)
-    keyval_block = jnp.pad(keyval_block, ((0, in_give - in_rows - 2), (0, 0)))
-    both_block = jnp.concatenate([query_weight.astype(low), output_weight.astype(low)], axis=1)
-    both_block = jnp.pad(both_block, ((0, in_give - in_rows), (0, 0)))
+    every_block = pack_rows(
+        keyval_weight, query_weight, output_weight, small_weight, small_second, in_give
+    )
     gateup_pieces = cut_columns(gateup_weight, n_dp, part_wide, in_give)
-    every_pieces = group_pieces(jnp.concatenate([keyval_block, both_block], axis=1))
+    every_pieces = group_pieces(every_block)
     every_column = jnp.concatenate(after(every_pieces, gateup_pieces), axis=0)
     keyval_column = every_column[:, : 2 * kv_width]
     both_column = every_column[:, 2 * kv_width :]
     keyval_own = gather_chips(keyval_column)
-    keyval_full, small_all = gather_rows(
-        keyval_own, flip(keyval_own, 1), in_rows
+    small_shape = (2, device_count, 2 * kv_width)
+    keyval_full, small_all = assembled(
+        assemble_kernel, "assemble_rows", device, keyval_own, flip(keyval_own, 1), in_rows, (),
+        [(small_shape, wide)],
     )
     small_all = small_all[:, :, : 2 * small_piece].reshape(2, device_count, 2, small_piece)
     small_values = small_all[0, :, 0].reshape(small_size)
@@ -880,7 +1009,6 @@
 
     down_part = lax.all_gather(down_weight.astype(low), "group", axis=0, tiled=True)
     down_part = jnp.pad(down_part, ((0, part_wide - part), (0, 0)))
-    me_group = my_index.astype(jnp.int32)[None]
 
     gain_one = small_values[:D]
     gain_two = small_values[D : 2 * D]
@@ -890,7 +1018,6 @@
     local_places = lax.dynamic_slice_in_dim(place_row, my_index * row_count, row_count, 0)
     starts = (local_index - local_places).reshape(2, half).astype(jnp.int32)
     starts = jnp.broadcast_to(starts[:, None, :], (2, 8, half))
-    meta = jnp.stack([my_index, my_index]).astype(jnp.int32)
     angles = rotary_angles(local_places)
     cosine, sine_table = jnp.cos(angles), jnp.sin(angles)
     cos_wide = jnp.concatenate([cosine] * 4, axis=1)
@@ -920,36 +1047,39 @@
     )
     cot_all = lax.all_gather(after(cotangent, both_own), "dp", axis=0, tiled=True)
     both_other = flip(both_own, 1)
-    query_full, _ = gather_rows(both_own, both_other, in_rows, 0, 2)
-    output_full, _ = gather_rows(both_own, both_other, in_rows, 1, 2)
-    query_pre = (
-        jnp.dot(normed_one, query_full, preferred_element_type=wide) + bias_qkv[:query_width]
+    query_full, query_pre = assembled(
+        project_kernel, "project_query", device, both_own, both_other, in_rows,
+        (normed_one, bias_qkv[None, :query_width]), [((row_count, query_width), wide)], 0, 2,
     )
     gateup_pieces = group_pieces(gateup_column)
     attn_float, log_total, query_low = attention_forward(
-        query_pre, cos_wide, sin_wide, starts, keyval_parts, meta
+        query_pre, cos_wide, sin_wide, starts, keyval_parts, device
     )
     attn_float = after(attn_float, gateup_pieces)
-    attn_low = attn_float.astype(low)
-    middle = act_in + jnp.dot(attn_low, output_full, preferred_element_type=wide)
-    inv_two = lax.rsqrt(jnp.mean(middle * middle, axis=1, keepdims=True) + norm_eps)
-    scaled_two = middle * inv_two
-    normed_two = (scaled_two * gain_two).astype(low)
+    output_full, attn_low, middle, inv_two, normed_two = assembled(
+        attend_kernel, "attention_output", device, both_own, both_other, in_rows,
+        (attn_float, tokens, gain_two[None]),
+        [
+            ((row_count, query_width), low),
+            ((row_count, D), wide),
+            ((row_count, 1), wide),
+            ((row_count, D), low),
+        ],
+        1, 2,
+    )
 
     gateup_pieces = after(gateup_pieces, normed_two)
-    gateup_part = stack_rows(gateup_pieces, n_dp, in_rows, me_group, D)
+    gateup_part = stack_rows(gateup_pieces, n_dp, in_rows, device, D)
     chips = n_dp // 2
     pieces, down_shape = (chips, 2, group_size), (1, 1, group_size)
-    device = jnp.stack([my_dp & 1, my_dp >> 1, my_index]).astype(jnp.int32)
     kept, sides, back = None, {0: normed_two}, {}
     for k in range(1, chips):
         if n_dp != 8 or k != 3:
             sides[k] = flip(normed_two, 2 * k)
 
     def visit(k, kept):
-        place = jnp.stack([my_dp ^ (2 * k), my_dp ^ (2 * k + 1)]).astype(jnp.int32)
         back_a, back_b, *kept = feed_forward(
-            sides[k], flip(sides[k], 1), cot_all, gateup_part, down_part, place, kept
+            sides[k], flip(sides[k], 1), cot_all, gateup_part, down_part, device, kept, k
         )
         back[k] = (back_a, flip(back_b, 1))
         return kept
@@ -964,41 +1094,40 @@
         corner = add_up(back[3]).astype(low)
         across = [flip(corner[:half], 2), flip(corner[half:], 4)]
         kept = visit(2, kept)
-        (down_term,) = weight_gradient(kept[1], cot_all, down_shape, down_rows, device)
+        down_term = weight_gradient(kept[1], cot_all, down_shape, down_rows, device)
         across = after(across, down_term)
-        nothing = jnp.zeros_like(across[0])
-        x_sum = add_up([*back[1], jnp.concatenate([nothing, across[1]], axis=0)]).astype(low)
-        y_sum = add_up([*back[2], jnp.concatenate([across[0], nothing], axis=0)]).astype(low)
+        x_sum, y_sum = return_sums(across, back[1], back[2])
         kept, y_sum = after((kept, y_sum))
         returned = [*back[0], flip(x_sum, 2), flip(y_sum, 4)]
     else:
         for k in range(chips):
             kept = visit(k, kept)
-        (down_term,) = weight_gradient(kept[1], cot_all, down_shape, down_rows, device)
+        down_term = weight_gradient(kept[1], cot_all, down_shape, down_rows, device)
         returned = list(back[0])
         returned += [flip(add_up(back[k]).astype(low), 2 * k) for k in range(1, chips)]
     out_all, _, gate_all, normed_all = kept
     down_got = group_send(down_term)
-    (gateup_term,) = weight_gradient(normed_all, gate_all, pieces, in_rows, device)
+    gateup_term = weight_gradient(normed_all, gate_all, pieces, in_rows, device)
     gateup_got = group_send(gateup_term)
     returned, gateup_got[0], down_got = after((returned, gateup_got[0], down_got))
-    grad_normed_two = add_up(returned)
     out_sum = lax.psum_scatter(after(out_all, returned), "dp", scatter_dimension=0, tiled=True)
 
-    grad_out = cotangent.astype(wide)
-    gain_scaled_two = grad_normed_two * gain_two
-    gain_two_term = jnp.sum(grad_normed_two * scaled_two, axis=0)
-    grad_middle = grad_out + inv_two * (
-        gain_scaled_two - scaled_two * jnp.mean(gain_scaled_two * scaled_two, axis=1, keepdims=True)
-    )
-    grad_middle_low = grad_middle.astype(low)
-    grad_attn_low = lax.dot_general(
-        grad_middle_low, output_full, NT, preferred_element_type=wide
-    ).astype(low)
-    both_terms = weight_gradient(
-        attn_low, grad_middle_low, pieces, in_rows, device, split=True, column=1, columns=2
-    )
-    grad_attn_low = after(grad_attn_low, both_terms)
+    if len(returned) > 4:
+        returned = returned[:3] + [add_up(returned[3:])]
+    grad_middle, grad_attn_low, gain_two_term, *both_terms = feed_back(
+        pieces,
+        in_rows,
+        device,
+        (
+            *returned,
+            middle,
+            inv_two,
+            gain_two[None],
+            cotangent,
+            attn_low,
+            output_full,
+        ),
+    )
     grad_query_pre, *keyval_terms = attention_backward(
         query_low,
         grad_attn_low,
@@ -1008,19 +1137,20 @@
         cosine.T,
         sine_table.T,
         keyval_parts,
-        meta,
-    )
-    grad_query_pre, keyval_terms = after(
-        (grad_query_pre, keyval_terms), gateup_got
-    )
+        device,
+    )
+    grad_query_pre, keyval_terms, gateup_got = after((grad_query_pre, keyval_terms, gateup_got))
     keyval_got = [keyval_terms[0]]
     keyval_got += [shift_within(keyval_terms[s], s) for s in range(1, group_size)]
     both_terms = weight_gradient(
         normed_one, grad_query_pre, pieces, in_rows, device, split=True, columns=2, into=both_terms
     )
-    both_pair = scatter_pair(both_terms[0], after(both_terms[1], keyval_got, out_sum))
+    gateup_sum = sum_pieces(after(gateup_got, both_terms)).reshape(n_dp, -1, 2 * part_wide)
+    to_send, gateup_sum = after((both_terms[1], gateup_sum), keyval_got, out_sum)
+    both_pair = scatter_pair(both_terms[0], to_send)
+    gateup_sum = lax.all_to_all(gateup_sum, "dp", 0, 0, tiled=True)
     both_total = scatter_chips(both_pair)
-    keyval_got = after(keyval_got, both_pair)
+    keyval_got, gateup_sum = after((keyval_got, gateup_sum), both_pair)
     bias_term = jnp.sum(grad_query_pre.astype(wide), axis=0)
     *last_terms, tokens_grad = finish_keyval(
         pieces,
@@ -1040,30 +1170,26 @@
             keyval_full,
             cos_wide,
             sin_wide,
-            jnp.concatenate([gain_two_term, bias_term])[None],
+            jnp.concatenate([gain_two_term, bias_term[None]], axis=1),
         ),
     )
     small_width = small_piece + rest_piece + value_piece
-    gateup_sum = sum_pieces(after(gateup_got, last_terms)).reshape(n_dp, -1, 2 * part_wide)
-    gateup_sum = lax.all_to_all(gateup_sum, "dp", 0, 0, tiled=True)
-    last_terms, gateup_sum = after((last_terms, gateup_sum), both_total)
+    gateup_grad, gateup_second_out, gateup_weight_out = update_columns(
+        after(gateup_sum, last_terms), gateup_first, gateup_second, gateup_weight
+    )
+    last_terms, gateup_second_out = after((last_terms, gateup_second_out), both_total)
     last_total = scatter_chips(scatter_pair(*last_terms))
     down_got = after(down_got, last_total)
     late_middle, out_sum = after((middle, out_sum), last_total)
     layer_out = (late_middle + out_sum.astype(wide)).astype(low)
     down_grad = add_up(down_got)[:down_rows]
-    gateup_grad, gateup_second_out, gateup_weight_out = update_columns(
-        gateup_sum, gateup_first, gateup_second, gateup_weight
-    )
     some = last_total.shape[1] - both_total.shape[1]
     both_total = jnp.pad(both_total, ((0, 0), (0, some), (0, 0)))
     down_second_out, down_weight_out = adamw_step(
         down_grad, down_first, down_second, down_weight, rate_proj, decay_rate
     )
     every_got = group_send(jnp.concatenate([both_total, last_total], axis=2))
-    every_got, gateup_second_out, down_second_out, layer_out = after(
-        (every_got, gateup_second_out, down_second_out, layer_out)
-    )
+    every_got, down_second_out, layer_out = after((every_got, down_second_out, layer_out))
     every_sum = add_up(every_got)
     query_grad = every_sum[:in_rows, :query_width]
     output_grad = every_sum[:in_rows, query_width : query_width + D]

time: 453 us -> 442 us (0.976)
  other arithmetic: 44.6 us -> 23.8 us
  Pallas kernels: 168 us -> 184 us
  matrix products: 9.99 us -> 0.44 us
    pallas_call x3 -> x6, Pallas kernels: 10.9 us -> 31.4 us  [the longest x3 14.6 us: assembled(): pl.pallas_call(functools.partial(kernel, (n_dp, n_group, take, give)), gr...]
    convert_element_type x10 -> x0, other arithmetic: 14.9 us -> none  [the longest x1 4.68 us: body(): grad_middle_low = grad_middle.astype(low)]
    dot_general x3 -> x0, matrix products: 9.55 us -> none  [the longest x1 4.07 us: body(): jnp.dot(normed_one, query_full, preferred_element_type=wide)]
    ppermute x15, waiting for transfers between devices: 67.4 us -> 74.2 us  [shift(): lax.ppermute(value, 'group', [((i + step) % count, i) for i in range(coun...]
    pallas_call x4 -> x3, Pallas kernels: 38.3 us -> 32.9 us  [weight_gradient(): pl.pallas_call(functools.partial(weight_kernel, steps, shape, take, give,...]
    unnamed x130 -> x158, local copies, waits for them, and re-layouts: 7.49 us -> 12.5 us
  transfers between devices with their start and end apart: 58 -> 58, of which waited for: 21 -> 19; matrix products, arithmetic and copies ran while one was open for 13% -> 7% of each run, Pallas kernels for 38% -> 42%
where the time goes in v3:
time: 442 us; the launch traced here: 435 us
  Pallas kernels  184 us (42%)
  waiting for transfers between devices  118 us (27%)
  starting transfers between devices  70.2 us (16%)
  other arithmetic  23.8 us (5%)
  local copies, waits for them, and re-layouts  23.5 us (5%)
  between operations  15.3 us (3%)
    ppermute x15, waiting for transfers between devices, shift(): lax.ppermute(value, 'group', [((i + step) % count, i) for i in range(coun...  74.2 us
    pallas_call x4, Pallas kernels, feed_forward(): pl.pallas_call(functools.partial(feed_kernel, steps, fresh), grid_spec=sp...  65.1 us
    pallas_call x3, Pallas kernels, weight_gradient(): pl.pallas_call(functools.partial(weight_kernel, steps, shape, take, give,...  32.9 us
    ppermute x32, starting transfers between devices, flip(): return lax.ppermute(value, 'dp', [(i, i ^ mask) for i in range(count)])  24.6 us
    ppermute x15, starting transfers between devices, shift(): lax.ppermute(value, 'group', [((i + step) % count, i) for i in range(coun...  23.9 us
    ppermute x32, waiting for transfers between devices, flip(): return lax.ppermute(value, 'dp', [(i, i ^ mask) for i in range(count)])  22.5 us
    ppermute x6, waiting for transfers between devices, shift_within(): return lax.ppermute(value, 'group', pairs)  16.5 us
    pallas_call x1, Pallas kernels, attention_forward(): pl.pallas_call(functools.partial(forward_kernel, pieces), grid_spec=spec,...  16.4 us
  transfers between devices with their start and end apart: 58, of which 19 were waited for; matrix products, arithmetic and copies ran while one was open for 7% of the time, Pallas kernels for 42%

profile of v3, /device:TPU:0, one launch (start us, length us, event | category | flops | bytes accessed | tf_op | source)
XLA Modules:
  0.0 435.3 jit_solution(2074867188716134)
XLA Ops:
  9.1 5.0 %collective-permute-start = (bf16[32,2048]{1,0:T(8,128)(2,1)}, bf16[32,2048]{1,0:T(8,128)(2,1)S(1)}, u32[]{:S(2)}, u32[]{:S(2)}) collective-permute-start(bf16[32,2048]{1,0:T(8,128)(2,1)} %pack_rows.1), channel_id=1, source_target_pairs={{1,0},{2,1},{3,2},{0,3},{5,4},{6,5},{7,6},{4,7},{9,8},{10,9},{11,1... | collective-permute-start | bytes 393224 | tf_op jit(solution)/shard_map/ppermute | solution.py:904
  20.1 5.5 %collective-permute-done.1 = bf16[32,2048]{1,0:T(8,128)(2,1)S(1)} collective-permute-done((bf16[32,2048]{1,0:T(8,128)(2,1)}, bf16[32,2048]{1,0:T(8,128)(2,1)S(1)}, u32[]{:S(2)}, u32[]{:S(2)}) %collective-permute-start.1) | collective-permute-done | bytes 131104 | tf_op jit(solution)/shard_map/ppermute | solution.py:904
  61.0 5.9 %collective-permute-done.8 = bf16[128,1792]{1,0:T(8,128)(2,1)S(1)} collective-permute-done((bf16[128,1792]{1,0:T(8,128)(2,1)S(1)}, bf16[128,1792]{1,0:T(8,128)(2,1)S(1)}, u32[]{:S(2)}, u32[]{:S(2)}) %collective-permute-start.8) | collective-permute-done | bytes 458784 | tf_op jit(solution)/shard_map/ppermute | solution.py:899
  75.5 7.7 %collective-permute-start.14 = (bf16[256,1280]{1,0:T(8,128)(2,1)}, bf16[256,1280]{1,0:T(8,128)(2,1)S(1)}, u32[]{:S(2)}, u32[]{:S(2)}) collective-permute-start(bf16[256,1280]{1,0:T(8,128)(2,1)} %bitcast.7.refs_0_), channel_id=1, source_target_pairs={{1,0},{2,1},{3,2},{0,3},{5,4},{6,5},{7,6},{4,7},{9,8},{10,9},{11,1... | collective-permute-start | bytes 1966088 | tf_op jit(solution)/shard_map/ppermute | solution.py:904
  83.8 5.5 %project_query.1 = (bf16[896,896]{1,0:T(8,128)(2,1)}, f32[512,896]{1,0:T(8,128)}) custom-call(s32[4]{0:T(128)} %pad_add_fusion.device.meta.where, bf16[512,1792]{1,0:T(8,128)(2,1)} %copy-done.9, bf16[512,1792]{1,0:T(8,128)(2,1)} %collective-permute-done.13.other_ref, bf16[512,896]{1,0:T(8,128)(2,1)} %copy-done.10, f32[1,896]{1,0:T(1,128)} %broadcast_in_dim.36.bias_ref), custom_call_target="tpu_custom_call" | custom-call | flops 1000000000 | bytes 1000000 | tf_op jit(solution)/shard_map/project_query/pallas_call | solution.py:696
  89.4 16.4 %attention_forward.1 = (f32[512,896]{1,0:T(8,128)S(1)}, f32[7,8,1024]{2,1,0:T(8,128)S(1)}, bf16[512,896]{1,0:T(8,128)(2,1)S(1)}) custom-call(s32[4]{0:T(128)S(1)} %copy-done.5, f32[512,896]{1,0:T(8,128)} %get-tuple-element.169.pre_ref, f32[512,128]{1,0:T(8,128)S(1)} %get-tuple-element.340.cos_ref, f32[512,128]{1,0:T(8,128)S(1)} %get-tuple-element.315.sin_ref, ...), custom_call_target="tpu_custom_call" | custom-call | flops 40000000000 | bytes 1000000 | tf_op jit(solution)/shard_map/attention_forward/pallas_call | solution.py:227
  107.1 32.2 %collective-permute-done.15.refs_2_ = bf16[256,1280]{1,0:T(8,128)(2,1)S(1)} collective-permute-done((bf16[256,1280]{1,0:T(8,128)(2,1)}, bf16[256,1280]{1,0:T(8,128)(2,1)S(1)}, u32[]{:S(2)}, u32[]{:S(2)}) %collective-permute-start.15) | collective-permute-done | bytes 655392 | tf_op jit(solution)/shard_map/ppermute | solution.py:904
  139.3 6.5 %attention_output.1 = (bf16[896,896]{1,0:T(8,128)(2,1)}, bf16[512,896]{1,0:T(8,128)(2,1)}, f32[512,896]{1,0:T(8,128)}, f32[512,1]{1,0:T(8,128)}, bf16[512,896]{1,0:T(8,128)(2,1)}) custom-call(s32[4]{0:T(128)} %pad_add_fusion.device.meta.where, bf16[512,1792]{1,0:T(8,128)(2,1)} %copy-done.9, bf16[512,1792]{1,0:T(8,128)(2,1)} %collective-permute-done.13.other_ref, ...), custom_call_target="tpu_custom_call" | custom-call | flops 1000000000 | bytes 1000000 | tf_op jit(solution)/shard_map/attention_output/pallas_call | solution.py:696
  149.1 4.8 %stack_rows.1.gateup_ref = bf16[896,1280]{1,0:T(8,128)(2,1)} custom-call(s32[4]{0:T(128)} %pad_add_fusion.device.meta.where, bf16[256,1280]{1,0:T(8,128)(2,1)} %bitcast.7.refs_0_, bf16[256,1280]{1,0:T(8,128)(2,1)} %copy-done.24, bf16[256,1280]{1,0:T(8,128)(2,1)} %copy-done.25, bf16[256,1280]{1,0:T(8,128)(2,1)} %copy-done.26), custom_call_target="tpu_custom_call" | custom-call | flops 1000000000 | bytes 1000000 | tf_op jit(solution)/shard_map/stack_rows/pallas_call | solution.py:818
  153.8 16.6 %feed_forward.4 = (bf16[512,896]{1,0:T(8,128)(2,1)}, bf16[512,896]{1,0:T(8,128)(2,1)}, bf16[4096,896]{1,0:T(8,128)(2,1)}, bf16[4096,640]{1,0:T(8,128)(2,1)}, bf1...) custom-call(s32[4]{0:T(128)} %pad_add_fusion.device.meta.where, bf16[512,896]{1,0:T(8,128)(2,1)} %get-tuple-element.178.n_a, ...), custom_call_target="tpu_custom_call" | custom-call | flops 15000000512 | bytes 1000000 | tf_op jit(solution)/shard_map/feed_forward/pallas_call | solution.py:406
  175.5 16.1 %feed_forward.5 = (bf16[512,896]{1,0:T(8,128)(2,1)}, bf16[512,896]{1,0:T(8,128)(2,1)}, bf16[4096,896]{1,0:T(8,128)(2,1)}, bf16[4096,640]{1,0:T(8,128)(2,1)}, bf1...) custom-call(s32[4]{0:T(128)} %pad_add_fusion.device.meta.where, ...), custom_call_target="tpu_custom_call", output_to_operand_aliasing={{2}: (6, {}), {3}: (7, {}), {4}: (8, {}), {5}: (9, {})} | custom-call | flops 15000000512 | bytes 1000000 | tf_op jit(solution)/shard_map/feed_forward/pallas_call | solution.py:406
  195.8 16.1 %feed_forward.6 = (bf16[512,896]{1,0:T(8,128)(2,1)}, bf16[512,896]{1,0:T(8,128)(2,1)}, bf16[4096,896]{1,0:T(8,128)(2,1)}, bf16[4096,640]{1,0:T(8,128)(2,1)}, bf1...) custom-call(s32[4]{0:T(128)} %pad_add_fusion.device.meta.where, ...), custom_call_target="tpu_custom_call", output_to_operand_aliasing={{2}: (6, {}), {3}: (7, {}), {4}: (8, {}), {5}: (9, {})} | custom-call | flops 15000000512 | bytes 1000000 | tf_op jit(solution)/shard_map/feed_forward/pallas_call | solution.py:406
  212.9 16.2 %feed_forward.7 = (bf16[512,896]{1,0:T(8,128)(2,1)}, bf16[512,896]{1,0:T(8,128)(2,1)}, bf16[4096,896]{1,0:T(8,128)(2,1)}, bf16[4096,640]{1,0:T(8,128)(2,1)}, bf1...) custom-call(s32[4]{0:T(128)} %pad_add_fusion.device.meta.where, ...), custom_call_target="tpu_custom_call", output_to_operand_aliasing={{2}: (6, {}), {3}: (7, {}), {4}: (8, {}), {5}: (9, {})} | custom-call | flops 15000000512 | bytes 1000000 | tf_op jit(solution)/shard_map/feed_forward/pallas_call | solution.py:406
  232.1 11.1 %weight_gradient.3 = (bf16[160,896]{1,0:T(8,128)(2,1)}, bf16[160,896]{1,0:T(8,128)(2,1)}, bf16[160,896]{1,0:T(8,128)(2,1)}, bf16[160,896]{1,0:T(8,128)(2,1)}) custom-call(s32[4]{0:T(128)} %pad_add_fusion.device.meta.where, bf16[4096,640]{1,0:T(8,128)(2,1)} %get-tuple-element.205.x_ref, bf16[4096,896]{1,0:T(8,128)(2,1)} %all-gather.5.cloned.1.call-done.cot_ref.y_ref), custom_call_target="tpu_custom_call" | custom-call | flops 200000000 | bytes 1000000 | tf_op jit(solution)/shard_map/weight_gradient/pallas_call | solution.py:470
  255.6 16.9 %weight_gradient.4 = (bf16[256,1280]{1,0:T(8,128)(2,1)}, bf16[256,1280]{1,0:T(8,128)(2,1)}, bf16[256,1280]{1,0:T(8,128)(2,1)}, bf16[256,1280]{1,0:T(8,128)(2,1)}) custom-call(s32[4]{0:T(128)} %pad_add_fusion.device.meta.where, bf16[4096,896]{1,0:T(8,128)(2,1)} %get-tuple-element.222.x_ref, bf16[4096,1280]{1,0:T(8,128)(2,1)} %get-tuple-element.223.y_ref), custom_call_target="tpu_custom_call" | custom-call | flops 200000000 | bytes 1000000 | tf_op jit(solution)/shard_map/weight_gradient/pallas_call | solution.py:470
  272.5 6.6 %collective-permute-done.34 = bf16[160,896]{1,0:T(8,128)(2,1)S(1)} collective-permute-done((bf16[160,896]{1,0:T(8,128)(2,1)S(1)}, bf16[160,896]{1,0:T(8,128)(2,1)S(1)}, u32[]{:S(2)}, u32[]{:S(2)}) %collective-permute-start.34) | collective-permute-done | bytes 286752 | tf_op jit(solution)/shard_map/ppermute | solution.py:904
  282.3 11.4 %feed_back.1 = (f32[512,896]{1,0:T(8,128)}, bf16[512,896]{1,0:T(8,128)(2,1)}, f32[1,896]{1,0:T(1,128)}, bf16[4,4,32,1792]{3,2,1,0:T(8,128)(2,1)}, bf16[4,4,32,1792]{3,2,1,0:T(8,128)(2,1)}) custom-call(s32[4]{0:T(128)} %pad_add_fusion.device.meta.where, bf16[512,896]{1,0:T(8,128)(2,1)} %get-tuple-element.225.a_ref, ...), custom_call_target="tpu_custom_call" | custom-call | flops 1000000000 | bytes 1000000 | tf_op jit(solution)/shard_map/feed_back/pallas_call | solution.py:533
  294.9 14.9 %attention_backward.1 = (bf16[512,896]{1,0:T(8,128)(2,1)S(1)}, f32[512,256]{1,0:T(8,128)S(1)}, bf16[512,256]{1,0:T(8,128)(2,1)S(1)}, bf16[512,256]{1,0:T(8,128)(2,1)S(1)}, bf16[512,256]{1,0:T(8,128)(2,1)S(1)}) custom-call(s32[4]{0:T(128)S(1)} %copy-done.6, bf16[512,896]{1,0:T(8,128)(2,1)S(1)} %get-tuple-element.174.q_ref, bf16[512,896]{1,0:T(8,128)(2,1)S(1)} %copy-done.7, ...), custom_call_target="tpu_custom_call" | custom-call | flops 40000000000 | bytes 1000000 | tf_op jit(solution)/shard_map/attention_backward/pallas_call | solution.py:330
  311.5 25.6 %collective-permute-done.37.refs_2_ = bf16[256,1280]{1,0:T(8,128)(2,1)S(1)} collective-permute-done((bf16[256,1280]{1,0:T(8,128)(2,1)}, bf16[256,1280]{1,0:T(8,128)(2,1)S(1)}, u32[]{:S(2)}, u32[]{:S(2)}) %collective-permute-start.37) | collective-permute-done | bytes 655392 | tf_op jit(solution)/shard_map/ppermute | solution.py:904
  341.0 4.8 %weight_gradient.5 = (bf16[4,4,32,1792]{3,2,1,0:T(8,128)(2,1)}, bf16[4,4,32,1792]{3,2,1,0:T(8,128)(2,1)}) custom-call(s32[4]{0:T(128)} %pad_add_fusion.device.meta.where, bf16[512,896]{1,0:T(8,128)(2,1)} %copy-done.10, bf16[512,896]{1,0:T(8,128)(2,1)} %copy-done, ...), custom_call_target="tpu_custom_call", output_to_operand_aliasing={{0}: (3, {}), {1}: (4, {})} | custom-call | flops 200000000 | bytes 1000000 | tf_op jit(solution)/shard_map/weight_gradient/pallas_call | solution.py:470
  348.7 16.5 %collective-permute-done.40.refs_2_ = bf16[512,256]{1,0:T(8,128)(2,1)S(1)} collective-permute-done((bf16[512,256]{1,0:T(8,128)(2,1)S(1)}, bf16[512,256]{1,0:T(8,128)(2,1)S(1)}, u32[]{:S(2)}, u32[]{:S(2)}) %collective-permute-start.40) | collective-permute-done | bytes 262176 | tf_op jit(solution)/shard_map/ppermute | solution.py:910
  383.4 7.8 %finish_keyval.1 = (bf16[4,4,32,256]{3,2,1,0:T(8,128)(2,1)}, bf16[4,4,32,256]{3,2,1,0:T(8,128)(2,1)}, bf16[512,896]{1,0:T(8,128)(2,1)}) custom-call(s32[4]{0:T(128)} %pad_add_fusion.device.meta.where, bf16[512,896]{1,0:T(8,128)(2,1)} %copy-done.10, f32[512,896]{1,0:T(8,128)} %get-tuple-element.321.scaled_ref, f32[512,1]{1,0:T(8,128)} %copy.61.inv_ref, ...), custom_call_target="tpu_custom_call" | custom-call | flops 20000000000 | bytes 1000000 | tf_op jit(solution)/shard_map/finish_keyval/pallas_call | solution.py:619
  391.2 5.1 %update_columns.1 = (f32[28,9728]{1,0:T(8,128)}, f32[28,9728]{1,0:T(8,128)}, f32[28,9728]{1,0:T(8,128)}) custom-call(bf16[8,32,1280]{2,1,0:T(8,128)(2,1)} %copy-done.14, f32[28,9728]{1,0:T(8,128)} %m_ref.1, f32[28,9728]{1,0:T(8,128)} %v_ref.1, f32[28,9728]{1,0:T(8,128)} %w_ref.3), custom_call_target="tpu_custom_call" | custom-call | flops 1000000000 | bytes 1000000 | tf_op jit(solution)/shard_map/update_columns/pallas_call | solution.py:883
  396.4 6.1 %collective-permute-done.44 = bf16[4,32,1792]{2,1,0:T(8,128)(2,1)S(1)} collective-permute-done((bf16[4,32,1792]{2,1,0:T(8,128)(2,1)S(1)}, bf16[4,32,1792]{2,1,0:T(8,128)(2,1)S(1)}, u32[]{:S(2)}, u32[]{:S(2)}) %collective-permute-start.44) | collective-permute-done | bytes 458784 | tf_op jit(solution)/shard_map/ppermute | solution.py:899
  (334 shorter events, 138.6 us)
Async XLA Ops:
  7.2 62.1 %all-gather.3.cloned.1.call-start = ((), (), s32[]{:S(2)}) async-start(), calls=%async_computation.3 | async-start | bytes 1361920 | tf_op jit(solution)/shard_map/all_gather | solution.py:1010
  44.7 22.2 %collective-permute-start.8 = (bf16[128,1792]{1,0:T(8,128)(2,1)S(1)}, bf16[128,1792]{1,0:T(8,128)(2,1)S(1)}, u32[]{:S(2)}, u32[]{:S(2)}) collective-permute-start(bf16[128,1792]{1,0:T(8,128)(2,1)S(1)} %slice.205), channel_id=1, source_target_pairs={{0,16},{4,20},{8,24},{12,28},{16,0},{20,4},{24,8},{28,12},{1,17},{... | collective-permute-start | bytes 1376264 | tf_op jit(solution)/shard_map/ppermute | solution.py:899
  45.3 22.5 %collective-permute-start.7 = (bf16[128,1792]{1,0:T(8,128)(2,1)S(1)}, bf16[128,1792]{1,0:T(8,128)(2,1)}, u32[]{:S(2)}, u32[]{:S(2)}) collective-permute-start(bf16[128,1792]{1,0:T(8,128)(2,1)S(1)} %slice.205), channel_id=1, source_target_pairs={{0,8},{4,12},{8,0},{12,4},{16,24},{20,28},{24,16},{28,20},{1,9},{5... | collective-permute-start | bytes 1376264 | tf_op jit(solution)/shard_map/ppermute | solution.py:899
  46.7 27.4 %all-to-all-start = ((bf16[8,32,1280]{2,1,0:T(8,128)(2,1)}), bf16[8,32,1280]{2,1,0:T(8,128)(2,1)}, u32[]{:S(2)}, u32[]{:S(2)}) async-start(bf16[8,32,1280]{2,1,0:T(8,128)(2,1)} %cut_columns.1), calls=%async_computation | async-start | bytes 1310720 | tf_op jit(solution)/shard_map/all_to_all | solution.py:1043
  50.9 102.9 %all-gather.5.cloned.1.call-start = ((), (), s32[]{:S(2)}) async-start(), calls=%async_computation.4 | async-start | bytes 8257536 | tf_op jit(solution)/shard_map/all_gather | solution.py:1048
  74.1 291.8 %reduce-scatter.2.cloned.1.call-start = ((), (), s32[]{:S(2)}) async-start(), calls=%async_computation.5 | async-start | bytes 8257536 | tf_op jit(solution)/shard_map/reduce_scatter | solution.py:1113
  75.5 31.6 %collective-permute-start.14 = (bf16[256,1280]{1,0:T(8,128)(2,1)}, bf16[256,1280]{1,0:T(8,128)(2,1)S(1)}, u32[]{:S(2)}, u32[]{:S(2)}) collective-permute-start(bf16[256,1280]{1,0:T(8,128)(2,1)} %bitcast.7.refs_0_), channel_id=1, source_target_pairs={{1,0},{2,1},{3,2},{0,3},{5,4},{6,5},{7,6},{4,7},{9,8},{10,9},{11,1... | collective-permute-start | bytes 1966088 | tf_op jit(solution)/shard_map/ppermute | solution.py:904
  83.2 56.1 %collective-permute-start.15 = (bf16[256,1280]{1,0:T(8,128)(2,1)}, bf16[256,1280]{1,0:T(8,128)(2,1)S(1)}, u32[]{:S(2)}, u32[]{:S(2)}) collective-permute-start(bf16[256,1280]{1,0:T(8,128)(2,1)} %bitcast.7.refs_0_), channel_id=1, source_target_pairs={{2,0},{3,1},{0,2},{1,3},{6,4},{7,5},{4,6},{5,7},{10,8},{11,9},{8,1... | collective-permute-start | bytes 1966088 | tf_op jit(solution)/shard_map/ppermute | solution.py:904
  83.2 56.1 %collective-permute-start.16 = (bf16[256,1280]{1,0:T(8,128)(2,1)}, bf16[256,1280]{1,0:T(8,128)(2,1)S(1)}, u32[]{:S(2)}, u32[]{:S(2)}) collective-permute-start(bf16[256,1280]{1,0:T(8,128)(2,1)} %bitcast.7.refs_0_), channel_id=1, source_target_pairs={{3,0},{0,1},{1,2},{2,3},{7,4},{4,5},{5,6},{6,7},{11,8},{8,9},{9,10... | collective-permute-start | bytes 1966088 | tf_op jit(solution)/shard_map/ppermute | solution.py:904
  145.8 24.6 %collective-permute-start.19 = (bf16[512,896]{1,0:T(8,128)(2,1)}, bf16[512,896]{1,0:T(8,128)(2,1)}, u32[]{:S(2)}, u32[]{:S(2)}) collective-permute-start(bf16[512,896]{1,0:T(8,128)(2,1)} %get-tuple-element.178.n_a), channel_id=1, source_target_pairs={{0,8},{4,12},{8,0},{12,4},{16,24},{20,28},{24,16},{28,20},{1,9},{5... | collective-permute-start | bytes 2752520 | tf_op jit(solution)/shard_map/ppermute | solution.py:899
  147.6 22.8 %collective-permute-start.20 = (bf16[512,896]{1,0:T(8,128)(2,1)}, bf16[512,896]{1,0:T(8,128)(2,1)}, u32[]{:S(2)}, u32[]{:S(2)}) collective-permute-start(bf16[512,896]{1,0:T(8,128)(2,1)} %get-tuple-element.178.n_a), channel_id=1, source_target_pairs={{0,16},{4,20},{8,24},{12,28},{16,0},{20,4},{24,8},{28,12},{1,17},{... | collective-permute-start | bytes 2752520 | tf_op jit(solution)/shard_map/ppermute | solution.py:899
  193.1 50.6 %collective-permute-start.29 = (bf16[512,896]{1,0:T(8,128)(2,1)S(1)}, bf16[512,896]{1,0:T(8,128)(2,1)S(1)}, u32[]{:S(2)}, u32[]{:S(2)}) collective-permute-start(bf16[512,896]{1,0:T(8,128)(2,1)S(1)} %copy-done.66), channel_id=1, source_target_pairs={{0,4},{4,0},{8,12},{12,8},{16,20},{20,16},{24,28},{28,24},{1,5},{5... | collective-permute-start | bytes 2752520 | tf_op jit(solution)/shard_map/ppermute | solution.py:899
  248.6 30.6 %collective-permute-start.31 = (bf16[512,896]{1,0:T(8,128)(2,1)}, bf16[512,896]{1,0:T(8,128)(2,1)}, u32[]{:S(2)}, u32[]{:S(2)}) collective-permute-start(bf16[512,896]{1,0:T(8,128)(2,1)} %get-tuple-element.216), channel_id=1, source_target_pairs={{0,8},{4,12},{8,0},{12,4},{16,24},{20,28},{24,16},{28,20},{1,9},{5... | collective-permute-start | bytes 2752520 | tf_op jit(solution)/shard_map/ppermute | solution.py:899
  249.1 30.1 %collective-permute-start.32 = (bf16[512,896]{1,0:T(8,128)(2,1)}, bf16[512,896]{1,0:T(8,128)(2,1)}, u32[]{:S(2)}, u32[]{:S(2)}) collective-permute-start(bf16[512,896]{1,0:T(8,128)(2,1)} %get-tuple-element.221), channel_id=1, source_target_pairs={{0,16},{4,20},{8,24},{12,28},{16,0},{20,4},{24,8},{28,12},{1,17},{... | collective-permute-start | bytes 2752520 | tf_op jit(solution)/shard_map/ppermute | solution.py:899
  250.2 22.4 %collective-permute-start.33 = (bf16[160,896]{1,0:T(8,128)(2,1)}, bf16[160,896]{1,0:T(8,128)(2,1)S(1)}, u32[]{:S(2)}, u32[]{:S(2)}) collective-permute-start(bf16[160,896]{1,0:T(8,128)(2,1)} %get-tuple-element.209), channel_id=1, source_target_pairs={{1,0},{2,1},{3,2},{0,3},{5,4},{6,5},{7,6},{4,7},{9,8},{10,9},{11,1... | collective-permute-start | bytes 860168 | tf_op jit(solution)/shard_map/ppermute | solution.py:904
  250.2 29.0 %collective-permute-start.34 = (bf16[160,896]{1,0:T(8,128)(2,1)S(1)}, bf16[160,896]{1,0:T(8,128)(2,1)S(1)}, u32[]{:S(2)}, u32[]{:S(2)}) collective-permute-start(bf16[160,896]{1,0:T(8,128)(2,1)S(1)} %copy-done.72), channel_id=1, source_target_pairs={{2,0},{3,1},{0,2},{1,3},{6,4},{7,5},{4,6},{5,7},{10,8},{11,9},{8,1... | collective-permute-start | bytes 860168 | tf_op jit(solution)/shard_map/ppermute | solution.py:904
  253.6 25.6 %collective-permute-start.35 = (bf16[160,896]{1,0:T(8,128)(2,1)S(1)}, bf16[160,896]{1,0:T(8,128)(2,1)}, u32[]{:S(2)}, u32[]{:S(2)}) collective-permute-start(bf16[160,896]{1,0:T(8,128)(2,1)S(1)} %copy-done.71), channel_id=1, source_target_pairs={{3,0},{0,1},{1,2},{2,3},{7,4},{4,5},{5,6},{6,7},{11,8},{8,9},{9,10... | collective-permute-start | bytes 860168 | tf_op jit(solution)/shard_map/ppermute | solution.py:904
  280.2 31.3 %collective-permute-start.36 = (bf16[256,1280]{1,0:T(8,128)(2,1)}, bf16[256,1280]{1,0:T(8,128)(2,1)S(1)}, u32[]{:S(2)}, u32[]{:S(2)}) collective-permute-start(bf16[256,1280]{1,0:T(8,128)(2,1)} %get-tuple-element.241), channel_id=1, source_target_pairs={{1,0},{2,1},{3,2},{0,3},{5,4},{6,5},{7,6},{4,7},{9,8},{10,9},{11,1... | collective-permute-start | bytes 1966088 | tf_op jit(solution)/shard_map/ppermute | solution.py:904
  280.3 56.8 %collective-permute-start.37 = (bf16[256,1280]{1,0:T(8,128)(2,1)}, bf16[256,1280]{1,0:T(8,128)(2,1)S(1)}, u32[]{:S(2)}, u32[]{:S(2)}) collective-permute-start(bf16[256,1280]{1,0:T(8,128)(2,1)} %get-tuple-element.242), channel_id=1, source_target_pairs={{2,0},{3,1},{0,2},{1,3},{6,4},{7,5},{4,6},{5,7},{10,8},{11,9},{8,1... | collective-permute-start | bytes 1966088 | tf_op jit(solution)/shard_map/ppermute | solution.py:904
  280.4 56.7 %collective-permute-start.38 = (bf16[256,1280]{1,0:T(8,128)(2,1)S(1)}, bf16[256,1280]{1,0:T(8,128)(2,1)S(1)}, u32[]{:S(2)}, u32[]{:S(2)}) collective-permute-start(bf16[256,1280]{1,0:T(8,128)(2,1)S(1)} %copy-done.70), channel_id=1, source_target_pairs={{3,0},{0,1},{1,2},{2,3},{7,4},{4,5},{5,6},{6,7},{11,8},{8,9},{9,10... | collective-permute-start | bytes 1966088 | tf_op jit(solution)/shard_map/ppermute | solution.py:904
  338.4 26.8 %collective-permute-start.40 = (bf16[512,256]{1,0:T(8,128)(2,1)S(1)}, bf16[512,256]{1,0:T(8,128)(2,1)S(1)}, u32[]{:S(2)}, u32[]{:S(2)}) collective-permute-start(bf16[512,256]{1,0:T(8,128)(2,1)S(1)} %get-tuple-element.259), channel_id=1, source_target_pairs={{2,0},{3,1},{6,4},{7,5},{10,8},{11,9},{14,12},{15,13},{18,16},{19,... | collective-permute-start | bytes 786440 | tf_op jit(solution)/shard_map/ppermute | solution.py:910
  339.7 26.2 %collective-permute-start.41 = (bf16[512,256]{1,0:T(8,128)(2,1)S(1)}, bf16[512,256]{1,0:T(8,128)(2,1)}, u32[]{:S(2)}, u32[]{:S(2)}) collective-permute-start(bf16[512,256]{1,0:T(8,128)(2,1)S(1)} %get-tuple-element.260), channel_id=1, source_target_pairs={{3,0},{7,4},{11,8},{15,12},{19,16},{23,20},{27,24},{31,28}} | collective-permute-start | bytes 786440 | tf_op jit(solution)/shard_map/ppermute | solution.py:910
  379.4 23.0 %collective-permute-start.44 = (bf16[4,32,1792]{2,1,0:T(8,128)(2,1)S(1)}, bf16[4,32,1792]{2,1,0:T(8,128)(2,1)S(1)}, u32[]{:S(2)}, u32[]{:S(2)}) collective-permute-start(bf16[4,32,1792]{2,1,0:T(8,128)(2,1)S(1)} %get-tuple-element.320), channel_id=1, source_target_pairs={{0,16},{4,20},{8,24},{12,28},{16,0},{20,4},{24,8},{28,12},{1,17},{... | collective-permute-start | bytes 1376264 | tf_op jit(solution)/shard_map/ppermute | solution.py:899
  380.0 22.5 %collective-permute-start.43 = (bf16[4,32,1792]{2,1,0:T(8,128)(2,1)S(1)}, bf16[4,32,1792]{2,1,0:T(8,128)(2,1)S(1)}, u32[]{:S(2)}, u32[]{:S(2)}) collective-permute-start(bf16[4,32,1792]{2,1,0:T(8,128)(2,1)S(1)} %get-tuple-element.318), channel_id=1, source_target_pairs={{0,8},{4,12},{8,0},{12,4},{16,24},{20,28},{24,16},{28,20},{1,9},{5... | collective-permute-start | bytes 1376264 | tf_op jit(solution)/shard_map/ppermute | solution.py:899
  (111 other events, 1074.3 us)
Sparse Core Ops, SparseCore 0:
  16.0 29.0 all-gather.2
  74.3 55.4 all-gather.4
  279.4 64.3 reduce-scatter.1

commit v4 on v3

--- a/solution.py
+++ b/solution.py
@@ -494,11 +494,18 @@
 ):
     chips, cores, groups = shape
     size = attn_ref.shape[1]
+    step = pl.program_id(0)
+
+    @pl.when(step == 0)
+    def _():
+        gain_out[...] = jnp.zeros_like(gain_out)
+        acc_ref[...] = jnp.zeros_like(acc_ref)
+
     grad = a_ref[...].astype(wide) + b_ref[...].astype(wide)
     grad = grad + (c_ref[...].astype(wide) + d_ref[...].astype(wide))
     inv = inv_ref[...]
     scaled = middle_ref[...] * inv
-    gain_out[...] = jnp.sum(grad * scaled, axis=0, keepdims=True)
+    gain_out[...] += jnp.sum(grad * scaled, axis=0, keepdims=True)
     grad = grad * gain_ref[...]
     mean = jnp.sum(grad * scaled, axis=1, keepdims=True) * (1.0 / size)
     grad = cot_ref[...].astype(wide) + inv * (grad - scaled * mean)
@@ -507,7 +514,7 @@
     do_ref[...] = lax.dot_general(
         grad_low, weight_ref[...], NT, preferred_element_type=wide
     ).astype(low)
-    acc_ref[:size] = lax.dot_general(attn_ref[...], grad_low, TN, preferred_element_type=wide)
+    acc_ref[:size] += lax.dot_general(attn_ref[...], grad_low, TN, preferred_element_type=wide)
     keep = lax.broadcasted_iota(jnp.int32, (give, 1), 0) < take
 
     def write(mine):
@@ -521,22 +528,26 @@
                     target[chip ^ where[1], at] = value.astype(low)
 
     for mine in range(cores):
-        pl.when(where[0] == mine)(functools.partial(write, mine))
+        here = (step == pl.num_programs(0) - 1) & (where[0] == mine)
+        pl.when(here)(functools.partial(write, mine))
 
 
 def feed_back(shape, take, where, operands):
     chips, cores, groups = shape
     rows, size = operands[8].shape
     give = padded(take, ROWS)
+    block = min(256, rows)
+    part = lambda n: pl.BlockSpec((block, n), lambda i, w: (i, 0))
+    spec = lambda a: part(a.shape[1]) if a.shape[0] == rows else whole(a.shape)
     whole = lambda shape: pl.BlockSpec(shape, lambda i, w: (0,) * len(shape))
     pieces = pl.BlockSpec((chips, groups, give, size), lambda i, w: (0, 0, 0, 1))
     return pl.pallas_call(
         functools.partial(feed_back_kernel, shape, take, give),
         grid_spec=pltpu.PrefetchScalarGridSpec(
             num_scalar_prefetch=1,
-            grid=(1,),
-            in_specs=[whole(a.shape) for a in operands],
-            out_specs=[whole((rows, size)), whole((rows, size)), whole((1, size)), pieces, pieces],
+            grid=(rows // block,),
+            in_specs=[spec(a) for a in operands],
+            out_specs=[part(size), part(size), whole((1, size)), pieces, pieces],
             scratch_shapes=[pltpu.VMEM((padded(size, 8) + give, size), wide)],
         ),
         out_shape=[
@@ -649,13 +660,39 @@
         acc_ref[i * take : i * take + give] = at_ref[i]
 
 
-def assemble_kernel(sizes, device, own_ref, other_ref, o_ref, small_ref, at_ref, acc_ref):
+def keyval_kernel(
+    piece, sizes, device, own_ref, other_ref, tokens_ref, cos_ref, sin_ref, o_ref, small_ref,
+    second_ref, inv_ref, scaled_ref, normed_ref, keyval_ref, at_ref, acc_ref
+):
     place_rows(*sizes, device, own_ref, other_ref, at_ref, acc_ref)
     count, take = sizes[0] * sizes[1], sizes[2]
+    o_ref[...] = acc_ref[: o_ref.shape[0]].astype(low)
     for i in range(count):
-        for j in range(2):
-            small_ref[j, i : i + 1] = at_ref[i, take + j : take + j + 1]
-    o_ref[...] = acc_ref[: o_ref.shape[0]].astype(low)
+        first = at_ref[i, take : take + 1]
+        rest = at_ref[i, take + 1 : take + 2]
+        cut = slice(i * piece, (i + 1) * piece)
+        small_ref[:, cut] = first[:, :piece]
+        second_ref[:, cut] = (
+            first[:, piece : 2 * piece] + rest[:, :piece] + rest[:, piece : 2 * piece]
+        )
+    tokens = tokens_ref[...].astype(wide)
+    size, width = tokens.shape[1], o_ref.shape[1]
+    mean = jnp.sum(tokens * tokens, axis=1, keepdims=True) * (1.0 / size)
+    inv = lax.rsqrt(mean + norm_eps)
+    inv_ref[...] = inv
+    scaled = tokens * inv
+    scaled_ref[...] = scaled
+    normed = (scaled * small_ref[:, :size]).astype(low)
+    normed_ref[...] = normed
+    pre = jnp.dot(normed, o_ref[...], preferred_element_type=wide)
+    pre = pre + small_ref[:, small_ref.shape[1] - width :]
+    keys = pre[:, :LANES]
+    lane = lax.broadcasted_iota(jnp.int32, keys.shape, 1)
+    swapped = jnp.where(
+        lane % HD < HD // 2, pltpu.roll(keys, LANES - HD // 2, 1), pltpu.roll(keys, HD // 2, 1)
+    )
+    keyval_ref[:, :LANES] = (keys * cos_ref[...] + swapped * sin_ref[...]).astype(low)
+    keyval_ref[:, LANES:] = pre[:, LANES:].astype(low)
 
 
 def project_kernel(
@@ -708,7 +745,7 @@
         ),
         out_shape=[jax.ShapeDtypeStruct(*output) for output in outputs],
         compiler_params=params(),
-        cost_estimate=cost(1),
+        cost_estimate=cost(0.1),
         name=name,
     )(device, own, other, *operands)
 
@@ -795,6 +832,25 @@
         cost_estimate=cost(0.5),
         name="pack_rows",
     )(*arrays)
+
+
+def fill_kernel(x_ref, o_ref):
+    rows = x_ref.shape[0]
+    o_ref[:rows] = x_ref[...]
+    o_ref[rows:] = jnp.zeros_like(o_ref[rows:])
+
+
+def fill_rows(block, rows):
+    return pl.pallas_call(
+        fill_kernel,
+        grid=(1,),
+        in_specs=[pl.BlockSpec(block.shape, lambda i: (0, 0))],
+        out_specs=pl.BlockSpec((rows, block.shape[1]), lambda i: (0, 0)),
+        out_shape=jax.ShapeDtypeStruct((rows, block.shape[1]), block.dtype),
+        compiler_params=params(),
+        cost_estimate=cost(20),
+        name="fill_rows",
+    )(block)
 
 
 def stack_kernel(outer, count, take, give, meta, *refs):
@@ -990,29 +1046,6 @@
     every_block = pack_rows(
         keyval_weight, query_weight, output_weight, small_weight, small_second, in_give
     )
-    gateup_pieces = cut_columns(gateup_weight, n_dp, part_wide, in_give)
-    every_pieces = group_pieces(every_block)
-    every_column = jnp.concatenate(after(every_pieces, gateup_pieces), axis=0)
-    keyval_column = every_column[:, : 2 * kv_width]
-    both_column = every_column[:, 2 * kv_width :]
-    keyval_own = gather_chips(keyval_column)
-    small_shape = (2, device_count, 2 * kv_width)
-    keyval_full, small_all = assembled(
-        assemble_kernel, "assemble_rows", device, keyval_own, flip(keyval_own, 1), in_rows, (),
-        [(small_shape, wide)],
-    )
-    small_all = small_all[:, :, : 2 * small_piece].reshape(2, device_count, 2, small_piece)
-    small_values = small_all[0, :, 0].reshape(small_size)
-    small_second_all = (small_all[0, :, 1] + small_all[1, :, 0] + small_all[1, :, 1]).reshape(
-        small_size
-    )
-
-    down_part = lax.all_gather(down_weight.astype(low), "group", axis=0, tiled=True)
-    down_part = jnp.pad(down_part, ((0, part_wide - part), (0, 0)))
-
-    gain_one = small_values[:D]
-    gain_two = small_values[D : 2 * D]
-    bias_qkv = small_values[2 * D :]
     place_row = positions[0]
     local_index = my_index * row_count + jnp.arange(row_count, dtype=jnp.int32)
     local_places = lax.dynamic_slice_in_dim(place_row, my_index * row_count, row_count, 0)
@@ -1023,42 +1056,49 @@
     cos_wide = jnp.concatenate([cosine] * 4, axis=1)
     sin_wide = jnp.concatenate([-sine_table, sine_table] * 2, axis=1)
 
-    def swap(values):
-        quarter = HD // 2
-        pieces = [values[:, i * quarter : (i + 1) * quarter] for i in range(2 * HK)]
-        return jnp.concatenate([pieces[i ^ 1] for i in range(2 * HK)], axis=1)
-
-    act_in = tokens.astype(wide)
-    inv_one = lax.rsqrt(jnp.mean(act_in * act_in, axis=1, keepdims=True) + norm_eps)
-    scaled_one = act_in * inv_one
-    normed_one = (scaled_one * gain_one).astype(low)
-    keyval_pre = (
-        jnp.dot(normed_one, keyval_full, preferred_element_type=wide) + bias_qkv[query_width:]
-    )
-    key_pre = keyval_pre[:, :kv_width]
-    key_low = (key_pre * cos_wide + swap(key_pre) * sin_wide).astype(low)
-    keyval_low = jnp.concatenate([key_low, keyval_pre[:, kv_width:].astype(low)], axis=1)
+    gateup_pieces = cut_columns(gateup_weight, n_dp, part_wide, in_give)
+    every_pieces = group_pieces(every_block)
+    every_pieces, cos_wide, sin_wide = after((every_pieces, cos_wide, sin_wide), gateup_pieces)
+    every_column = jnp.concatenate(every_pieces, axis=0)
+    keyval_column = every_column[:, : 2 * kv_width]
+    both_column = every_column[:, 2 * kv_width :]
+    keyval_own = gather_chips(keyval_column)
+    down_part = lax.all_gather(down_weight.astype(low), "group", axis=0, tiled=True)
+
+    keyval_full, small_row, second_row, inv_one, scaled_one, normed_one, keyval_low = assembled(
+        functools.partial(keyval_kernel, small_piece), "project_keyval", device,
+        keyval_own, flip(keyval_own, 1), in_rows, (tokens, cos_wide, sin_wide),
+        [
+            ((1, small_size), wide),
+            ((1, small_size), wide),
+            ((row_count, 1), wide),
+            ((row_count, D), wide),
+            ((row_count, D), low),
+            ((row_count, 2 * kv_width), low),
+        ],
+    )
+    gain_one, gain_two = small_row[:, :D], small_row[:, D : 2 * D]
+    bias_query = small_row[:, 2 * D : 2 * D + query_width]
     keyval_parts = [keyval_low] + [shift_within(keyval_low, -s) for s in range(1, group_size)]
     both_own = gather_chips(after(both_column, keyval_low))
     gateup_column = lax.all_to_all(after(gateup_pieces, keyval_low), "dp", 0, 0, tiled=True)
     gateup_column = gateup_column.reshape(n_dp * in_give, 2 * part_wide)
-    both_own, keyval_parts, gateup_column, down_part = after(
-        (both_own, keyval_parts, gateup_column, down_part)
-    )
+    keyval_parts, down_part = after((keyval_parts, down_part))
+    down_part = fill_rows(down_part, part_wide)
+    both_own, gateup_column, down_part = after((both_own, gateup_column, down_part))
     cot_all = lax.all_gather(after(cotangent, both_own), "dp", axis=0, tiled=True)
     both_other = flip(both_own, 1)
     query_full, query_pre = assembled(
         project_kernel, "project_query", device, both_own, both_other, in_rows,
-        (normed_one, bias_qkv[None, :query_width]), [((row_count, query_width), wide)], 0, 2,
+        (normed_one, bias_query), [((row_count, query_width), wide)], 0, 2,
     )
     gateup_pieces = group_pieces(gateup_column)
     attn_float, log_total, query_low = attention_forward(
         query_pre, cos_wide, sin_wide, starts, keyval_parts, device
     )
-    attn_float = after(attn_float, gateup_pieces)
     output_full, attn_low, middle, inv_two, normed_two = assembled(
         attend_kernel, "attention_output", device, both_own, both_other, in_rows,
-        (attn_float, tokens, gain_two[None]),
+        (attn_float, tokens, gain_two),
         [
             ((row_count, query_width), low),
             ((row_count, D), wide),
@@ -1068,7 +1108,7 @@
         1, 2,
     )
 
-    gateup_pieces = after(gateup_pieces, normed_two)
+    normed_two, gateup_pieces = after((normed_two, gateup_pieces))
     gateup_part = stack_rows(gateup_pieces, n_dp, in_rows, device, D)
     chips = n_dp // 2
     pieces, down_shape = (chips, 2, group_size), (1, 1, group_size)
@@ -1109,7 +1149,8 @@
     down_got = group_send(down_term)
     gateup_term = weight_gradient(normed_all, gate_all, pieces, in_rows, device)
     gateup_got = group_send(gateup_term)
-    returned, gateup_got[0], down_got = after((returned, gateup_got[0], down_got))
+    returned, gateup_got[0], early = after((returned, gateup_got[0], down_got[1:-1]))
+    down_got[1:-1] = early
     out_sum = lax.psum_scatter(after(out_all, returned), "dp", scatter_dimension=0, tiled=True)
 
     if len(returned) > 4:
@@ -1122,7 +1163,7 @@
             *returned,
             middle,
             inv_two,
-            gain_two[None],
+            gain_two,
             cotangent,
             attn_low,
             output_full,
@@ -1139,17 +1180,18 @@
         keyval_parts,
         device,
     )
-    grad_query_pre, keyval_terms, gateup_got = after((grad_query_pre, keyval_terms, gateup_got))
+    both_terms = weight_gradient(
+        normed_one, grad_query_pre, pieces, in_rows, device, split=True, columns=2, into=both_terms
+    )
+    keyval_terms, both_terms, gateup_got, down_got = after(
+        (keyval_terms, both_terms, gateup_got, down_got)
+    )
     keyval_got = [keyval_terms[0]]
     keyval_got += [shift_within(keyval_terms[s], s) for s in range(1, group_size)]
-    both_terms = weight_gradient(
-        normed_one, grad_query_pre, pieces, in_rows, device, split=True, columns=2, into=both_terms
-    )
-    gateup_sum = sum_pieces(after(gateup_got, both_terms)).reshape(n_dp, -1, 2 * part_wide)
-    to_send, gateup_sum = after((both_terms[1], gateup_sum), keyval_got, out_sum)
-    both_pair = scatter_pair(both_terms[0], to_send)
+    both_pair = scatter_pair(both_terms[0], after(both_terms[1], out_sum))
+    both_total = scatter_chips(both_pair)
+    gateup_sum = sum_pieces(gateup_got).reshape(n_dp, -1, 2 * part_wide)
     gateup_sum = lax.all_to_all(gateup_sum, "dp", 0, 0, tiled=True)
-    both_total = scatter_chips(both_pair)
     keyval_got, gateup_sum = after((keyval_got, gateup_sum), both_pair)
     bias_term = jnp.sum(grad_query_pre.astype(wide), axis=0)
     *last_terms, tokens_grad = finish_keyval(
@@ -1163,7 +1205,7 @@
             normed_one,
             scaled_one,
             inv_one,
-            gain_one[None],
+            gain_one,
             grad_query_pre,
             query_full,
             grad_middle,
@@ -1213,10 +1255,10 @@
         small_grad, small_first, small_second, small_weight, rate_small, 0.0
     )
     rest_second = lax.dynamic_slice_in_dim(
-        small_second_all, flat_index * rest_piece, rest_piece, 0
+        second_row[0], flat_index * rest_piece, rest_piece, 0
     )
     value_second = lax.dynamic_slice_in_dim(
-        small_second_all, rest_length + flat_index * value_piece, value_piece, 0
+        second_row[0], rest_length + flat_index * value_piece, value_piece, 0
     )
     small_second_out = beta_two * rest_second + (1.0 - beta_two) * rest_grad * rest_grad
     value_bias_second_out = beta_two * value_second + (1.0 - beta_two) * value_grad * value_grad

time: 442 us -> 414 us (0.937)
  waiting for transfers between devices: 118 us -> 90.3 us
  local copies, waits for them, and re-layouts: 23.5 us -> 15.5 us
  Pallas kernels: 184 us -> 189 us
    ppermute x15, waiting for transfers between devices: 74.2 us -> 61.2 us  [shift(): lax.ppermute(value, 'group', [((i + step) % count, i) for i in range(coun...]
    ppermute x6, waiting for transfers between devices: 16.5 us -> 8.51 us  [shift_within(): return lax.ppermute(value, 'group', pairs)]
    ppermute x15, starting transfers between devices: 23.9 us -> 28.6 us  [shift(): lax.ppermute(value, 'group', [((i + step) % count, i) for i in range(coun...]
    unnamed x158 -> x124, local copies, waits for them, and re-layouts: 12.5 us -> 11.6 us
  transfers between devices with their start and end apart: 58 -> 58, of which waited for: 19 -> 21; matrix products, arithmetic and copies ran while one was open for 7% -> 5% of each run, Pallas kernels for 42% -> 46%
where the time goes in v4:
time: 414 us; the launch traced here: 408 us
  Pallas kernels  189 us (46%)
  waiting for transfers between devices  90.3 us (22%)
  starting transfers between devices  74.4 us (18%)
  other arithmetic  23 us (6%)
  local copies, waits for them, and re-layouts  15.5 us (4%)
  between operations  15.1 us (4%)
    pallas_call x4, Pallas kernels, feed_forward(): pl.pallas_call(functools.partial(feed_kernel, steps, fresh), grid_spec=sp...  65 us
    ppermute x15, waiting for transfers between devices, shift(): lax.ppermute(value, 'group', [((i + step) % count, i) for i in range(coun...  61.2 us
    pallas_call x3, Pallas kernels, weight_gradient(): pl.pallas_call(functools.partial(weight_kernel, steps, shape, take, give,...  33.1 us
    ppermute x15, starting transfers between devices, shift(): lax.ppermute(value, 'group', [((i + step) % count, i) for i in range(coun...  28.6 us
    ppermute x32, starting transfers between devices, flip(): return lax.ppermute(value, 'dp', [(i, i ^ mask) for i in range(count)])  24 us
    ppermute x32, waiting for transfers between devices, flip(): return lax.ppermute(value, 'dp', [(i, i ^ mask) for i in range(count)])  18.3 us
    pallas_call x3, Pallas kernels, assembled(): pl.pallas_call(functools.partial(kernel, (n_dp, n_group, take, give)), gr...  17.7 us
    pallas_call x1, Pallas kernels, attention_forward(): pl.pallas_call(functools.partial(forward_kernel, pieces), grid_spec=spec,...  16.4 us
  transfers between devices with their start and end apart: 58, of which 21 were waited for; matrix products, arithmetic and copies ran while one was open for 5% of the time, Pallas kernels for 46%

profile of v4, /device:TPU:0, one launch (start us, length us, event | category | flops | bytes accessed | tf_op | source)
XLA Modules:
  0.0 407.5 jit_solution(9520451289777876636)
XLA Ops:
  9.0 5.0 %collective-permute-start = (bf16[32,2048]{1,0:T(8,128)(2,1)}, bf16[32,2048]{1,0:T(8,128)(2,1)S(1)}, u32[]{:S(2)}, u32[]{:S(2)}) collective-permute-start(bf16[32,2048]{1,0:T(8,128)(2,1)} %pack_rows.1), channel_id=1, source_target_pairs={{1,0},{2,1},{3,2},{0,3},{5,4},{6,5},{7,6},{4,7},{9,8},{10,9},{11,1... | collective-permute-start | bytes 393224 | tf_op jit(solution)/shard_map/ppermute | solution.py:960
  35.2 5.4 %project_keyval.1 = (bf16[896,256]{1,0:T(8,128)(2,1)}, f32[1,2944]{1,0:T(1,128)}, f32[1,2944]{1,0:T(1,128)}, f32[512,1]{1,0:T(8,128)}, f32[512,896]{1,0:T(8,128)...) custom-call(s32[4]{0:T(128)} %pad_add_fusion.device.meta.where, bf16[512,256]{1,0:T(8,128)(2,1)} %copy-done.19, ...), custom_call_target="tpu_custom_call" | custom-call | flops 100000000 | bytes 1000000 | tf_op jit(solution)/shard_map/project_keyval/pallas_call | solution.py:733
  58.4 5.6 %collective-permute-done.8 = bf16[128,1792]{1,0:T(8,128)(2,1)S(1)} collective-permute-done((bf16[128,1792]{1,0:T(8,128)(2,1)S(1)}, bf16[128,1792]{1,0:T(8,128)(2,1)S(1)}, u32[]{:S(2)}, u32[]{:S(2)}) %collective-permute-start.8) | collective-permute-done | bytes 458784 | tf_op jit(solution)/shard_map/ppermute | solution.py:955
  71.7 5.4 %collective-permute-start.14 = (bf16[256,1280]{1,0:T(8,128)(2,1)S(1)}, bf16[256,1280]{1,0:T(8,128)(2,1)S(1)}, u32[]{:S(2)}, u32[]{:S(2)}) collective-permute-start(bf16[256,1280]{1,0:T(8,128)(2,1)S(1)} %bitcast.64), channel_id=1, source_target_pairs={{1,0},{2,1},{3,2},{0,3},{5,4},{6,5},{7,6},{4,7},{9,8},{10,9},{11,1... | collective-permute-start | bytes 1966088 | tf_op jit(solution)/shard_map/ppermute | solution.py:960
  77.8 5.9 %project_query.1 = (bf16[896,896]{1,0:T(8,128)(2,1)}, f32[512,896]{1,0:T(8,128)}) custom-call(s32[4]{0:T(128)} %pad_add_fusion.device.meta.where, bf16[512,1792]{1,0:T(8,128)(2,1)} %copy-done.10, bf16[512,1792]{1,0:T(8,128)(2,1)} %collective-permute-done.13.other_ref, bf16[512,896]{1,0:T(8,128)(2,1)} %get-tuple-element.177.normed_ref.x_ref, ...), custom_call_target="tpu_custom_call" | custom-call | flops 100000000 | bytes 1000000 | tf_op jit(solution)/shard_map/project_query/pallas_call | solution.py:733
  83.8 16.4 %attention_forward.1 = (f32[512,896]{1,0:T(8,128)S(1)}, f32[7,8,1024]{2,1,0:T(8,128)S(1)}, bf16[512,896]{1,0:T(8,128)(2,1)S(1)}) custom-call(s32[4]{0:T(128)S(1)} %copy-done.5, f32[512,896]{1,0:T(8,128)} %get-tuple-element.179.pre_ref, f32[512,128]{1,0:T(8,128)S(1)} %copy-done.3, f32[512,128]{1,0:T(8,128)S(1)} %copy-done.4, ...), custom_call_target="tpu_custom_call" | custom-call | flops 40000000000 | bytes 1000000 | tf_op jit(solution)/shard_map/attention_forward/pallas_call | solution.py:227
  101.5 6.5 %attention_output.1 = (bf16[896,896]{1,0:T(8,128)(2,1)}, bf16[512,896]{1,0:T(8,128)(2,1)}, f32[512,896]{1,0:T(8,128)}, f32[512,1]{1,0:T(8,128)}, bf16[512,896]{1,0:T(8,128)(2,1)}) custom-call(s32[4]{0:T(128)} %pad_add_fusion.device.meta.where, bf16[512,1792]{1,0:T(8,128)(2,1)} %copy-done.10, bf16[512,1792]{1,0:T(8,128)(2,1)} %collective-permute-done.13.other_ref, ...), custom_call_target="tpu_custom_call" | custom-call | flops 100000000 | bytes 1000000 | tf_op jit(solution)/shard_map/attention_output/pallas_call | solution.py:733
  108.0 25.2 %collective-permute-done.15.refs_2_ = bf16[256,1280]{1,0:T(8,128)(2,1)S(1)} collective-permute-done((bf16[256,1280]{1,0:T(8,128)(2,1)S(1)}, bf16[256,1280]{1,0:T(8,128)(2,1)S(1)}, u32[]{:S(2)}, u32[]{:S(2)}) %collective-permute-start.15) | collective-permute-done | bytes 655392 | tf_op jit(solution)/shard_map/ppermute | solution.py:960
  135.4 4.7 %stack_rows.1.gateup_ref = bf16[896,1280]{1,0:T(8,128)(2,1)} custom-call(s32[4]{0:T(128)} %pad_add_fusion.device.meta.where, bf16[256,1280]{1,0:T(8,128)(2,1)} %bitcast.67, bf16[256,1280]{1,0:T(8,128)(2,1)} %copy-done.25, bf16[256,1280]{1,0:T(8,128)(2,1)} %copy-done.26, bf16[256,1280]{1,0:T(8,128)(2,1)} %copy-done.27), custom_call_target="tpu_custom_call" | custom-call | flops 1000000000 | bytes 1000000 | tf_op jit(solution)/shard_map/stack_rows/pallas_call | solution.py:874
  140.1 16.6 %feed_forward.4 = (bf16[512,896]{1,0:T(8,128)(2,1)}, bf16[512,896]{1,0:T(8,128)(2,1)}, bf16[4096,896]{1,0:T(8,128)(2,1)}, bf16[4096,640]{1,0:T(8,128)(2,1)}, bf1...) custom-call(s32[4]{0:T(128)} %pad_add_fusion.device.meta.where, bf16[512,896]{1,0:T(8,128)(2,1)} %get-tuple-element.188.n_a, ...), custom_call_target="tpu_custom_call" | custom-call | flops 15000000512 | bytes 1000000 | tf_op jit(solution)/shard_map/feed_forward/pallas_call | solution.py:406
  162.0 16.1 %feed_forward.5 = (bf16[512,896]{1,0:T(8,128)(2,1)}, bf16[512,896]{1,0:T(8,128)(2,1)}, bf16[4096,896]{1,0:T(8,128)(2,1)}, bf16[4096,640]{1,0:T(8,128)(2,1)}, bf1...) custom-call(s32[4]{0:T(128)} %pad_add_fusion.device.meta.where, ...), custom_call_target="tpu_custom_call", output_to_operand_aliasing={{2}: (6, {}), {3}: (7, {}), {4}: (8, {}), {5}: (9, {})} | custom-call | flops 15000000512 | bytes 1000000 | tf_op jit(solution)/shard_map/feed_forward/pallas_call | solution.py:406
  181.7 16.1 %feed_forward.6 = (bf16[512,896]{1,0:T(8,128)(2,1)}, bf16[512,896]{1,0:T(8,128)(2,1)}, bf16[4096,896]{1,0:T(8,128)(2,1)}, bf16[4096,640]{1,0:T(8,128)(2,1)}, bf1...) custom-call(s32[4]{0:T(128)} %pad_add_fusion.device.meta.where, ...), custom_call_target="tpu_custom_call", output_to_operand_aliasing={{2}: (6, {}), {3}: (7, {}), {4}: (8, {}), {5}: (9, {})} | custom-call | flops 15000000512 | bytes 1000000 | tf_op jit(solution)/shard_map/feed_forward/pallas_call | solution.py:406
  199.0 16.3 %feed_forward.7 = (bf16[512,896]{1,0:T(8,128)(2,1)}, bf16[512,896]{1,0:T(8,128)(2,1)}, bf16[4096,896]{1,0:T(8,128)(2,1)}, bf16[4096,640]{1,0:T(8,128)(2,1)}, bf1...) custom-call(s32[4]{0:T(128)} %pad_add_fusion.device.meta.where, ...), custom_call_target="tpu_custom_call", output_to_operand_aliasing={{2}: (6, {}), {3}: (7, {}), {4}: (8, {}), {5}: (9, {})} | custom-call | flops 15000000512 | bytes 1000000 | tf_op jit(solution)/shard_map/feed_forward/pallas_call | solution.py:406
  217.9 11.1 %weight_gradient.3 = (bf16[160,896]{1,0:T(8,128)(2,1)}, bf16[160,896]{1,0:T(8,128)(2,1)}, bf16[160,896]{1,0:T(8,128)(2,1)}, bf16[160,896]{1,0:T(8,128)(2,1)}) custom-call(s32[4]{0:T(128)} %pad_add_fusion.device.meta.where, bf16[4096,640]{1,0:T(8,128)(2,1)} %get-tuple-element.215.x_ref, bf16[4096,896]{1,0:T(8,128)(2,1)} %all-gather.5.cloned.1.call-done.cot_ref.y_ref), custom_call_target="tpu_custom_call" | custom-call | flops 200000000 | bytes 1000000 | tf_op jit(solution)/shard_map/weight_gradient/pallas_call | solution.py:470
  236.1 4.3 %collective-permute-start.33 = (bf16[160,896]{1,0:T(8,128)(2,1)}, bf16[160,896]{1,0:T(8,128)(2,1)}, u32[]{:S(2)}, u32[]{:S(2)}) collective-permute-start(bf16[160,896]{1,0:T(8,128)(2,1)} %get-tuple-element.219), channel_id=1, source_target_pairs={{1,0},{2,1},{3,2},{0,3},{5,4},{6,5},{7,6},{4,7},{9,8},{10,9},{11,1... | collective-permute-start | bytes 860168 | tf_op jit(solution)/shard_map/ppermute | solution.py:960
  240.5 16.9 %weight_gradient.4 = (bf16[256,1280]{1,0:T(8,128)(2,1)}, bf16[256,1280]{1,0:T(8,128)(2,1)}, bf16[256,1280]{1,0:T(8,128)(2,1)}, bf16[256,1280]{1,0:T(8,128)(2,1)}) custom-call(s32[4]{0:T(128)} %pad_add_fusion.device.meta.where, bf16[4096,896]{1,0:T(8,128)(2,1)} %get-tuple-element.232.x_ref, bf16[4096,1280]{1,0:T(8,128)(2,1)} %get-tuple-element.233.y_ref), custom_call_target="tpu_custom_call" | custom-call | flops 200000000 | bytes 1000000 | tf_op jit(solution)/shard_map/weight_gradient/pallas_call | solution.py:470
  265.7 10.8 %feed_back.1 = (f32[512,896]{1,0:T(8,128)}, bf16[512,896]{1,0:T(8,128)(2,1)}, f32[1,896]{1,0:T(1,128)}, bf16[4,4,32,1792]{3,2,1,0:T(8,128)(2,1)}, bf16[4,4,32,1792]{3,2,1,0:T(8,128)(2,1)}) custom-call(s32[4]{0:T(128)} %pad_add_fusion.device.meta.where, bf16[512,896]{1,0:T(8,128)(2,1)} %get-tuple-element.235.a_ref, bf16[512,896]{1,0:T(8,128)(2,1)} %copy-done.21, ...), custom_call_target="tpu_custom_call" | custom-call | flops 1000000000 | bytes 1000000 | tf_op jit(solution)/shard_map/feed_back/pallas_call | solution.py:544
  277.7 14.9 %attention_backward.1 = (bf16[512,896]{1,0:T(8,128)(2,1)S(1)}, f32[512,256]{1,0:T(8,128)S(1)}, bf16[512,256]{1,0:T(8,128)(2,1)S(1)}, bf16[512,256]{1,0:T(8,128)(2,1)S(1)}, bf16[512,256]{1,0:T(8,128)(2,1)S(1)}) custom-call(s32[4]{0:T(128)S(1)} %copy-done.6, bf16[512,896]{1,0:T(8,128)(2,1)S(1)} %get-tuple-element.184.q_ref, bf16[512,896]{1,0:T(8,128)(2,1)S(1)} %copy-done.7, ...), custom_call_target="tpu_custom_call" | custom-call | flops 40000000000 | bytes 1000000 | tf_op jit(solution)/shard_map/attention_backward/pallas_call | solution.py:330
  294.3 5.0 %weight_gradient.5 = (bf16[4,4,32,1792]{3,2,1,0:T(8,128)(2,1)}, bf16[4,4,32,1792]{3,2,1,0:T(8,128)(2,1)}) custom-call(s32[4]{0:T(128)} %pad_add_fusion.device.meta.where, bf16[512,896]{1,0:T(8,128)(2,1)} %get-tuple-element.177.normed_ref.x_ref, bf16[512,896]{1,0:T(8,128)(2,1)} %copy-done, ...), custom_call_target="tpu_custom_call", output_to_operand_aliasing={{0}: (3, {}), {1}: (4, {})} | custom-call | flops 200000000 | bytes 1000000 | tf_op jit(solution)/shard_map/weight_gradient/pallas_call | solution.py:470
  299.3 26.5 %collective-permute-done.36.refs_2_ = bf16[256,1280]{1,0:T(8,128)(2,1)} collective-permute-done((bf16[256,1280]{1,0:T(8,128)(2,1)}, bf16[256,1280]{1,0:T(8,128)(2,1)}, u32[]{:S(2)}, u32[]{:S(2)}) %collective-permute-start.36) | collective-permute-done | bytes 655392 | tf_op jit(solution)/shard_map/ppermute | solution.py:960
  346.7 8.5 %collective-permute-done.44.refs_2_ = bf16[512,256]{1,0:T(8,128)(2,1)S(1)} collective-permute-done((bf16[512,256]{1,0:T(8,128)(2,1)S(1)}, bf16[512,256]{1,0:T(8,128)(2,1)S(1)}, u32[]{:S(2)}, u32[]{:S(2)}) %collective-permute-start.44) | collective-permute-done | bytes 262176 | tf_op jit(solution)/shard_map/ppermute | solution.py:966
  355.9 7.8 %finish_keyval.1 = (bf16[4,4,32,256]{3,2,1,0:T(8,128)(2,1)}, bf16[4,4,32,256]{3,2,1,0:T(8,128)(2,1)}, bf16[512,896]{1,0:T(8,128)(2,1)}) custom-call(s32[4]{0:T(128)} %pad_add_fusion.device.meta.where, bf16[512,896]{1,0:T(8,128)(2,1)} %get-tuple-element.177.normed_ref.x_ref, f32[512,896]{1,0:T(8,128)} %get-tuple-element.265.scaled_ref, ...), custom_call_target="tpu_custom_call" | custom-call | flops 20000000000 | bytes 1000000 | tf_op jit(solution)/shard_map/finish_keyval/pallas_call | solution.py:630
  363.7 5.1 %update_columns.1 = (f32[28,9728]{1,0:T(8,128)}, f32[28,9728]{1,0:T(8,128)}, f32[28,9728]{1,0:T(8,128)}) custom-call(bf16[8,32,1280]{2,1,0:T(8,128)(2,1)} %all-to-all-done.1.g_ref, f32[28,9728]{1,0:T(8,128)} %m_ref.1, f32[28,9728]{1,0:T(8,128)} %v_ref.1, f32[28,9728]{1,0:T(8,128)} %w_ref.3), custom_call_target="tpu_custom_call" | custom-call | flops 1000000000 | bytes 1000000 | tf_op jit(solution)/shard_map/update_columns/pallas_call | solution.py:939
  381.1 5.1 %collective-permute-start.50 = (bf16[32,2048]{1,0:T(8,128)(2,1)S(1)}, bf16[32,2048]{1,0:T(8,128)(2,1)S(1)}, u32[]{:S(2)}, u32[]{:S(2)}) collective-permute-start(bf16[32,2048]{1,0:T(8,128)(2,1)S(1)} %get-tuple-element.333), channel_id=1, source_target_pairs={{1,0},{2,1},{3,2},{0,3},{5,4},{6,5},{7,6},{4,7},{9,8},{10,9},{11,1... | collective-permute-start | bytes 393224 | tf_op jit(solution)/shard_map/ppermute | solution.py:960
  (284 shorter events, 131.3 us)
Async XLA Ops:
  7.2 59.3 %all-gather.3.cloned.1.call-start = ((), (), s32[]{:S(2)}) async-start(), calls=%async_computation.3 | async-start | bytes 1361920 | tf_op jit(solution)/shard_map/all_gather | solution.py:1066
  42.1 21.9 %collective-permute-start.8 = (bf16[128,1792]{1,0:T(8,128)(2,1)S(1)}, bf16[128,1792]{1,0:T(8,128)(2,1)S(1)}, u32[]{:S(2)}, u32[]{:S(2)}) collective-permute-start(bf16[128,1792]{1,0:T(8,128)(2,1)S(1)} %slice.146), channel_id=1, source_target_pairs={{0,16},{4,20},{8,24},{12,28},{16,0},{20,4},{24,8},{28,12},{1,17},{... | collective-permute-start | bytes 1376264 | tf_op jit(solution)/shard_map/ppermute | solution.py:955
  42.6 22.3 %collective-permute-start.7 = (bf16[128,1792]{1,0:T(8,128)(2,1)S(1)}, bf16[128,1792]{1,0:T(8,128)(2,1)}, u32[]{:S(2)}, u32[]{:S(2)}) collective-permute-start(bf16[128,1792]{1,0:T(8,128)(2,1)S(1)} %slice.146), channel_id=1, source_target_pairs={{0,8},{4,12},{8,0},{12,4},{16,24},{20,28},{24,16},{28,20},{1,9},{5... | collective-permute-start | bytes 1376264 | tf_op jit(solution)/shard_map/ppermute | solution.py:955
  44.1 22.4 %collective-permute-start.10 = (bf16[512,256]{1,0:T(8,128)(2,1)}, bf16[512,256]{1,0:T(8,128)(2,1)S(1)}, u32[]{:S(2)}, u32[]{:S(2)}) collective-permute-start(bf16[512,256]{1,0:T(8,128)(2,1)} %get-tuple-element.180.refs_0_), channel_id=1, source_target_pairs={{0,1},{1,2},{2,3},{4,5},{5,6},{6,7},{8,9},{9,10},{10,11},{12,13},{... | collective-permute-start | bytes 786440 | tf_op jit(solution)/shard_map/ppermute | solution.py:966
  54.1 86.0 %all-gather.5.cloned.1.call-start = ((), (), s32[]{:S(2)}) async-start(), calls=%async_computation.4 | async-start | bytes 8257536 | tf_op jit(solution)/shard_map/all_gather | solution.py:1089
  71.0 255.5 %reduce-scatter.2.cloned.1.call-start = ((), (), s32[]{:S(2)}) async-start(), calls=%async_computation.5 | async-start | bytes 8257536 | tf_op jit(solution)/shard_map/reduce_scatter | solution.py:1154
  71.7 36.2 %collective-permute-start.14 = (bf16[256,1280]{1,0:T(8,128)(2,1)S(1)}, bf16[256,1280]{1,0:T(8,128)(2,1)S(1)}, u32[]{:S(2)}, u32[]{:S(2)}) collective-permute-start(bf16[256,1280]{1,0:T(8,128)(2,1)S(1)} %bitcast.64), channel_id=1, source_target_pairs={{1,0},{2,1},{3,2},{0,3},{5,4},{6,5},{7,6},{4,7},{9,8},{10,9},{11,1... | collective-permute-start | bytes 1966088 | tf_op jit(solution)/shard_map/ppermute | solution.py:960
  77.2 56.0 %collective-permute-start.15 = (bf16[256,1280]{1,0:T(8,128)(2,1)S(1)}, bf16[256,1280]{1,0:T(8,128)(2,1)S(1)}, u32[]{:S(2)}, u32[]{:S(2)}) collective-permute-start(bf16[256,1280]{1,0:T(8,128)(2,1)S(1)} %bitcast.65), channel_id=1, source_target_pairs={{2,0},{3,1},{0,2},{1,3},{6,4},{7,5},{4,6},{5,7},{10,8},{11,9},{8,1... | collective-permute-start | bytes 1966088 | tf_op jit(solution)/shard_map/ppermute | solution.py:960
  77.2 56.0 %collective-permute-start.16 = (bf16[256,1280]{1,0:T(8,128)(2,1)S(1)}, bf16[256,1280]{1,0:T(8,128)(2,1)S(1)}, u32[]{:S(2)}, u32[]{:S(2)}) collective-permute-start(bf16[256,1280]{1,0:T(8,128)(2,1)S(1)} %bitcast.66), channel_id=1, source_target_pairs={{3,0},{0,1},{1,2},{2,3},{7,4},{4,5},{5,6},{6,7},{11,8},{8,9},{9,10... | collective-permute-start | bytes 1966088 | tf_op jit(solution)/shard_map/ppermute | solution.py:960
  133.2 23.5 %collective-permute-start.19 = (bf16[512,896]{1,0:T(8,128)(2,1)}, bf16[512,896]{1,0:T(8,128)(2,1)}, u32[]{:S(2)}, u32[]{:S(2)}) collective-permute-start(bf16[512,896]{1,0:T(8,128)(2,1)} %get-tuple-element.188.n_a), channel_id=1, source_target_pairs={{0,8},{4,12},{8,0},{12,4},{16,24},{20,28},{24,16},{28,20},{1,9},{5... | collective-permute-start | bytes 2752520 | tf_op jit(solution)/shard_map/ppermute | solution.py:955
  134.7 22.6 %collective-permute-start.20 = (bf16[512,896]{1,0:T(8,128)(2,1)}, bf16[512,896]{1,0:T(8,128)(2,1)S(1)}, u32[]{:S(2)}, u32[]{:S(2)}) collective-permute-start(bf16[512,896]{1,0:T(8,128)(2,1)} %get-tuple-element.188.n_a), channel_id=1, source_target_pairs={{0,16},{4,20},{8,24},{12,28},{16,0},{20,4},{24,8},{28,12},{1,17},{... | collective-permute-start | bytes 2752520 | tf_op jit(solution)/shard_map/ppermute | solution.py:955
  179.6 49.5 %collective-permute-start.29 = (bf16[512,896]{1,0:T(8,128)(2,1)S(1)}, bf16[512,896]{1,0:T(8,128)(2,1)S(1)}, u32[]{:S(2)}, u32[]{:S(2)}) collective-permute-start(bf16[512,896]{1,0:T(8,128)(2,1)S(1)} %copy-done.53), channel_id=1, source_target_pairs={{0,4},{4,0},{8,12},{12,8},{16,20},{20,16},{24,28},{28,24},{1,5},{5... | collective-permute-start | bytes 2752520 | tf_op jit(solution)/shard_map/ppermute | solution.py:955
  217.9 39.5 %collective-permute-start.18 = (bf16[512,896]{1,0:T(8,128)(2,1)}, bf16[512,896]{1,0:T(8,128)(2,1)S(1)}, u32[]{:S(2)}, u32[]{:S(2)}) collective-permute-start(bf16[512,896]{1,0:T(8,128)(2,1)} %get-tuple-element.196), channel_id=1, source_target_pairs={{0,4},{4,0},{8,12},{12,8},{16,20},{20,16},{24,28},{28,24},{1,5},{5... | collective-permute-start | bytes 2752520 | tf_op jit(solution)/shard_map/ppermute | solution.py:955
  234.0 24.9 %collective-permute-start.31 = (bf16[512,896]{1,0:T(8,128)(2,1)}, bf16[512,896]{1,0:T(8,128)(2,1)}, u32[]{:S(2)}, u32[]{:S(2)}) collective-permute-start(bf16[512,896]{1,0:T(8,128)(2,1)} %get-tuple-element.226), channel_id=1, source_target_pairs={{0,8},{4,12},{8,0},{12,4},{16,24},{20,28},{24,16},{28,20},{1,9},{5... | collective-permute-start | bytes 2752520 | tf_op jit(solution)/shard_map/ppermute | solution.py:955
  235.2 23.8 %collective-permute-start.32 = (bf16[512,896]{1,0:T(8,128)(2,1)}, bf16[512,896]{1,0:T(8,128)(2,1)}, u32[]{:S(2)}, u32[]{:S(2)}) collective-permute-start(bf16[512,896]{1,0:T(8,128)(2,1)} %get-tuple-element.231), channel_id=1, source_target_pairs={{0,16},{4,20},{8,24},{12,28},{16,0},{20,4},{24,8},{28,12},{1,17},{... | collective-permute-start | bytes 2752520 | tf_op jit(solution)/shard_map/ppermute | solution.py:955
  259.3 40.0 %collective-permute-start.38 = (bf16[160,896]{1,0:T(8,128)(2,1)}, bf16[160,896]{1,0:T(8,128)(2,1)}, u32[]{:S(2)}, u32[]{:S(2)}) collective-permute-start(bf16[160,896]{1,0:T(8,128)(2,1)} %get-tuple-element.217), channel_id=1, source_target_pairs={{3,0},{0,1},{1,2},{2,3},{7,4},{4,5},{5,6},{6,7},{11,8},{8,9},{9,10... | collective-permute-start | bytes 860168 | tf_op jit(solution)/shard_map/ppermute | solution.py:960
  260.3 39.0 %collective-permute-start.35 = (bf16[256,1280]{1,0:T(8,128)(2,1)}, bf16[256,1280]{1,0:T(8,128)(2,1)}, u32[]{:S(2)}, u32[]{:S(2)}) collective-permute-start(bf16[256,1280]{1,0:T(8,128)(2,1)} %get-tuple-element.255), channel_id=1, source_target_pairs={{1,0},{2,1},{3,2},{0,3},{5,4},{6,5},{7,6},{4,7},{9,8},{10,9},{11,1... | collective-permute-start | bytes 1966088 | tf_op jit(solution)/shard_map/ppermute | solution.py:960
  263.2 62.6 %collective-permute-start.36 = (bf16[256,1280]{1,0:T(8,128)(2,1)}, bf16[256,1280]{1,0:T(8,128)(2,1)}, u32[]{:S(2)}, u32[]{:S(2)}) collective-permute-start(bf16[256,1280]{1,0:T(8,128)(2,1)} %get-tuple-element.256), channel_id=1, source_target_pairs={{2,0},{3,1},{0,2},{1,3},{6,4},{7,5},{4,6},{5,7},{10,8},{11,9},{8,1... | collective-permute-start | bytes 1966088 | tf_op jit(solution)/shard_map/ppermute | solution.py:960
  263.7 62.1 %collective-permute-start.37 = (bf16[256,1280]{1,0:T(8,128)(2,1)}, bf16[256,1280]{1,0:T(8,128)(2,1)}, u32[]{:S(2)}, u32[]{:S(2)}) collective-permute-start(bf16[256,1280]{1,0:T(8,128)(2,1)} %get-tuple-element.257), channel_id=1, source_target_pairs={{3,0},{0,1},{1,2},{2,3},{7,4},{4,5},{5,6},{6,7},{11,8},{8,9},{9,10... | collective-permute-start | bytes 1966088 | tf_op jit(solution)/shard_map/ppermute | solution.py:960
  328.1 27.1 %collective-permute-start.44 = (bf16[512,256]{1,0:T(8,128)(2,1)S(1)}, bf16[512,256]{1,0:T(8,128)(2,1)S(1)}, u32[]{:S(2)}, u32[]{:S(2)}) collective-permute-start(bf16[512,256]{1,0:T(8,128)(2,1)S(1)} %get-tuple-element.273), channel_id=1, source_target_pairs={{2,0},{3,1},{6,4},{7,5},{10,8},{11,9},{14,12},{15,13},{18,16},{19,... | collective-permute-start | bytes 786440 | tf_op jit(solution)/shard_map/ppermute | solution.py:966
  329.4 25.8 %collective-permute-start.45 = (bf16[512,256]{1,0:T(8,128)(2,1)S(1)}, bf16[512,256]{1,0:T(8,128)(2,1)}, u32[]{:S(2)}, u32[]{:S(2)}) collective-permute-start(bf16[512,256]{1,0:T(8,128)(2,1)S(1)} %get-tuple-element.274), channel_id=1, source_target_pairs={{3,0},{7,4},{11,8},{15,12},{19,16},{23,20},{27,24},{31,28}} | collective-permute-start | bytes 786440 | tf_op jit(solution)/shard_map/ppermute | solution.py:966
  343.2 25.6 %collective-permute-start.42 = (bf16[4,32,1792]{2,1,0:T(8,128)(2,1)}, bf16[4,32,1792]{2,1,0:T(8,128)(2,1)S(1)}, u32[]{:S(2)}, u32[]{:S(2)}) collective-permute-start(bf16[4,32,1792]{2,1,0:T(8,128)(2,1)} %get-tuple-element.327), channel_id=1, source_target_pairs={{0,24},{4,28},{8,16},{12,20},{16,8},{20,12},{24,0},{28,4},{1,25},{... | collective-permute-start | bytes 1376264 | tf_op jit(solution)/shard_map/ppermute | solution.py:955
  346.0 22.8 %collective-permute-start.41 = (bf16[4,32,1792]{2,1,0:T(8,128)(2,1)S(1)}, bf16[4,32,1792]{2,1,0:T(8,128)(2,1)S(1)}, u32[]{:S(2)}, u32[]{:S(2)}) collective-permute-start(bf16[4,32,1792]{2,1,0:T(8,128)(2,1)S(1)} %get-tuple-element.328), channel_id=1, source_target_pairs={{0,16},{4,20},{8,24},{12,28},{16,0},{20,4},{24,8},{28,12},{1,17},{... | collective-permute-start | bytes 1376264 | tf_op jit(solution)/shard_map/ppermute | solution.py:955
  346.6 22.3 %collective-permute-start.40 = (bf16[4,32,1792]{2,1,0:T(8,128)(2,1)S(1)}, bf16[4,32,1792]{2,1,0:T(8,128)(2,1)S(1)}, u32[]{:S(2)}, u32[]{:S(2)}) collective-permute-start(bf16[4,32,1792]{2,1,0:T(8,128)(2,1)S(1)} %get-tuple-element.326), channel_id=1, source_target_pairs={{0,8},{4,12},{8,0},{12,4},{16,24},{20,28},{24,16},{28,20},{1,9},{5... | collective-permute-start | bytes 1376264 | tf_op jit(solution)/shard_map/ppermute | solution.py:955
  (94 other events, 814.3 us)
Sparse Core Ops, SparseCore 0:
  16.0 29.0 all-gather.2
  71.1 52.1 all-gather.4
  259.1 67.3 reduce-scatter.1

commit v5 on v4

--- a/solution.py
+++ b/solution.py
@@ -113,19 +113,21 @@
         mask = mask_of(
             start_of(sel), first_query + block * half, first_query + sel * half, half, sel == block
         )
-        visit(sel, 0, block, mask)
+        visit(sel, 0, block, 1, mask)
     for piece in range(1, pieces):
         first_key = (mine - piece) * 2 * half
 
         def region(cut):
-            for block in range(2):
-                for sel in range(2):
-                    if cut and block == 0:
-                        mask = mask_of(start_of(sel), first_key, first_query, half, False)
-                    else:
-                        mask = start_of(sel) <= first_key + block * half
-                        mask = jnp.concatenate([mask, mask], axis=0 if turned else 1)
-                    visit(sel, piece, block, mask)
+            axis = 0 if turned else 1
+            for sel in range(2):
+                if cut:
+                    mask = mask_of(start_of(sel), first_key, first_query, half, False)
+                    visit(sel, piece, 0, 1, mask)
+                    mask = start_of(sel) <= first_key + half
+                    visit(sel, piece, 1, 1, jnp.concatenate([mask, mask], axis=axis))
+                else:
+                    mask = start_of(sel) <= first_key
+                    visit(sel, piece, 0, 2, jnp.concatenate([mask, mask], axis=axis))
 
         pl.when(mine == piece)(functools.partial(region, True))
         pl.when(mine > piece)(functools.partial(region, False))
@@ -151,30 +153,30 @@
     sum_ref[...] = jnp.zeros_like(sum_ref)
     acc_ref[...] = jnp.zeros_like(acc_ref)
 
-    def scores_of(sel, piece, block):
-        part = slice(block * half, (block + 1) * half)
+    def scores_of(sel, piece, block, count):
+        part = slice(block * half, (block + count) * half)
         return lax.dot_general(
             two_ref[sel], kv_refs[piece][part, :LANES], NT, preferred_element_type=wide
         )
 
-    def find_top(sel, piece, block, mask):
-        scores = scores_of(sel, piece, block)
+    def find_top(sel, piece, block, count, mask):
+        scores = scores_of(sel, piece, block, count)
         if mask.shape[1] > LANES:
             scores = jnp.where(mask, scores, masked_score)
-        peak = functools.reduce(jnp.maximum, [scores[:, i : i + LANES] for i in range(0, half, LANES)])
+        peak = functools.reduce(jnp.maximum, [scores[:, i : i + LANES] for i in range(0, count * half, LANES)])
         if mask.shape[1] <= LANES:
             peak = jnp.where(mask, peak, masked_score)
         top_ref[sel] = jnp.maximum(top_ref[sel], peak)
 
-    def sum_up(sel, piece, block, mask):
-        part = slice(block * half, (block + 1) * half)
-        scores = scores_of(sel, piece, block)
+    def sum_up(sel, piece, block, count, mask):
+        part = slice(block * half, (block + count) * half)
+        scores = scores_of(sel, piece, block, count)
         level = top_ref[sel]
         if mask.shape[1] > LANES:
             scores = jnp.where(mask, scores, masked_score)
         else:
             level = jnp.where(mask, level, -masked_score)
-        weights = [jnp.exp(scores[:, i : i + LANES] - level) for i in range(0, half, LANES)]
+        weights = [jnp.exp(scores[:, i : i + LANES] - level) for i in range(0, count * half, LANES)]
         sum_ref[sel] += functools.reduce(jnp.add, weights)
         acc_ref[sel] += jnp.dot(
             jnp.concatenate(weights, axis=1).astype(low),
@@ -272,8 +274,8 @@
             axis=1,
         )
 
-    def visit(sel, piece, block, mask):
-        part = slice(block * half, (block + 1) * half)
+    def visit(sel, piece, block, count, mask):
+        part = slice(block * half, (block + count) * half)
         two, dot = two_ref[sel], dot_ref[sel]
         keys, values = kv_refs[piece][part, :LANES], kv_refs[piece][part, LANES:]
         scores = lax.dot_general(keys, two, NT, preferred_element_type=wide)
@@ -701,7 +703,7 @@
     place_rows(*sizes, device, own_ref, other_ref, at_ref, acc_ref)
     o_ref[...] = acc_ref[: o_ref.shape[0]].astype(low)
     pre_ref[...] = (
-        jnp.dot(normed_ref[...], o_ref[...], preferred_element_type=wide) + bias_ref[...]
+        jnp.dot(normed_ref[...], o_ref[...], preferred_element_type=wide) + bias_ref[0:1]
     )
 
 
@@ -848,9 +850,23 @@
         out_specs=pl.BlockSpec((rows, block.shape[1]), lambda i: (0, 0)),
         out_shape=jax.ShapeDtypeStruct((rows, block.shape[1]), block.dtype),
         compiler_params=params(),
-        cost_estimate=cost(20),
+        cost_estimate=cost(0.1),
         name="fill_rows",
     )(block)
+
+
+def widen_kernel(x_ref, o_ref):
+    o_ref[...] = jnp.broadcast_to(x_ref[...], o_ref.shape)
+
+
+def widen(row, rows):
+    return pl.pallas_call(
+        widen_kernel,
+        out_shape=jax.ShapeDtypeStruct((rows, row.shape[1]), row.dtype),
+        compiler_params=pltpu.CompilerParams(vmem_limit_bytes=MIB),
+        cost_estimate=cost(20),
+        name="widen",
+    )(row)
 
 
 def stack_kernel(outer, count, take, give, meta, *refs):
@@ -983,8 +999,15 @@
     return functools.reduce(jnp.add, [term.astype(wide) for term in terms])
 
 
-def gather_chips(column):
-    evens = [column] + [flip(column, r) for r in range(2, lax.axis_size("dp"), 2)]
+def gather_chips(column, forward=None):
+    n_dp = lax.axis_size("dp")
+    if forward is not None and n_dp == 8:
+        half = column.shape[0] // 2
+        x_side, y_side = flip(column, 2), flip(column, 4)
+        x_side, y_side = after((x_side, y_side), forward)
+        across = [flip(x_side[:half], 4), flip(y_side[half:], 2)]
+        return jnp.concatenate([column, x_side, y_side, *across], axis=0)
+    evens = [column] + [flip(column, r) for r in range(2, n_dp, 2)]
     return jnp.concatenate(evens, axis=0)
 
 
@@ -1080,12 +1103,13 @@
     gain_one, gain_two = small_row[:, :D], small_row[:, D : 2 * D]
     bias_query = small_row[:, 2 * D : 2 * D + query_width]
     keyval_parts = [keyval_low] + [shift_within(keyval_low, -s) for s in range(1, group_size)]
-    both_own = gather_chips(after(both_column, keyval_low))
+    both_own = gather_chips(after(both_column, keyval_low), down_part)
     gateup_column = lax.all_to_all(after(gateup_pieces, keyval_low), "dp", 0, 0, tiled=True)
     gateup_column = gateup_column.reshape(n_dp * in_give, 2 * part_wide)
-    keyval_parts, down_part = after((keyval_parts, down_part))
     down_part = fill_rows(down_part, part_wide)
-    both_own, gateup_column, down_part = after((both_own, gateup_column, down_part))
+    keyval_parts, down_part, bias_query = after((keyval_parts, down_part, bias_query))
+    bias_query = widen(bias_query, 8)
+    both_own, gateup_column, bias_query = after((both_own, gateup_column, bias_query))
     cot_all = lax.all_gather(after(cotangent, both_own), "dp", axis=0, tiled=True)
     both_other = flip(both_own, 1)
     query_full, query_pre = assembled(

time: 414 us -> 415 us (level)
  local copies, waits for them, and re-layouts: 15.5 us -> 21 us
    unnamed x124 -> x128, local copies, waits for them, and re-layouts: 11.6 us -> 14.3 us
    ppermute x32 -> x33, waiting for transfers between devices: 18.3 us -> 16.6 us  [flip(): return lax.ppermute(value, 'dp', [(i, i ^ mask) for i in range(count)])]
    ppermute x32 -> x33, starting transfers between devices: 24 us -> 25.6 us  [flip(): return lax.ppermute(value, 'dp', [(i, i ^ mask) for i in range(count)])]
  transfers between devices with their start and end apart: 58 -> 59, of which waited for: 21 -> 17; matrix products, arithmetic and copies ran while one was open for 5% -> 6% of each run, Pallas kernels for 46% -> 46%
where the time goes in v5:
time: 415 us; the launch traced here: 408 us
  Pallas kernels  188 us (45%)
  waiting for transfers between devices  88.2 us (21%)
  starting transfers between devices  73.7 us (18%)
  other arithmetic  21.8 us (5%)
  local copies, waits for them, and re-layouts  21 us (5%)
  between operations  15.2 us (4%)
    pallas_call x4, Pallas kernels, feed_forward(): pl.pallas_call(functools.partial(feed_kernel, steps, fresh), grid_spec=sp...  64.9 us
    ppermute x15, waiting for transfers between devices, shift(): lax.ppermute(value, 'group', [((i + step) % count, i) for i in range(coun...  64 us
    pallas_call x3, Pallas kernels, weight_gradient(): pl.pallas_call(functools.partial(weight_kernel, steps, shape, take, give,...  33.1 us
    ppermute x15, starting transfers between devices, shift(): lax.ppermute(value, 'group', [((i + step) % count, i) for i in range(coun...  28.2 us
    ppermute x33, starting transfers between devices, flip(): return lax.ppermute(value, 'dp', [(i, i ^ mask) for i in range(count)])  25.6 us
    pallas_call x3, Pallas kernels, assembled(): pl.pallas_call(functools.partial(kernel, (n_dp, n_group, take, give)), gr...  17.6 us
    ppermute x33, waiting for transfers between devices, flip(): return lax.ppermute(value, 'dp', [(i, i ^ mask) for i in range(count)])  16.6 us
    pallas_call x1, Pallas kernels, attention_forward(): pl.pallas_call(functools.partial(forward_kernel, pieces), grid_spec=spec,...  16.4 us
  transfers between devices with their start and end apart: 59, of which 17 were waited for; matrix products, arithmetic and copies ran while one was open for 6% of the time, Pallas kernels for 46%

profile of v5, /device:TPU:0, one launch (start us, length us, event | category | flops | bytes accessed | tf_op | source)
XLA Modules:
  0.0 407.9 jit_solution(17147346475210268503)
XLA Ops:
  9.0 5.0 %collective-permute-start = (bf16[32,2048]{1,0:T(8,128)(2,1)}, bf16[32,2048]{1,0:T(8,128)(2,1)S(1)}, u32[]{:S(2)}, u32[]{:S(2)}) collective-permute-start(bf16[32,2048]{1,0:T(8,128)(2,1)} %pack_rows.1), channel_id=1, source_target_pairs={{1,0},{2,1},{3,2},{0,3},{5,4},{6,5},{7,6},{4,7},{9,8},{10,9},{11,1... | collective-permute-start | bytes 393224 | tf_op jit(solution)/shard_map/ppermute | solution.py:976
  35.2 5.4 %project_keyval.1 = (bf16[896,256]{1,0:T(8,128)(2,1)}, f32[1,2944]{1,0:T(1,128)}, f32[1,2944]{1,0:T(1,128)}, f32[512,1]{1,0:T(8,128)}, f32[512,896]{1,0:T(8,128)...) custom-call(s32[4]{0:T(128)} %pad_add_fusion.device.meta.where, bf16[512,256]{1,0:T(8,128)(2,1)} %copy-done.18, ...), custom_call_target="tpu_custom_call" | custom-call | flops 100000000 | bytes 1000000 | tf_op jit(solution)/shard_map/project_keyval/pallas_call | solution.py:735
  70.0 4.9 %collective-permute-start.15 = (bf16[256,1280]{1,0:T(8,128)(2,1)}, bf16[256,1280]{1,0:T(8,128)(2,1)S(1)}, u32[]{:S(2)}, u32[]{:S(2)}) collective-permute-start(bf16[256,1280]{1,0:T(8,128)(2,1)} %bitcast.7.refs_0_), channel_id=1, source_target_pairs={{1,0},{2,1},{3,2},{0,3},{5,4},{6,5},{7,6},{4,7},{9,8},{10,9},{11,1... | collective-permute-start | bytes 1966088 | tf_op jit(solution)/shard_map/ppermute | solution.py:976
  75.6 5.7 %project_query.1 = (bf16[896,896]{1,0:T(8,128)(2,1)}, f32[512,896]{1,0:T(8,128)}) custom-call(s32[4]{0:T(128)} %pad_add_fusion.device.meta.where, bf16[512,1792]{1,0:T(8,128)(2,1)} %copy-done.11, bf16[512,1792]{1,0:T(8,128)(2,1)} %collective-permute-done.14.other_ref, bf16[512,896]{1,0:T(8,128)(2,1)} %get-tuple-element.183.normed_ref.x_ref, f32[8,896]{1,0:T(8,128)} %copy-done.7), custom_call_target="tpu_custom_call" | custom-call | flops 100000000 | bytes 1000000 | tf_op jit(solution)/shard_map/project_query/pallas_call | solution.py:735
  81.5 16.4 %attention_forward.1 = (f32[512,896]{1,0:T(8,128)S(1)}, f32[7,8,1024]{2,1,0:T(8,128)S(1)}, bf16[512,896]{1,0:T(8,128)(2,1)S(1)}) custom-call(s32[4]{0:T(128)S(1)} %copy-done.5, f32[512,896]{1,0:T(8,128)} %get-tuple-element.185.pre_ref, f32[512,128]{1,0:T(8,128)S(1)} %copy-done.3, f32[512,128]{1,0:T(8,128)S(1)} %copy-done.4, ...), custom_call_target="tpu_custom_call" | custom-call | flops 40000000000 | bytes 1000000 | tf_op jit(solution)/shard_map/attention_forward/pallas_call | solution.py:229
  99.1 6.5 %attention_output.1 = (bf16[896,896]{1,0:T(8,128)(2,1)}, bf16[512,896]{1,0:T(8,128)(2,1)}, f32[512,896]{1,0:T(8,128)}, f32[512,1]{1,0:T(8,128)}, bf16[512,896]{1,0:T(8,128)(2,1)}) custom-call(s32[4]{0:T(128)} %pad_add_fusion.device.meta.where, bf16[512,1792]{1,0:T(8,128)(2,1)} %copy-done.11, bf16[512,1792]{1,0:T(8,128)(2,1)} %collective-permute-done.14.other_ref, ...), custom_call_target="tpu_custom_call" | custom-call | flops 100000000 | bytes 1000000 | tf_op jit(solution)/shard_map/attention_output/pallas_call | solution.py:735
  105.6 25.5 %collective-permute-done.16.refs_2_ = bf16[256,1280]{1,0:T(8,128)(2,1)S(1)} collective-permute-done((bf16[256,1280]{1,0:T(8,128)(2,1)}, bf16[256,1280]{1,0:T(8,128)(2,1)S(1)}, u32[]{:S(2)}, u32[]{:S(2)}) %collective-permute-start.16) | collective-permute-done | bytes 655392 | tf_op jit(solution)/shard_map/ppermute | solution.py:976
  133.2 4.8 %stack_rows.1.gateup_ref = bf16[896,1280]{1,0:T(8,128)(2,1)} custom-call(s32[4]{0:T(128)} %pad_add_fusion.device.meta.where, bf16[256,1280]{1,0:T(8,128)(2,1)} %bitcast.7.refs_0_, bf16[256,1280]{1,0:T(8,128)(2,1)} %copy-done.23, bf16[256,1280]{1,0:T(8,128)(2,1)} %copy-done.24, bf16[256,1280]{1,0:T(8,128)(2,1)} %copy-done.25), custom_call_target="tpu_custom_call" | custom-call | flops 1000000000 | bytes 1000000 | tf_op jit(solution)/shard_map/stack_rows/pallas_call | solution.py:890
  138.0 16.5 %feed_forward.4 = (bf16[512,896]{1,0:T(8,128)(2,1)}, bf16[512,896]{1,0:T(8,128)(2,1)}, bf16[4096,896]{1,0:T(8,128)(2,1)}, bf16[4096,640]{1,0:T(8,128)(2,1)}, bf1...) custom-call(s32[4]{0:T(128)} %pad_add_fusion.device.meta.where, bf16[512,896]{1,0:T(8,128)(2,1)} %get-tuple-element.194.n_a, ...), custom_call_target="tpu_custom_call" | custom-call | flops 15000000512 | bytes 1000000 | tf_op jit(solution)/shard_map/feed_forward/pallas_call | solution.py:408
  160.5 16.1 %feed_forward.5 = (bf16[512,896]{1,0:T(8,128)(2,1)}, bf16[512,896]{1,0:T(8,128)(2,1)}, bf16[4096,896]{1,0:T(8,128)(2,1)}, bf16[4096,640]{1,0:T(8,128)(2,1)}, bf1...) custom-call(s32[4]{0:T(128)} %pad_add_fusion.device.meta.where, ...), custom_call_target="tpu_custom_call", output_to_operand_aliasing={{2}: (6, {}), {3}: (7, {}), {4}: (8, {}), {5}: (9, {})} | custom-call | flops 15000000512 | bytes 1000000 | tf_op jit(solution)/shard_map/feed_forward/pallas_call | solution.py:408
  180.8 16.1 %feed_forward.6 = (bf16[512,896]{1,0:T(8,128)(2,1)}, bf16[512,896]{1,0:T(8,128)(2,1)}, bf16[4096,896]{1,0:T(8,128)(2,1)}, bf16[4096,640]{1,0:T(8,128)(2,1)}, bf1...) custom-call(s32[4]{0:T(128)} %pad_add_fusion.device.meta.where, ...), custom_call_target="tpu_custom_call", output_to_operand_aliasing={{2}: (6, {}), {3}: (7, {}), {4}: (8, {}), {5}: (9, {})} | custom-call | flops 15000000512 | bytes 1000000 | tf_op jit(solution)/shard_map/feed_forward/pallas_call | solution.py:408
  198.0 16.2 %feed_forward.7 = (bf16[512,896]{1,0:T(8,128)(2,1)}, bf16[512,896]{1,0:T(8,128)(2,1)}, bf16[4096,896]{1,0:T(8,128)(2,1)}, bf16[4096,640]{1,0:T(8,128)(2,1)}, bf1...) custom-call(s32[4]{0:T(128)} %pad_add_fusion.device.meta.where, ...), custom_call_target="tpu_custom_call", output_to_operand_aliasing={{2}: (6, {}), {3}: (7, {}), {4}: (8, {}), {5}: (9, {})} | custom-call | flops 15000000512 | bytes 1000000 | tf_op jit(solution)/shard_map/feed_forward/pallas_call | solution.py:408
  217.1 11.2 %weight_gradient.3 = (bf16[160,896]{1,0:T(8,128)(2,1)}, bf16[160,896]{1,0:T(8,128)(2,1)}, bf16[160,896]{1,0:T(8,128)(2,1)}, bf16[160,896]{1,0:T(8,128)(2,1)}) custom-call(s32[4]{0:T(128)} %pad_add_fusion.device.meta.where, bf16[4096,640]{1,0:T(8,128)(2,1)} %get-tuple-element.221.x_ref, bf16[4096,896]{1,0:T(8,128)(2,1)} %all-gather.5.cloned.1.call-done.cot_ref.y_ref), custom_call_target="tpu_custom_call" | custom-call | flops 200000000 | bytes 1000000 | tf_op jit(solution)/shard_map/weight_gradient/pallas_call | solution.py:472
  238.4 17.0 %weight_gradient.4 = (bf16[256,1280]{1,0:T(8,128)(2,1)}, bf16[256,1280]{1,0:T(8,128)(2,1)}, bf16[256,1280]{1,0:T(8,128)(2,1)}, bf16[256,1280]{1,0:T(8,128)(2,1)}) custom-call(s32[4]{0:T(128)} %pad_add_fusion.device.meta.where, bf16[4096,896]{1,0:T(8,128)(2,1)} %get-tuple-element.238.x_ref, bf16[4096,1280]{1,0:T(8,128)(2,1)} %get-tuple-element.239.y_ref), custom_call_target="tpu_custom_call" | custom-call | flops 200000000 | bytes 1000000 | tf_op jit(solution)/shard_map/weight_gradient/pallas_call | solution.py:472
  265.1 10.7 %feed_back.1 = (f32[512,896]{1,0:T(8,128)}, bf16[512,896]{1,0:T(8,128)(2,1)}, f32[1,896]{1,0:T(1,128)}, bf16[4,4,32,1792]{3,2,1,0:T(8,128)(2,1)}, bf16[4,4,32,1792]{3,2,1,0:T(8,128)(2,1)}) custom-call(s32[4]{0:T(128)} %pad_add_fusion.device.meta.where, bf16[512,896]{1,0:T(8,128)(2,1)} %get-tuple-element.241.a_ref, ...), custom_call_target="tpu_custom_call" | custom-call | flops 1000000000 | bytes 1000000 | tf_op jit(solution)/shard_map/feed_back/pallas_call | solution.py:546
  277.0 14.9 %attention_backward.1 = (bf16[512,896]{1,0:T(8,128)(2,1)S(1)}, f32[512,256]{1,0:T(8,128)S(1)}, bf16[512,256]{1,0:T(8,128)(2,1)S(1)}, bf16[512,256]{1,0:T(8,128)(2,1)S(1)}, bf16[512,256]{1,0:T(8,128)(2,1)S(1)}) custom-call(s32[4]{0:T(128)S(1)} %copy-done.6, bf16[512,896]{1,0:T(8,128)(2,1)S(1)} %get-tuple-element.190.q_ref, bf16[512,896]{1,0:T(8,128)(2,1)S(1)} %copy-done.8, ...), custom_call_target="tpu_custom_call" | custom-call | flops 40000000000 | bytes 1000000 | tf_op jit(solution)/shard_map/attention_backward/pallas_call | solution.py:332
  293.6 5.0 %weight_gradient.5 = (bf16[4,4,32,1792]{3,2,1,0:T(8,128)(2,1)}, bf16[4,4,32,1792]{3,2,1,0:T(8,128)(2,1)}) custom-call(s32[4]{0:T(128)} %pad_add_fusion.device.meta.where, bf16[512,896]{1,0:T(8,128)(2,1)} %get-tuple-element.183.normed_ref.x_ref, bf16[512,896]{1,0:T(8,128)(2,1)} %copy-done, ...), custom_call_target="tpu_custom_call", output_to_operand_aliasing={{0}: (3, {}), {1}: (4, {})} | custom-call | flops 200000000 | bytes 1000000 | tf_op jit(solution)/shard_map/weight_gradient/pallas_call | solution.py:472
  298.6 27.2 %collective-permute-done.37.refs_2_ = bf16[256,1280]{1,0:T(8,128)(2,1)} collective-permute-done((bf16[256,1280]{1,0:T(8,128)(2,1)}, bf16[256,1280]{1,0:T(8,128)(2,1)}, u32[]{:S(2)}, u32[]{:S(2)}) %collective-permute-start.37) | collective-permute-done | bytes 655392 | tf_op jit(solution)/shard_map/ppermute | solution.py:976
  336.9 4.5 %fusion.22 = (bf16[4,4,32,1792]{3,2,1,0:T(8,128)(2,1)S(1)}, f32[4,4,32,1792]{3,2,1,0:T(8,128)}) fusion(bf16[4,4,32,1792]{3,2,1,0:T(8,128)(2,1)} %collective-permute-done.40, bf16[4,4,32,1792]{3,2,1,0:T(8,128)(2,1)} %get-tuple-element.266), kind=kLoop, calls=%fused_computation.85 | loop fusion | flops 3670016 | bytes 9175040 | tf_op jit(solution)/shard_map/convert.8
  346.6 7.4 %collective-permute-done.45.refs_2_ = bf16[512,256]{1,0:T(8,128)(2,1)} collective-permute-done((bf16[512,256]{1,0:T(8,128)(2,1)S(1)}, bf16[512,256]{1,0:T(8,128)(2,1)}, u32[]{:S(2)}, u32[]{:S(2)}) %collective-permute-start.45) | collective-permute-done | bytes 262176 | tf_op jit(solution)/shard_map/ppermute | solution.py:982
  354.1 7.8 %finish_keyval.1 = (bf16[4,4,32,256]{3,2,1,0:T(8,128)(2,1)}, bf16[4,4,32,256]{3,2,1,0:T(8,128)(2,1)}, bf16[512,896]{1,0:T(8,128)(2,1)}) custom-call(s32[4]{0:T(128)} %pad_add_fusion.device.meta.where, bf16[512,896]{1,0:T(8,128)(2,1)} %get-tuple-element.183.normed_ref.x_ref, f32[512,896]{1,0:T(8,128)} %get-tuple-element.271.scaled_ref, ...), custom_call_target="tpu_custom_call" | custom-call | flops 20000000000 | bytes 1000000 | tf_op jit(solution)/shard_map/finish_keyval/pallas_call | solution.py:632
  361.9 5.1 %update_columns.1 = (f32[28,9728]{1,0:T(8,128)}, f32[28,9728]{1,0:T(8,128)}, f32[28,9728]{1,0:T(8,128)}) custom-call(bf16[8,32,1280]{2,1,0:T(8,128)(2,1)} %copy-done.13, f32[28,9728]{1,0:T(8,128)} %m_ref.1, f32[28,9728]{1,0:T(8,128)} %v_ref.1, f32[28,9728]{1,0:T(8,128)} %w_ref.3), custom_call_target="tpu_custom_call" | custom-call | flops 1000000000 | bytes 1000000 | tf_op jit(solution)/shard_map/update_columns/pallas_call | solution.py:955
  379.3 6.5 %collective-permute-start.51 = (bf16[32,2048]{1,0:T(8,128)(2,1)S(1)}, bf16[32,2048]{1,0:T(8,128)(2,1)S(1)}, u32[]{:S(2)}, u32[]{:S(2)}) collective-permute-start(bf16[32,2048]{1,0:T(8,128)(2,1)S(1)} %get-tuple-element.339), channel_id=1, source_target_pairs={{1,0},{2,1},{3,2},{0,3},{5,4},{6,5},{7,6},{4,7},{9,8},{10,9},{11,1... | collective-permute-start | bytes 393224 | tf_op jit(solution)/shard_map/ppermute | solution.py:976
  391.3 4.9 %collective-permute-done.52 = bf16[32,2048]{1,0:T(8,128)(2,1)S(1)} collective-permute-done((bf16[32,2048]{1,0:T(8,128)(2,1)S(1)}, bf16[32,2048]{1,0:T(8,128)(2,1)S(1)}, u32[]{:S(2)}, u32[]{:S(2)}) %collective-permute-start.52) | collective-permute-done | bytes 131104 | tf_op jit(solution)/shard_map/ppermute | solution.py:976
  (293 shorter events, 131.4 us)
Async XLA Ops:
  7.2 48.2 %all-gather.3.cloned.1.call-start = ((), (), s32[]{:S(2)}) async-start(), calls=%async_computation.3 | async-start | bytes 1361920 | tf_op jit(solution)/shard_map/all_gather | solution.py:1089
  42.6 21.5 %collective-permute-start.11 = (bf16[512,256]{1,0:T(8,128)(2,1)}, bf16[512,256]{1,0:T(8,128)(2,1)S(1)}, u32[]{:S(2)}, u32[]{:S(2)}) collective-permute-start(bf16[512,256]{1,0:T(8,128)(2,1)} %get-tuple-element.186.refs_0_), channel_id=1, source_target_pairs={{0,1},{1,2},{2,3},{4,5},{5,6},{6,7},{8,9},{9,10},{10,11},{12,13},{... | collective-permute-start | bytes 786440 | tf_op jit(solution)/shard_map/ppermute | solution.py:982
  54.7 83.3 %all-gather.5.cloned.1.call-start = ((), (), s32[]{:S(2)}) async-start(), calls=%async_computation.4 | async-start | bytes 8257536 | tf_op jit(solution)/shard_map/all_gather | solution.py:1113
  69.8 256.0 %reduce-scatter.2.cloned.1.call-start = ((), (), s32[]{:S(2)}) async-start(), calls=%async_computation.5 | async-start | bytes 8257536 | tf_op jit(solution)/shard_map/reduce_scatter | solution.py:1178
  70.0 35.6 %collective-permute-start.15 = (bf16[256,1280]{1,0:T(8,128)(2,1)}, bf16[256,1280]{1,0:T(8,128)(2,1)S(1)}, u32[]{:S(2)}, u32[]{:S(2)}) collective-permute-start(bf16[256,1280]{1,0:T(8,128)(2,1)} %bitcast.7.refs_0_), channel_id=1, source_target_pairs={{1,0},{2,1},{3,2},{0,3},{5,4},{6,5},{7,6},{4,7},{9,8},{10,9},{11,1... | collective-permute-start | bytes 1966088 | tf_op jit(solution)/shard_map/ppermute | solution.py:976
  74.9 56.2 %collective-permute-start.16 = (bf16[256,1280]{1,0:T(8,128)(2,1)}, bf16[256,1280]{1,0:T(8,128)(2,1)S(1)}, u32[]{:S(2)}, u32[]{:S(2)}) collective-permute-start(bf16[256,1280]{1,0:T(8,128)(2,1)} %bitcast.7.refs_0_), channel_id=1, source_target_pairs={{2,0},{3,1},{0,2},{1,3},{6,4},{7,5},{4,6},{5,7},{10,8},{11,9},{8,1... | collective-permute-start | bytes 1966088 | tf_op jit(solution)/shard_map/ppermute | solution.py:976
  74.9 56.2 %collective-permute-start.17 = (bf16[256,1280]{1,0:T(8,128)(2,1)}, bf16[256,1280]{1,0:T(8,128)(2,1)S(1)}, u32[]{:S(2)}, u32[]{:S(2)}) collective-permute-start(bf16[256,1280]{1,0:T(8,128)(2,1)} %bitcast.7.refs_0_), channel_id=1, source_target_pairs={{3,0},{0,1},{1,2},{2,3},{7,4},{4,5},{5,6},{6,7},{11,8},{8,9},{9,10... | collective-permute-start | bytes 1966088 | tf_op jit(solution)/shard_map/ppermute | solution.py:976
  131.2 23.3 %collective-permute-start.20 = (bf16[512,896]{1,0:T(8,128)(2,1)}, bf16[512,896]{1,0:T(8,128)(2,1)}, u32[]{:S(2)}, u32[]{:S(2)}) collective-permute-start(bf16[512,896]{1,0:T(8,128)(2,1)} %get-tuple-element.194.n_a), channel_id=1, source_target_pairs={{0,8},{4,12},{8,0},{12,4},{16,24},{20,28},{24,16},{28,20},{1,9},{5... | collective-permute-start | bytes 2752520 | tf_op jit(solution)/shard_map/ppermute | solution.py:971
  132.7 22.7 %collective-permute-start.21 = (bf16[512,896]{1,0:T(8,128)(2,1)}, bf16[512,896]{1,0:T(8,128)(2,1)}, u32[]{:S(2)}, u32[]{:S(2)}) collective-permute-start(bf16[512,896]{1,0:T(8,128)(2,1)} %get-tuple-element.194.n_a), channel_id=1, source_target_pairs={{0,16},{4,20},{8,24},{12,28},{16,0},{20,4},{24,8},{28,12},{1,17},{... | collective-permute-start | bytes 2752520 | tf_op jit(solution)/shard_map/ppermute | solution.py:971
  178.1 50.2 %collective-permute-start.30 = (bf16[512,896]{1,0:T(8,128)(2,1)S(1)}, bf16[512,896]{1,0:T(8,128)(2,1)S(1)}, u32[]{:S(2)}, u32[]{:S(2)}) collective-permute-start(bf16[512,896]{1,0:T(8,128)(2,1)S(1)} %copy-done.52), channel_id=1, source_target_pairs={{0,4},{4,0},{8,12},{12,8},{16,20},{20,16},{24,28},{28,24},{1,5},{5... | collective-permute-start | bytes 2752520 | tf_op jit(solution)/shard_map/ppermute | solution.py:971
  217.1 38.3 %collective-permute-start.19 = (bf16[512,896]{1,0:T(8,128)(2,1)}, bf16[512,896]{1,0:T(8,128)(2,1)}, u32[]{:S(2)}, u32[]{:S(2)}) collective-permute-start(bf16[512,896]{1,0:T(8,128)(2,1)} %get-tuple-element.202), channel_id=1, source_target_pairs={{0,4},{4,0},{8,12},{12,8},{16,20},{20,16},{24,28},{28,24},{1,5},{5... | collective-permute-start | bytes 2752520 | tf_op jit(solution)/shard_map/ppermute | solution.py:971
  233.3 24.6 %collective-permute-start.32 = (bf16[512,896]{1,0:T(8,128)(2,1)}, bf16[512,896]{1,0:T(8,128)(2,1)}, u32[]{:S(2)}, u32[]{:S(2)}) collective-permute-start(bf16[512,896]{1,0:T(8,128)(2,1)} %get-tuple-element.232), channel_id=1, source_target_pairs={{0,8},{4,12},{8,0},{12,4},{16,24},{20,28},{24,16},{28,20},{1,9},{5... | collective-permute-start | bytes 2752520 | tf_op jit(solution)/shard_map/ppermute | solution.py:971
  234.1 23.8 %collective-permute-start.33 = (bf16[512,896]{1,0:T(8,128)(2,1)}, bf16[512,896]{1,0:T(8,128)(2,1)}, u32[]{:S(2)}, u32[]{:S(2)}) collective-permute-start(bf16[512,896]{1,0:T(8,128)(2,1)} %get-tuple-element.237), channel_id=1, source_target_pairs={{0,16},{4,20},{8,24},{12,28},{16,0},{20,4},{24,8},{28,12},{1,17},{... | collective-permute-start | bytes 2752520 | tf_op jit(solution)/shard_map/ppermute | solution.py:971
  235.1 20.3 %collective-permute-start.34 = (bf16[160,896]{1,0:T(8,128)(2,1)}, bf16[160,896]{1,0:T(8,128)(2,1)S(1)}, u32[]{:S(2)}, u32[]{:S(2)}) collective-permute-start(bf16[160,896]{1,0:T(8,128)(2,1)} %get-tuple-element.225), channel_id=1, source_target_pairs={{1,0},{2,1},{3,2},{0,3},{5,4},{6,5},{7,6},{4,7},{9,8},{10,9},{11,1... | collective-permute-start | bytes 860168 | tf_op jit(solution)/shard_map/ppermute | solution.py:976
  259.0 39.6 %collective-permute-start.39 = (bf16[160,896]{1,0:T(8,128)(2,1)S(1)}, bf16[160,896]{1,0:T(8,128)(2,1)}, u32[]{:S(2)}, u32[]{:S(2)}) collective-permute-start(bf16[160,896]{1,0:T(8,128)(2,1)S(1)} %copy-done.56), channel_id=1, source_target_pairs={{3,0},{0,1},{1,2},{2,3},{7,4},{4,5},{5,6},{6,7},{11,8},{8,9},{9,10... | collective-permute-start | bytes 860168 | tf_op jit(solution)/shard_map/ppermute | solution.py:976
  259.7 38.9 %collective-permute-start.36 = (bf16[256,1280]{1,0:T(8,128)(2,1)}, bf16[256,1280]{1,0:T(8,128)(2,1)}, u32[]{:S(2)}, u32[]{:S(2)}) collective-permute-start(bf16[256,1280]{1,0:T(8,128)(2,1)} %get-tuple-element.261), channel_id=1, source_target_pairs={{1,0},{2,1},{3,2},{0,3},{5,4},{6,5},{7,6},{4,7},{9,8},{10,9},{11,1... | collective-permute-start | bytes 1966088 | tf_op jit(solution)/shard_map/ppermute | solution.py:976
  262.8 63.0 %collective-permute-start.37 = (bf16[256,1280]{1,0:T(8,128)(2,1)}, bf16[256,1280]{1,0:T(8,128)(2,1)}, u32[]{:S(2)}, u32[]{:S(2)}) collective-permute-start(bf16[256,1280]{1,0:T(8,128)(2,1)} %get-tuple-element.262), channel_id=1, source_target_pairs={{2,0},{3,1},{0,2},{1,3},{6,4},{7,5},{4,6},{5,7},{10,8},{11,9},{8,1... | collective-permute-start | bytes 1966088 | tf_op jit(solution)/shard_map/ppermute | solution.py:976
  263.0 62.7 %collective-permute-start.38 = (bf16[256,1280]{1,0:T(8,128)(2,1)}, bf16[256,1280]{1,0:T(8,128)(2,1)}, u32[]{:S(2)}, u32[]{:S(2)}) collective-permute-start(bf16[256,1280]{1,0:T(8,128)(2,1)} %get-tuple-element.263), channel_id=1, source_target_pairs={{3,0},{0,1},{1,2},{2,3},{7,4},{4,5},{5,6},{6,7},{11,8},{8,9},{9,10... | collective-permute-start | bytes 1966088 | tf_op jit(solution)/shard_map/ppermute | solution.py:976
  327.3 26.8 %collective-permute-start.45 = (bf16[512,256]{1,0:T(8,128)(2,1)S(1)}, bf16[512,256]{1,0:T(8,128)(2,1)}, u32[]{:S(2)}, u32[]{:S(2)}) collective-permute-start(bf16[512,256]{1,0:T(8,128)(2,1)S(1)} %get-tuple-element.279), channel_id=1, source_target_pairs={{2,0},{3,1},{6,4},{7,5},{10,8},{11,9},{14,12},{15,13},{18,16},{19,... | collective-permute-start | bytes 786440 | tf_op jit(solution)/shard_map/ppermute | solution.py:982
  328.6 25.5 %collective-permute-start.46 = (bf16[512,256]{1,0:T(8,128)(2,1)S(1)}, bf16[512,256]{1,0:T(8,128)(2,1)}, u32[]{:S(2)}, u32[]{:S(2)}) collective-permute-start(bf16[512,256]{1,0:T(8,128)(2,1)S(1)} %get-tuple-element.280), channel_id=1, source_target_pairs={{3,0},{7,4},{11,8},{15,12},{19,16},{23,20},{27,24},{31,28}} | collective-permute-start | bytes 786440 | tf_op jit(solution)/shard_map/ppermute | solution.py:982
  332.5 21.6 %all-to-all-start.1 = ((bf16[8,32,1280]{2,1,0:T(8,128)(2,1)}), bf16[8,32,1280]{2,1,0:T(8,128)(2,1)S(1)}, u32[]{:S(2)}, u32[]{:S(2)}) async-start(bf16[8,32,1280]{2,1,0:T(8,128)(2,1)} %bitcast.64), calls=%async_computation.2 | async-start | bytes 1310720 | tf_op jit(solution)/shard_map/all_to_all | solution.py:1218
  342.4 24.6 %collective-permute-start.43 = (bf16[4,32,1792]{2,1,0:T(8,128)(2,1)}, bf16[4,32,1792]{2,1,0:T(8,128)(2,1)S(1)}, u32[]{:S(2)}, u32[]{:S(2)}) collective-permute-start(bf16[4,32,1792]{2,1,0:T(8,128)(2,1)} %get-tuple-element.333), channel_id=1, source_target_pairs={{0,24},{4,28},{8,16},{12,20},{16,8},{20,12},{24,0},{28,4},{1,25},{... | collective-permute-start | bytes 1376264 | tf_op jit(solution)/shard_map/ppermute | solution.py:971
  345.3 21.7 %collective-permute-start.42 = (bf16[4,32,1792]{2,1,0:T(8,128)(2,1)}, bf16[4,32,1792]{2,1,0:T(8,128)(2,1)S(1)}, u32[]{:S(2)}, u32[]{:S(2)}) collective-permute-start(bf16[4,32,1792]{2,1,0:T(8,128)(2,1)} %get-tuple-element.334), channel_id=1, source_target_pairs={{0,16},{4,20},{8,24},{12,28},{16,0},{20,4},{24,8},{28,12},{1,17},{... | collective-permute-start | bytes 1376264 | tf_op jit(solution)/shard_map/ppermute | solution.py:971
  346.6 20.5 %collective-permute-start.41 = (bf16[4,32,1792]{2,1,0:T(8,128)(2,1)S(1)}, bf16[4,32,1792]{2,1,0:T(8,128)(2,1)S(1)}, u32[]{:S(2)}, u32[]{:S(2)}) collective-permute-start(bf16[4,32,1792]{2,1,0:T(8,128)(2,1)S(1)} %get-tuple-element.332), channel_id=1, source_target_pairs={{0,8},{4,12},{8,0},{12,4},{16,24},{20,28},{24,16},{28,20},{1,9},{5... | collective-permute-start | bytes 1376264 | tf_op jit(solution)/shard_map/ppermute | solution.py:971
  (95 other events, 790.8 us)
Sparse Core Ops, SparseCore 0:
  16.0 29.0 all-gather.2
  69.9 51.5 all-gather.4
  258.0 67.2 reduce-scatter.1
